TPU v7x, 256 devices: a whole 4x4x8 slice. The times are simulated.
256 devices in a mesh: seq: 64 (over y, z, core), head: 4 (over x).
Axes of the slice: x: 4, y: 4, z: 8, core: 2. Of those that a mesh axis runs over, the one named last changes fastest.
Arguments:
- activations: bfloat16 [8192, 4096], P('seq', 'head'), may hold values from -6 to 6
- grad_out: bfloat16 [8192, 4096], P('seq', 'head'), may hold values from -0.125 to 0.125
- write_proj: bfloat16 [8192, 128], P('seq'), may hold values from -1.75 to 1.75
- read_proj: bfloat16 [8192, 128], P('seq'), may hold values from -1.75 to 1.75
- step_raw: float32 [8192, 64], P('seq', 'head'), may hold values from -2 to 0
- step_table: float32 [1000, 64], P(None, 'head'), may hold values from -0.7 to 0.7
- decay_rate: float32 [64], P('head'), may hold values from 0 to 1, as said below
- frame_step: int32 [4], replicated, may hold values from 0 to 999
- scan_order: int32 [8192], P('seq'), may hold values from 0 to 127, as said below
Outputs:
- grad_act: bfloat16 [8192, 4096], P('seq', 'head')
- grad_write: bfloat16 [8192, 128], P('seq')
- grad_read: bfloat16 [8192, 128], P('seq')
- grad_pre: float32 [8192, 64], P('seq', 'head')
- grad_table: float32 [1000, 64], P(None, 'head')
Inputs may be any that keep to these rules, and one draw needn't show every extreme that they name: `scan_order`: within each device's block of 128 entries: a permutation of 0 to 127 in which each aligned run of 2 entries is one run r * 2 to r * 2 + 1, ascending or descending. `decay_rate`: Positive.
All inputs are finite; a program needn't handle non-finite values.
Results may differ from a plain program's by a relative error of at most 0.005.
Values may be sent and summed in bfloat16 or wider, within the bound.
No kernel may reach another device: no remote copies, remote signals or barrier semaphores. Data moves between devices by JAX's collectives and lax.ppermute only.
A program may use at most 192 MiB of HBM per device.

v0:
```python
import jax
import jax.numpy as jnp
from jax import lax
from jax.sharding import PartitionSpec as P

SPAN = 128
FRAME_TOK = 2048


precise = lax.Precision.HIGHEST


def prefix(part, axis, combine, identity, reverse):
    count = lax.axis_size(axis)
    place = lax.axis_index(axis)
    ahead = count - 1 - place if reverse else place
    gathered = jax.tree.map(lambda a: lax.all_gather(a, axis), part)
    state = jax.tree.map(lambda a, e: jnp.zeros_like(a) + jnp.asarray(e, a.dtype), part, identity)

    def one(lap, state):
        source = count - 1 - lap if reverse else lap
        return combine(
            state, jax.tree.map(lambda a: lax.dynamic_index_in_dim(a, source, 0, False), gathered)
        )

    return lax.fori_loop(0, ahead, one, state)


def state_part(signal, writer, deltas, slopes):
    running = jnp.cumsum(deltas * slopes[None, :], axis=0)
    totals = running[-1]
    to_end = jnp.exp(totals[None, :] - running)
    contrib = jnp.einsum(
        "jhp,jn->hpn", signal * (deltas * to_end)[:, :, None], writer, precision=precise
    )
    return (totals, contrib)


def adjoint_part(upstream, reader, deltas, slopes):
    running = jnp.cumsum(deltas * slopes[None, :], axis=0)
    totals = running[-1]
    contrib = jnp.einsum(
        "khp,kn->hpn", upstream * jnp.exp(running)[:, :, None], reader, precision=precise
    )
    return (totals, contrib)


def block_grads(signal, upstream, writer, reader, deltas, slopes, state_in, adjoint_in):
    length = signal.shape[0]
    running = jnp.cumsum(deltas * slopes[None, :], axis=0)
    totals = running[-1]
    order_idx = jnp.arange(length)
    lower_mask = order_idx[:, None] >= order_idx[None, :]
    lower_ones = lower_mask.astype(jnp.float32)
    upper_ones = lower_ones.T
    transposed = running.T
    spread = transposed[:, :, None] - transposed[:, None, :]
    decay_low = jnp.exp(jnp.where(lower_mask[None], spread, -jnp.inf))
    scaled = signal * deltas[:, :, None]
    to_end = jnp.exp(totals[None, :] - running)
    head_exp = jnp.exp(running)
    intersection = jnp.dot(reader, writer.T, precision=precise)
    weights = decay_low * intersection[None]
    carried = jnp.einsum("hpn,jn->jhp", adjoint_in, writer, precision=precise)
    upward = (
        jnp.einsum("hki,khp->ihp", weights, upstream, precision=precise)
        + to_end[:, :, None] * carried
    )
    grad_act = deltas[:, :, None] * upward
    mixing = decay_low * jnp.einsum("ihp,jhp->hij", upstream, scaled, precision=precise)
    grad_read = jnp.einsum("hij,jn->in", mixing, writer, precision=precise) + jnp.einsum(
        "ihp,hpn->in", upstream * head_exp[:, :, None], state_in, precision=precise
    )
    grad_write = jnp.einsum("hkj,kn->jn", mixing, reader, precision=precise) + jnp.einsum(
        "jhp,hpn->jn", scaled * to_end[:, :, None], adjoint_in, precision=precise
    )
    crossed = jnp.einsum("ik,hkj->hij", upper_ones, mixing * intersection[None], precision=precise)
    term_one = jnp.sum(crossed * lower_ones[None], axis=2).T
    state_read = jnp.einsum("hpn,kn->khp", state_in, reader, precision=precise)
    term_two = jnp.dot(
        upper_ones, head_exp * jnp.sum(upstream * state_read, axis=-1), precision=precise
    )
    term_three = jnp.dot(lower_ones, to_end * jnp.sum(scaled * carried, axis=-1), precision=precise)
    term_four = jnp.exp(totals) * jnp.sum(adjoint_in * state_in, axis=(1, 2))
    direct = jnp.sum(scaled * upward, axis=-1)
    log_grad = term_one + term_two + term_three + term_four[None, :] - direct
    grad_step = jnp.sum(signal * upward, axis=-1) + slopes[None, :] * log_grad
    return (grad_act, grad_write, grad_read, grad_step)


def combine_states(earlier, latter):
    return (earlier[0] + latter[0], jnp.exp(latter[0])[:, None, None] * earlier[1] + latter[1])


def forward_pass(signal, writer, deltas, slopes):
    zero_log = jnp.zeros((signal.shape[2],), jnp.float32)
    zero_state = jnp.zeros((signal.shape[2], signal.shape[3], writer.shape[2]), jnp.float32)

    def forward_advance(running, inputs):
        totals, contrib = state_part(inputs[0], inputs[1], inputs[2], slopes)
        updated = (running[0] + totals, jnp.exp(totals)[:, None, None] * running[1] + contrib)
        return (updated, running)

    final, before = lax.scan(forward_advance, (zero_log, zero_state), (signal, writer, deltas))
    log_start, state_start = prefix(final, "seq", combine_states, (zero_log, zero_state), False)
    return before[1] + jnp.exp(before[0])[:, :, None, None] * state_start[None]


def adjoint_pass(upstream, reader, deltas, slopes):
    zero_log = jnp.zeros((upstream.shape[2],), jnp.float32)
    zero_state = jnp.zeros((upstream.shape[2], upstream.shape[3], reader.shape[2]), jnp.float32)

    def adjoint_advance(running, inputs):
        totals, contrib = adjoint_part(inputs[0], inputs[1], inputs[2], slopes)
        updated = (running[0] + totals, jnp.exp(totals)[:, None, None] * running[1] + contrib)
        return (updated, running)

    final, after = lax.scan(
        adjoint_advance, (zero_log, zero_state), (upstream, reader, deltas), reverse=True
    )
    log_end, adjoint_end = prefix(final, "seq", combine_states, (zero_log, zero_state), True)
    return after[1] + jnp.exp(after[0])[:, :, None, None] * adjoint_end[None]


def shards(
    activations,
    grad_out,
    write_proj,
    read_proj,
    step_raw,
    step_table,
    decay_rate,
    frame_step,
    scan_order,
):
    tokens_here = activations.shape[0]
    heads_here = step_raw.shape[1]
    head_width = activations.shape[1] // heads_here
    state_width = write_proj.shape[1]
    device = lax.axis_index("seq")
    frame_here = device * tokens_here // FRAME_TOK
    step_index = lax.dynamic_index_in_dim(frame_step, frame_here, 0, keepdims=False)
    offset = lax.dynamic_index_in_dim(step_table, step_index, 0, keepdims=False)
    pre_step = step_raw + offset[None, :]
    deltas_bf = jax.nn.softplus(pre_step).astype(jnp.bfloat16)
    blocks = tokens_here // SPAN
    slopes = -decay_rate

    def to_blocks(values, trailing):
        return values[scan_order].astype(jnp.float32).reshape((blocks, SPAN) + trailing)

    act_recv, grad_recv, write_recv, read_recv, step_recv = (
        lax.all_to_all(activations, "seq", split_axis=0, concat_axis=0, tiled=True),
        lax.all_to_all(grad_out, "seq", split_axis=0, concat_axis=0, tiled=True),
        lax.all_to_all(write_proj, "seq", split_axis=0, concat_axis=0, tiled=True),
        lax.all_to_all(read_proj, "seq", split_axis=0, concat_axis=0, tiled=True),
        lax.all_to_all(deltas_bf, "seq", split_axis=0, concat_axis=0, tiled=True),
    )
    signal = to_blocks(act_recv, (heads_here, head_width))
    writer = to_blocks(write_recv, (state_width,))
    deltas = to_blocks(step_recv, (heads_here,))
    state_in = forward_pass(signal, writer, deltas, slopes)
    upstream = to_blocks(grad_recv, (heads_here, head_width))
    reader = to_blocks(read_recv, (state_width,))
    adjoint_in = adjoint_pass(upstream, reader, deltas, slopes)
    results = lax.map(
        lambda inputs: block_grads(
            inputs[0], inputs[1], inputs[2], inputs[3], inputs[4], slopes, inputs[5], inputs[6]
        ),
        (signal, upstream, writer, reader, deltas, state_in, adjoint_in),
    )
    scan_act = results[0].reshape(tokens_here, heads_here * head_width).astype(jnp.bfloat16)
    part_write = results[1].reshape(tokens_here, state_width)
    part_read = results[2].reshape(tokens_here, state_width)
    scan_step = results[3].reshape(tokens_here, heads_here).astype(jnp.bfloat16)

    def unscan(values):
        return jnp.zeros_like(values).at[scan_order].set(values)

    total_write, total_read = lax.psum((part_write, part_read), "head")
    joined = jnp.concatenate([total_write, total_read], axis=1).astype(jnp.bfloat16)
    back_act, back_joined, back_step = (
        lax.all_to_all(unscan(scan_act), "seq", split_axis=0, concat_axis=0, tiled=True),
        lax.all_to_all(unscan(joined), "seq", split_axis=0, concat_axis=0, tiled=True),
        lax.all_to_all(unscan(scan_step), "seq", split_axis=0, concat_axis=0, tiled=True),
    )
    grad_write = back_joined[:, :state_width]
    grad_read = back_joined[:, state_width:]
    grad_pre = back_step.astype(jnp.float32) * jax.nn.sigmoid(pre_step)
    column = jnp.sum(grad_pre, axis=0)
    tsteps = step_table.shape[0]
    picked = (jnp.arange(tsteps) == step_index).astype(jnp.float32)
    grad_table = lax.psum(picked[:, None] * column[None, :], "seq")
    return (back_act, grad_write, grad_read, grad_pre, grad_table)


def solution(mesh):
    in_specs = (
        P("seq", "head"),
        P("seq", "head"),
        P("seq", None),
        P("seq", None),
        P("seq", "head"),
        P(None, "head"),
        P("head"),
        P(),
        P("seq"),
    )
    out_specs = (
        P("seq", "head"),
        P("seq", None),
        P("seq", None),
        P("seq", "head"),
        P(None, "head"),
    )
    return jax.shard_map(shards, mesh=mesh, in_specs=in_specs, out_specs=out_specs, check_vma=False)
```

profile of v0, /device:TPU:1, one launch (start us, length us, event | category | flops | bytes accessed | tf_op | source)
XLA Modules:
  0.0 742.9 jit_solution(4864216173570576645)
XLA Ops:
  7.2 1.2 dynamic_slice.64
  12.1 13.2 %all-to-all-start = ((bf16[64,2,16]{2,1,0:T(2,128)(2,1)}), bf16[64,2,16]{2,1,0:T(2,128)(2,1)S(1)}, u32[]{:S(2)}, u32[]{:S(2)}) async-start(bf16[64,2,16]{2,1,0:T(2,128)(2,1)} %bitcast.5), calls=%async_computation | async-start | bytes 65536 | tf_op jit(solution)/shard_map/all_to_all | solution.py:157
  26.6 1.7 all_to_all.77
  28.3 6.1 all-to-all-done
  34.4 4.7 all-to-all-start.3
  40.3 8.2 %all-to-all-done.3 = bf16[64,2,128]{2,1,0:T(2,128)(2,1)S(1)} async-done(((bf16[64,2,128]{2,1,0:T(2,128)(2,1)}), bf16[64,2,128]{2,1,0:T(2,128)(2,1)S(1)}, u32[]{:S(2)}, u32[]{:S(2)}) %all-to-all-start.3) | async-done | bytes 32800 | tf_op jit(solution)/shard_map/all_to_all | solution.py:155
  48.5 4.7 all-to-all-start.5
  54.1 11.1 %all-to-all-done.5 = bf16[64,2,1024]{2,1,0:T(2,128)(2,1)S(1)} async-done(((bf16[64,2,1024]{2,1,0:T(2,128)(2,1)}), bf16[64,2,1024]{2,1,0:T(2,128)(2,1)S(1)}, u32[]{:S(2)}, u32[]{:S(2)}) %all-to-all-start.5) | async-done | bytes 262176 | tf_op jit(solution)/shard_map/all_to_all | solution.py:153
  66.3 1.2 convolution_add_fusion
  67.6 6.1 all-to-all-start.2
  73.7 1.8 all_to_all.65
  75.4 7.5 %all-to-all-done.2 = bf16[64,2,128]{2,1,0:T(2,128)(2,1)S(1)} async-done(((bf16[64,2,128]{2,1,0:T(2,128)(2,1)}), bf16[64,2,128]{2,1,0:T(2,128)(2,1)S(1)}, u32[]{:S(2)}, u32[]{:S(2)}) %all-to-all-start.2) | async-done | bytes 32800 | tf_op jit(solution)/shard_map/all_to_all | solution.py:156
  82.9 4.7 all-to-all-start.1
  88.5 13.8 %all-to-all-done.1 = bf16[64,2,1024]{2,1,0:T(2,128)(2,1)S(1)} async-done(((bf16[64,2,1024]{2,1,0:T(2,128)(2,1)}), bf16[64,2,1024]{2,1,0:T(2,128)(2,1)S(1)}, u32[]{:S(2)}, u32[]{:S(2)}) %all-to-all-start.1) | async-done | bytes 262176 | tf_op jit(solution)/shard_map/all_to_all | solution.py:154
  103.4 1.2 convolution_add_fusion.1
  104.8 38.3 %all-gather.2 = f32[64,1,16]{2,1,0:T(1,128)S(1)} all-gather(f32[1,1,16]{2,1,0:T(1,128)S(1)} %get-tuple-element.271), channel_id=1, replica_groups=mesh['seq'=64,'head'=4] {'seq'}, dimensions={0}, use_global_device_ids=true | all-gather | bytes 4160 | tf_op jit(solution)/shard_map/all_gather | solution.py:17
  145.1 66.6 %all-gather.8.cloned.1.call-done = f32[1024,64,128]{2,1,0:T(8,128)} async-done(((f32[16,64,128]{2,1,0:T(8,128)}), f32[1024,64,128]{2,1,0:T(8,128)}) %all-gather.8.cloned.1.call-update) | async-done | bytes 33554448 | tf_op jit(solution)/shard_map/all_gather | solution.py:17
  211.8 1.2 while.17
  211.8 1.2 bitcast_add_fusion.5
  213.4 140.7 %all-gather.6.cloned.1.call-done = f32[1024,64,128]{2,1,0:T(8,128)} async-done(((f32[16,64,128]{2,1,0:T(8,128)}), f32[1024,64,128]{2,1,0:T(8,128)}) %all-gather.6.cloned.1.call-update) | async-done | bytes 33554448 | tf_op jit(solution)/shard_map/all_gather | solution.py:17
  354.2 77.2 %while.16 = (s32[]{:T(128)}, f32[16,64,128]{2,1,0:T(8,128)S(1)}, s32[]{:T(128)}, f32[64,16]{1,0:T(8,128)S(1)}, f32[64,16,64,128]{3,2,1,0:T(8,128)}, /*index=5*/s32[]{:T(128)}, s32[]{:T(128)}, s32[]{:T(128)}, s32[]{:T(128)}) while((s32[]{:T(128)}, f32[16,64,128]{2,1,0:T(8,128)S(1)}, s32[]{:T(128)}, f32[64,16]{1,0:T(8,128)S(1)}, ...), condition=%wide.region_2.3_spmd, body=%wide.region_1.2_spmd.sunk | while | flops 262150 | bytes 1573203 | solution.py:26
  354.2 1.2 bitcast_add_fusion.4
  355.5 1.2 bitcast_add_fusion.4
  356.7 1.2 bitcast_add_fusion.4
  358.0 1.2 bitcast_add_fusion.4
  359.2 1.2 bitcast_add_fusion.4
  360.4 1.2 bitcast_add_fusion.4
  361.7 1.2 bitcast_add_fusion.4
  362.9 1.2 bitcast_add_fusion.4
  364.2 1.2 bitcast_add_fusion.4
  365.4 1.2 bitcast_add_fusion.4
  366.6 1.2 bitcast_add_fusion.4
  367.9 1.2 bitcast_add_fusion.4
  369.1 1.2 bitcast_add_fusion.4
  370.4 1.2 bitcast_add_fusion.4
  371.6 1.2 bitcast_add_fusion.4
  372.9 1.2 bitcast_add_fusion.4
  374.1 1.2 bitcast_add_fusion.4
  375.3 1.2 bitcast_add_fusion.4
  376.6 1.2 bitcast_add_fusion.4
  435.7 1.5 scatter_custom_fusion.2
  437.1 5.5 all-to-all-start.7
  443.1 14.9 %all-reduce.2 = (bf16[128,128]{1,0:T(8,128)(2,1)S(1)}, bf16[128,128]{1,0:T(8,128)(2,1)S(1)}) all-reduce(f32[128,128]{1,0:T(8,128)S(1)} %convolution_add_fusion.2, f32[128,128]{1,0:T(8,128)S(1)} %convolution_add_fusion.3), channel_id=1, replica_groups=mesh['seq'=64,'head'=4] {'head'}, use_global_device_ids=true, to_apply=%region_8.9 | all-reduce | flops 32768 | bytes 196608 | tf_op jit(solution)/shard_map/psum | solution.py:180
  459.7 13.9 %all-to-all-start.6 = ((bf16[64,2,256]{2,1,0:T(2,128)(2,1)}), bf16[64,2,256]{2,1,0:T(2,128)(2,1)S(1)}, u32[]{:S(2)}, u32[]{:S(2)}) async-start(bf16[64,2,256]{2,1,0:T(2,128)(2,1)} %all_to_all.80), calls=%async_computation.6 | async-start | bytes 131072 | tf_op jit(solution)/shard_map/all_to_all | solution.py:184
  474.4 1.2 scatter_custom_fusion
  476.5 7.0 all-to-all-done.6
  483.4 4.5 all-to-all-start.4
  488.7 246.0 %psum.23 = f32[1000,16]{0,1:T(8,128)} all-reduce(f32[1000,16]{0,1:T(8,128)S(1)} %broadcast_multiply_fusion), channel_id=1, replica_groups=mesh['seq'=64,'head'=4] {'seq'}, use_global_device_ids=true, to_apply=%region_18.19 | all-reduce | flops 16000 | bytes 128000 | tf_op jit(solution)/shard_map/psum | solution.py:193
  (173 shorter events, 73.0 us)
Async XLA Ops:
  7.2 4.0 copy-start
  12.1 22.4 %all-to-all-start = ((bf16[64,2,16]{2,1,0:T(2,128)(2,1)}), bf16[64,2,16]{2,1,0:T(2,128)(2,1)S(1)}, u32[]{:S(2)}, u32[]{:S(2)}) async-start(bf16[64,2,16]{2,1,0:T(2,128)(2,1)} %bitcast.5), calls=%async_computation | async-start | bytes 65536 | tf_op jit(solution)/shard_map/all_to_all | solution.py:157
  34.4 14.0 %all-to-all-start.3 = ((bf16[64,2,128]{2,1,0:T(2,128)(2,1)}), bf16[64,2,128]{2,1,0:T(2,128)(2,1)S(1)}, u32[]{:S(2)}, u32[]{:S(2)}) async-start(bf16[64,2,128]{2,1,0:T(2,128)(2,1)} %bitcast.105), calls=%async_computation.3 | async-start | bytes 65536 | tf_op jit(solution)/shard_map/all_to_all | solution.py:155
  48.5 16.8 %all-to-all-start.5 = ((bf16[64,2,1024]{2,1,0:T(2,128)(2,1)}), bf16[64,2,1024]{2,1,0:T(2,128)(2,1)S(1)}, u32[]{:S(2)}, u32[]{:S(2)}) async-start(bf16[64,2,1024]{2,1,0:T(2,128)(2,1)} %all_to_all.77), calls=%async_computation.5 | async-start | bytes 524288 | tf_op jit(solution)/shard_map/all_to_all | solution.py:153
  53.2 158.5 %all-gather.8.cloned.1.call-start = ((), (), s32[]{:S(2)}) async-start(), calls=%async_computation.9 | async-start | bytes 34078720 | tf_op jit(solution)/shard_map/all_gather | solution.py:17
  67.6 15.3 %all-to-all-start.2 = ((bf16[64,2,128]{2,1,0:T(2,128)(2,1)}), bf16[64,2,128]{2,1,0:T(2,128)(2,1)S(1)}, u32[]{:S(2)}, u32[]{:S(2)}) async-start(bf16[64,2,128]{2,1,0:T(2,128)(2,1)} %bitcast.106), calls=%async_computation.2 | async-start | bytes 65536 | tf_op jit(solution)/shard_map/all_to_all | solution.py:156
  82.9 19.4 %all-to-all-start.1 = ((bf16[64,2,1024]{2,1,0:T(2,128)(2,1)}), bf16[64,2,1024]{2,1,0:T(2,128)(2,1)S(1)}, u32[]{:S(2)}, u32[]{:S(2)}) async-start(bf16[64,2,1024]{2,1,0:T(2,128)(2,1)} %all_to_all.65), calls=%async_computation.1 | async-start | bytes 524288 | tf_op jit(solution)/shard_map/all_to_all | solution.py:154
  87.6 266.5 %all-gather.6.cloned.1.call-start = ((), (), s32[]{:S(2)}) async-start(), calls=%async_computation.8 | async-start | bytes 34078720 | tf_op jit(solution)/shard_map/all_gather | solution.py:17
  437.1 22.6 %all-to-all-start.7 = ((bf16[64,2,16]{2,1,0:T(2,128)(2,1)}), bf16[64,2,16]{2,1,0:T(2,128)(2,1)S(1)}, u32[]{:S(2)}, u32[]{:S(2)}) async-start(bf16[64,2,16]{2,1,0:T(2,128)(2,1)} %bitcast.30), calls=%async_computation.7 | async-start | bytes 65536 | tf_op jit(solution)/shard_map/all_to_all | solution.py:185
  459.7 23.7 %all-to-all-start.6 = ((bf16[64,2,256]{2,1,0:T(2,128)(2,1)}), bf16[64,2,256]{2,1,0:T(2,128)(2,1)S(1)}, u32[]{:S(2)}, u32[]{:S(2)}) async-start(bf16[64,2,256]{2,1,0:T(2,128)(2,1)} %all_to_all.80), calls=%async_computation.6 | async-start | bytes 131072 | tf_op jit(solution)/shard_map/all_to_all | solution.py:184
  483.4 251.9 %all-to-all-start.4 = ((bf16[64,2,1024]{2,1,0:T(2,128)(2,1)}), bf16[64,2,1024]{2,1,0:T(2,128)(2,1)S(1)}, u32[]{:S(2)}, u32[]{:S(2)}) async-start(bf16[64,2,1024]{2,1,0:T(2,128)(2,1)} %all_to_all.74), calls=%async_computation.4 | async-start | bytes 524288 | tf_op jit(solution)/shard_map/all_to_all | solution.py:183
Sparse Core Ops, SparseCore 0:
  67.7 144.0 all-gather.7
  214.5 139.5 all-gather.5
where the time goes:
time: 749 us; the launch traced here: 743 us
  blocking collectives  299 us (40%)
  waiting for transfers between devices  261 us (35%)
  other arithmetic  79.4 us (11%)
  starting transfers between devices  57.4 us (8%)
  local copies, waits for them, and re-layouts  18 us (2%)
  between operations  16.3 us (2%)
  matrix products  9.07 us (1%)
    psum x1, blocking collectives, shards(): grad_table = lax.psum(picked[:, None] * column[None, :], 'seq')  246 us
    all_gather x2, waiting for transfers between devices, prefix(): gathered = jax.tree.map(lambda a: lax.all_gather(a, axis), part)  207 us
    add x63, other arithmetic, combine_states(): jnp.exp(latter[0])[:, None, None] * earlier[1] + latter[1]  75 us
    all_gather x1, blocking collectives, prefix(): gathered = jax.tree.map(lambda a: lax.all_gather(a, axis), part)  38.3 us
  transfers between devices with their start and end apart: 10, of which 8 were waited for; matrix products, arithmetic and copies ran while one was open for 2% of the time, Pallas kernels for 0%

commit v1 on v0

v1 whole, which is shorter than its diff:
```python
import functools

import jax
import jax.numpy as jnp
import numpy as np
from jax import lax
from jax.experimental import pallas as pl
from jax.experimental.pallas import tpu as pltpu
from jax.sharding import PartitionSpec as P

F32 = jnp.float32
BF16 = jnp.bfloat16
FRAME_TOK = 2048
TOK = 128
LANES = 128
SEQ = 64
PARTS = 8
PAIRS = 8
BLOCKS = 8
SLOT_IN = 56
SLOT_STATE = 136
SLOT_OUT = 40
LOCAL = BLOCKS * TOK
PARAMS = pltpu.CompilerParams(vmem_limit_bytes=48 * 1024 * 1024)


def place(part, pair):
    y, low = part // 2, part % 2
    high, core = pair // 2, pair % 2
    return y * 16 + (high * 2 + low) * 2 + core


def my_place():
    me = lax.axis_index("seq")
    part = (me // 16) * 2 + (me // 2) % 2
    pair = ((me // 4) % 4) * 2 + me % 2
    return part, pair, me % 2


STATE_GROUPS = [[place(part, pair) for part in range(PARTS)] for pair in range(PAIRS)]


def nn(a, b):
    return lax.dot_general(a, b, (((1,), (0,)), ((), ())), preferred_element_type=F32)


def nt(a, b):
    return lax.dot_general(a, b, (((1,), (1,)), ((), ())), preferred_element_type=F32)


def split(value):
    high = value.astype(BF16)
    return high, (value - high.astype(F32)).astype(BF16)


def lane_iota(rows):
    return lax.broadcasted_iota(jnp.int32, (rows, LANES), 1)


def heads_over_lanes(first, second, rows):
    return jnp.where(lane_iota(rows) < 64, first, second)


def softplus(value):
    return jnp.maximum(value, 0.0) + jnp.log1p(jnp.exp(-jnp.abs(value)))


def sigmoid(value):
    return 1.0 / (1.0 + jnp.exp(-value))


def shifted_steps(frame_ref, raw_ref, table_ref):
    frame_here = lax.axis_index("seq") * TOK // FRAME_TOK
    index = frame_ref[frame_here]
    return raw_ref[...] + table_ref[pl.ds(index, 1), :]


def pack_kernel(frame_ref, order_ref, x_ref, dy_ref, b_ref, c_ref, raw_ref, table_ref, out_ref):
    heads = raw_ref.shape[1]
    pre = shifted_steps(frame_ref, raw_ref, table_ref)
    pre = jnp.concatenate([pre, jnp.zeros((TOK, LANES - heads), F32)], axis=1)
    pre = pre.T[:heads]
    delta = softplus(pre).astype(BF16).astype(F32)
    gate = sigmoid(pre)
    gate_high = gate.astype(BF16).astype(F32)
    gate_low = gate - gate_high
    order = jnp.broadcast_to(order_ref[...].astype(F32), (TOK, TOK)).T
    lane = lane_iota(TOK)
    token = ((lane % 64) * 2 + lane // 64).astype(F32)
    steps = lax.broadcasted_iota(jnp.int32, (TOK, TOK), 0).astype(F32)
    position = jnp.sum(jnp.where(order == token, steps, 0.0), axis=0, keepdims=True)
    for pair in range(PAIRS):
        own = slice(2 * pair, 2 * pair + 2)
        rows = jnp.concatenate(
            [position, delta[own], gate_high[own], gate_low[own], jnp.zeros((1, LANES), F32)], axis=0
        ).astype(BF16)
        proj_ref = c_ref if pair % 2 else b_ref
        columns = slice(LANES * pair, LANES * pair + LANES)
        for part in range(PARTS):
            slot = place(part, pair)
            tokens = slice(16 * part, 16 * part + 16)
            out_ref[slot, 0:16, :] = x_ref[tokens, columns]
            out_ref[slot, 16:32, :] = dy_ref[tokens, columns]
            out_ref[slot, 32:48, :] = proj_ref[tokens, :]
            out_ref[slot, 48:56, :] = rows


def to_columns(first, second):
    head_one = jnp.concatenate([first, pltpu.roll(first, LANES - 1, 1)], axis=0)
    head_two = jnp.concatenate([pltpu.roll(second, 1, 1), second], axis=0)
    return jnp.where(lane_iota(TOK) % 2 == 0, head_one, head_two)


def slope_lanes(decay_ref, pair, rows):
    first, second = -decay_ref[2 * pair], -decay_ref[2 * pair + 1]
    return first, second, jnp.where(lane_iota(rows) % 2 == 0, first, second)


def unpack_kernel(
    decay_ref, recv_ref, swap_ref,
    x_ref, dy_ref, b_ref, c_ref, send_ref, s_ref, r_ref, stat_ref,
    wide, misc,
):
    part, pair, core = my_place()

    def spread(value, target_ref):
        wide[...] = value.reshape(SEQ * 16, LANES)
        for row in range(16):
            target_ref[row * 64 : row * 64 + 64, :] = wide[pl.ds(row, 64, stride=16), :].astype(BF16)

    spread(recv_ref[:, 0:16, :].astype(F32), x_ref)
    spread(recv_ref[:, 16:32, :].astype(F32), dy_ref)
    mine = recv_ref[:, 32:48, :].astype(F32)
    other = swap_ref[:, 32:48, :].astype(F32)
    spread(jnp.where(core == 0, mine, other), b_ref)
    spread(jnp.where(core == 0, other, mine), c_ref)

    misc[...] = recv_ref[:, 48:56, :].astype(F32).reshape(SEQ * 8, LANES)
    shift = (LANES - 16 * part) % LANES

    def own_lanes(row):
        return pltpu.roll(misc[pl.ds(row, 64, stride=8), :], shift, 1)

    steps = to_columns(own_lanes(1), own_lanes(2))
    gates = to_columns(own_lanes(3) + own_lanes(5), own_lanes(4) + own_lanes(6))
    pos_rows = jnp.concatenate(
        [misc[pl.ds(part * 64 + 8 * block, 1), :] for block in range(BLOCKS)], axis=0
    )
    pos_cols = jnp.concatenate([pos_rows, jnp.zeros((LANES - BLOCKS, LANES), F32)], axis=0).T
    lane = lane_iota(TOK)
    steps_bf = steps.astype(BF16)
    sums = jnp.zeros((TOK, LANES), F32)
    for block in range(BLOCKS):
        later = (pos_cols[:, block : block + 1] >= pos_rows[block : block + 1, :]).astype(F32).astype(BF16)
        sums = jnp.where(lane // 2 == block, nn(later, steps_bf), sums)
    slope_one, slope_two, slopes = slope_lanes(decay_ref, pair, TOK)
    logs = sums * slopes
    totals = jnp.sum(steps, axis=0, keepdims=True) * slopes[:1]
    stat_ref[0] = steps
    stat_ref[1] = logs
    stat_ref[2] = gates
    stat_ref[3] = pos_cols
    stat_ref[4] = jnp.concatenate(
        [pos_rows, jnp.broadcast_to(totals, (8, LANES)), jnp.zeros((LANES - 16, LANES), F32)], axis=0
    )
    weights = steps * jnp.exp(totals - logs)
    starts = jnp.exp(logs)
    state = jnp.zeros((LANES, LANES), F32)
    for block in range(BLOCKS):
        rows = slice(block * TOK, block * TOK + TOK)
        j = 2 * block
        keep = jnp.exp(heads_over_lanes(totals[:, j : j + 1], totals[:, j + 1 : j + 2], 1))
        write_t = b_ref[rows, :].astype(F32).T.astype(BF16)
        read_t = c_ref[rows, :].astype(F32).T.astype(BF16)
        wx = heads_over_lanes(weights[:, j : j + 1], weights[:, j + 1 : j + 2], TOK)
        high, low = split(x_ref[rows, :].astype(F32) * wx)
        gained = nn(write_t, high) + nn(write_t, low)
        s_ref[block] = gained
        state = state * keep + gained
        wd = heads_over_lanes(starts[:, j : j + 1], starts[:, j + 1 : j + 2], TOK)
        high, low = split(dy_ref[rows, :].astype(F32) * wd)
        r_ref[block] = nn(read_t, high) + nn(read_t, low)
    adjoint = jnp.zeros((LANES, LANES), F32)
    whole = jnp.zeros((1, LANES), F32)
    for block in reversed(range(BLOCKS)):
        j = 2 * block
        total = heads_over_lanes(totals[:, j : j + 1], totals[:, j + 1 : j + 2], 1)
        adjoint = adjoint * jnp.exp(total) + r_ref[block]
        whole = whole + total
    top = whole.astype(BF16).astype(F32)
    middle = (whole - top).astype(BF16).astype(F32)
    bottom = whole - top - middle
    tail = jnp.concatenate([top, middle, bottom, jnp.zeros((5, LANES), F32)], axis=0).astype(BF16)
    state = state.astype(BF16)
    adjoint = adjoint.astype(BF16)
    for slot in range(PARTS):
        after = slot > part

        @pl.when(after)
        def _():
            send_ref[slot, 0:128, :] = state

        @pl.when(jnp.logical_not(after))
        def _():
            send_ref[slot, 0:128, :] = adjoint

        send_ref[slot, 128:136, :] = tail


def inner_kernel(x_ref, dy_ref, b_ref, c_ref, stat_ref, u_ref, gw_ref, gr_ref, t_ref):
    steps = stat_ref[0]
    logs = stat_ref[1]
    log_rows = logs.T
    pos_cols = stat_ref[3]
    pos_rows = stat_ref[4][:8]
    lane = lane_iota(TOK)
    t_ref[...] = jnp.zeros((LANES, LANES), F32)
    for block in range(BLOCKS):
        rows = slice(block * TOK, block * TOK + TOK)
        x = x_ref[rows, :]
        dy = dy_ref[rows, :]
        write = b_ref[rows, :]
        read = c_ref[rows, :]
        pos_col = pos_cols[:, block : block + 1]
        pos_row = pos_rows[block : block + 1, :]
        ahead = pos_row >= pos_col
        behind = (pos_col >= pos_row).astype(F32).astype(BF16)
        cross = nt(write, read)
        zero = jnp.zeros_like(dy)
        x_heads = (jnp.where(lane < 64, x, zero), jnp.where(lane < 64, zero, x))
        dy_stack = jnp.concatenate(
            [jnp.where(lane < 64, dy, zero), jnp.where(lane < 64, zero, dy)], axis=0
        )
        carry, mixed = [], []
        for head in range(2):
            j = 2 * block + head
            gap = log_rows[j : j + 1, :] - logs[:, j : j + 1]
            decay = jnp.exp(jnp.where(ahead, gap, -1e30))
            carry.append(decay * cross)
            mixed.append(decay * (nt(x_heads[head], dy) * steps[:, j : j + 1]))
            high, low = split(mixed[head] * cross)
            crossed = nn(high, behind) + nn(low, behind)
            t_ref[j : j + 1, :] = jnp.sum(jnp.where(ahead, crossed, 0.0), axis=0, keepdims=True)
        high, low = split(jnp.concatenate(carry, axis=1))
        u_ref[rows, :] = nn(high, dy_stack) + nn(low, dy_stack)
        both = mixed[0] + mixed[1]
        high, low = split(both)
        gw_ref[rows, :] = nn(high, read) + nn(low, read)
        high, low = split(both.T)
        gr_ref[rows, :] = nn(high, write) + nn(low, write)


def outer_kernel(
    decay_ref, recv_ref, x_ref, dy_ref, b_ref, c_ref, s_ref, r_ref, stat_ref,
    u_ref, gw_ref, gr_ref, t_ref,
    out_ref, keep_ref, give_ref,
    adj, wide, wide_w, wide_r,
):
    part, pair, core = my_place()
    slope_one, slope_two, slopes = slope_lanes(decay_ref, pair, TOK)

    def arrive(slot, state):
        tail = recv_ref[slot, 128:136, :].astype(F32)
        total = tail[0:1] + tail[1:2] + tail[2:3]
        return state * jnp.exp(total) + recv_ref[slot, 0:128, :].astype(F32)

    zero = jnp.zeros((LANES, LANES), F32)
    state = lax.fori_loop(0, part, arrive, zero)
    adjoint = lax.fori_loop(0, PARTS - 1 - part, lambda k, a: arrive(PARTS - 1 - k, a), zero)

    steps = stat_ref[0]
    logs = stat_ref[1]
    gates = stat_ref[2]
    pos_cols = stat_ref[3]
    pos_rows = stat_ref[4][:8]
    totals = stat_ref[4][8:9]
    starts = jnp.exp(logs)
    ends = jnp.exp(totals - logs)
    lane = lane_iota(TOK)
    sub = lax.broadcasted_iota(jnp.int32, (LANES, LANES), 0)

    def total_of(block):
        j = 2 * block
        return heads_over_lanes(totals[:, j : j + 1], totals[:, j + 1 : j + 2], 1)

    for block in reversed(range(BLOCKS)):
        adj[block] = adjoint
        adjoint = adjoint * jnp.exp(total_of(block)) + r_ref[block]

    direct = jnp.zeros((TOK, LANES), F32)
    log_grad = t_ref[...].T
    for block in range(BLOCKS):
        rows = slice(block * TOK, block * TOK + TOK)
        j = 2 * block
        x = x_ref[rows, :].astype(F32)
        dy = dy_ref[rows, :].astype(F32)
        write = b_ref[rows, :]
        read = c_ref[rows, :]
        adjoint = adj[block]
        state_high, state_low = split(state)
        adj_high, adj_low = split(adjoint)
        step = heads_over_lanes(steps[:, j : j + 1], steps[:, j + 1 : j + 2], TOK)
        start = heads_over_lanes(starts[:, j : j + 1], starts[:, j + 1 : j + 2], TOK)
        end = heads_over_lanes(ends[:, j : j + 1], ends[:, j + 1 : j + 2], TOK)
        keep = jnp.exp(total_of(block))
        carried = end * (nn(write, adj_high) + nn(write, adj_low))
        recalled = nn(read, state_high) + nn(read, state_low)
        u = u_ref[rows, :] + carried
        act = step * u
        out_rows = (pl.ds(2 * block, 64, stride=16), pl.ds(2 * block + 1, 64, stride=16))
        wide[out_rows[0], :] = act[:64]
        wide[out_rows[1], :] = act[64:]
        dy_start = start * dy
        x_end = (end * step) * x
        high, low = split(dy_start)
        gr = gr_ref[rows, :] + (nt(high, state_high) + (nt(high, state_low) + nt(low, state_high)))
        high, low = split(x_end)
        gw = gw_ref[rows, :] + (nt(high, adj_high) + (nt(high, adj_low) + nt(low, adj_high)))
        for half in range(2):
            wide_w[out_rows[half], :] = gw[64 * half : 64 * half + 64]
            wide_r[out_rows[half], :] = gr[64 * half : 64 * half + 64]
        pick = (lane == 2 * block + sub // 64).astype(F32).astype(BF16)

        def per_head(value):
            high, low = split(value)
            return nn(high, pick) + nn(low, pick)

        mine = lane // 2 == block
        read_part = per_head(dy_start * recalled)
        write_part = per_head(step * x * carried)
        direct = direct + per_head(x * u)
        ahead = (pos_rows[block : block + 1, :] >= pos_cols[:, block : block + 1]).astype(F32).astype(BF16)
        behind = (pos_cols[:, block : block + 1] >= pos_rows[block : block + 1, :]).astype(F32).astype(BF16)
        high, low = split(read_part)
        added = nn(ahead, high) + nn(ahead, low)
        high, low = split(write_part)
        added = added + (nn(behind, high) + nn(behind, low))
        overlap = jnp.sum(adjoint * state, axis=0, keepdims=True) * keep
        first = jnp.sum(jnp.where(lane_iota(1) < 64, overlap, 0.0), axis=1, keepdims=True)
        second = jnp.sum(jnp.where(lane_iota(1) < 64, 0.0, overlap), axis=1, keepdims=True)
        added = added + jnp.where(lane % 2 == 0, first, second)
        log_grad = log_grad + jnp.where(mine, added, 0.0)
        state = state * keep + s_ref[block]

    log_grad = log_grad - steps * direct
    grad_step = (direct + slopes * log_grad).astype(BF16).astype(F32)
    grad_step = jnp.where(lane < 2 * BLOCKS, grad_step, 0.0)
    grad_pre = grad_step * gates
    frames = []
    for frame in range(4):
        low_rows = slice(16 * frame, 16 * frame + 16)
        high_rows = slice(64 + 16 * frame, 80 + 16 * frame)
        frames.append(jnp.sum(grad_pre[low_rows] + grad_pre[high_rows], axis=0, keepdims=True))
    frames = jnp.concatenate(frames + [jnp.zeros((4, LANES), F32)], axis=0)
    frames_high = frames.astype(BF16).astype(F32)
    frames = frames_high + pltpu.roll(frames - frames_high, 64, 1)

    even = lane_iota(64) % 2 == 0
    top, bottom = grad_step[:64], grad_step[64:]
    shift = 16 * part
    row_one = pltpu.roll(jnp.where(even, top, pltpu.roll(bottom, 1, 1)), shift, 1)
    row_two = pltpu.roll(jnp.where(even, pltpu.roll(top, LANES - 1, 1), bottom), shift, 1)
    misc = jnp.concatenate(
        [
            row_one[:, None, :],
            row_two[:, None, :],
            jnp.broadcast_to(frames[None, :4, :], (SEQ, 4, LANES)),
            jnp.zeros((SEQ, 2, LANES), F32),
        ],
        axis=1,
    )
    out_ref[:, 0:16, :] = wide[...].reshape(SEQ, 16, LANES).astype(BF16)
    out_ref[:, 32:40, :] = misc.astype(BF16)

    @pl.when(core == 0)
    def _():
        keep_ref[...] = wide_w[...]
        give_ref[...] = wide_r[...]

    @pl.when(core == 1)
    def _():
        keep_ref[...] = wide_r[...]
        give_ref[...] = wide_w[...]


def join_kernel(in_ref, keep_ref, got_ref, out_ref):
    out_ref[:, 0:16, :] = in_ref[:, 0:16, :]
    out_ref[:, 16:32, :] = (keep_ref[...] + got_ref[...]).reshape(SEQ, 16, LANES).astype(BF16)
    out_ref[:, 32:40, :] = in_ref[:, 32:40, :]


def finish_kernel(frame_ref, recv_ref, raw_ref, table_ref, act_ref, proj_ref, pre_ref, grad_ref, rows_ref):
    heads = raw_ref.shape[1]
    for pair in range(PAIRS):
        columns = slice(LANES * pair, LANES * pair + LANES)
        for part in range(PARTS):
            act_ref[16 * part : 16 * part + 16, columns] = recv_ref[place(part, pair), 0:16, :]
    for part in range(PARTS):
        for core in range(2):
            total = recv_ref[place(part, core), 16:32, :].astype(F32)
            for high in range(1, 4):
                total = total + recv_ref[place(part, 2 * high + core), 16:32, :].astype(F32)
            proj_ref[16 * part : 16 * part + 16, LANES * core : LANES * core + LANES] = total.astype(BF16)
    lane = lane_iota(8)
    sub = lax.broadcasted_iota(jnp.int32, (8, LANES), 0)
    rows_ref[...] = jnp.zeros((LANES, LANES), F32)
    per_frame = jnp.zeros((8, LANES), F32)
    for pair in range(PAIRS):
        rows = recv_ref[place(0, pair), 32:40, :].astype(F32)
        for part in range(1, PARTS):
            rows = rows + recv_ref[place(part, pair), 32:40, :].astype(F32)
        rows_ref[2 * pair : 2 * pair + 2, :] = rows[0:2]
        rows = rows + pltpu.roll(rows, 64, 1)
        for head in range(2):
            inside = (lane < 2 * BLOCKS) & (lane % 2 == head)
            total = jnp.sum(jnp.where(inside, rows, 0.0), axis=1, keepdims=True)
            per_frame = jnp.where(lane == 2 * pair + head, total, per_frame)
    pre = shifted_steps(frame_ref, raw_ref, table_ref)
    pre_ref[...] = rows_ref[...].T[:, :heads] * sigmoid(pre)
    steps = lax.broadcasted_iota(jnp.int32, grad_ref.shape, 0)
    grad = jnp.zeros(grad_ref.shape, F32)
    for frame in range(4):
        grad = grad + jnp.where(steps == frame_ref[frame], per_frame[2 + frame : 3 + frame, :heads], 0.0)
    grad_ref[...] = grad


def total_kernel(own_ref, one_ref, two_ref, three_ref, write_ref, read_ref):
    even = own_ref[...].astype(F32) + two_ref[...].astype(F32)
    odd = one_ref[...].astype(F32) + three_ref[...].astype(F32)
    total = (even + odd).astype(BF16)
    write_ref[...] = total[:, :LANES]
    read_ref[...] = total[:, LANES:]


VMEM = pl.BlockSpec(memory_space=pltpu.VMEM)
SMEM = pl.BlockSpec(memory_space=pltpu.SMEM)


def call(kernel, name, in_specs, out_shape, scratch=(), cost=None):
    shapes = [jax.ShapeDtypeStruct(shape, dtype) for shape, dtype in out_shape]
    return pl.pallas_call(
        kernel,
        out_shape=shapes,
        in_specs=in_specs,
        out_specs=[VMEM] * len(shapes),
        scratch_shapes=list(scratch),
        compiler_params=PARAMS,
        cost_estimate=cost,
        name=name,
    )


def shards(
    activations, grad_out, write_proj, read_proj, step_raw, step_table, decay_rate, frame_step, scan_order
):
    heads = step_raw.shape[1]
    swap_core = [(i, i ^ 1) for i in range(SEQ)]
    (send,) = call(
        pack_kernel, "pack", [SMEM] + [VMEM] * 7, [((SEQ, SLOT_IN, LANES), BF16)]
    )(
        frame_step, scan_order.reshape(1, TOK), activations, grad_out, write_proj, read_proj,
        step_raw, step_table,
    )
    recv = lax.all_to_all(send, "seq", 0, 0, tiled=True)
    swap = lax.ppermute(recv, "seq", swap_core)
    tokens = ((LOCAL, LANES), BF16)
    sums = ((LOCAL, LANES), F32)
    blocks = ((BLOCKS, LANES, LANES), F32)
    x, dy, write, read, states, s_part, r_part, stat = call(
        unpack_kernel, "unpack", [SMEM, VMEM, VMEM],
        [tokens] * 4 + [((PARTS, SLOT_STATE, LANES), BF16), blocks, blocks, ((5, LANES, LANES), F32)],
        [pltpu.VMEM((LOCAL, LANES), F32), pltpu.VMEM((SEQ * 8, LANES), F32)],
    )(decay_rate, recv, swap)
    states = lax.all_to_all(states, "seq", 0, 0, tiled=True, axis_index_groups=STATE_GROUPS)
    u, gw, gr, t = call(
        inner_kernel, "inner", [VMEM] * 5, [sums] * 3 + [((LANES, LANES), F32)],
        cost=pl.CostEstimate(flops=10**9, bytes_accessed=4 * 2**20, transcendentals=2**18),
    )(x, dy, write, read, stat)
    out, keep, give = call(
        outer_kernel, "outer", [SMEM] + [VMEM] * 12,
        [((SEQ, SLOT_OUT, LANES), BF16), sums, sums],
        [pltpu.VMEM((BLOCKS, LANES, LANES), F32)] + [pltpu.VMEM((LOCAL, LANES), F32)] * 3,
    )(decay_rate, states, x, dy, write, read, s_part, r_part, stat, u, gw, gr, t)
    got = lax.ppermute(give, "seq", swap_core)
    (out,) = call(join_kernel, "join", [VMEM] * 3, [((SEQ, SLOT_OUT, LANES), BF16)])(out, keep, got)
    back = lax.all_to_all(out, "seq", 0, 0, tiled=True)
    act, proj, grad_pre, grad_table = call(
        finish_kernel, "finish", [SMEM] + [VMEM] * 3,
        [
            (activations.shape, BF16),
            ((TOK, 2 * LANES), BF16),
            (step_raw.shape, F32),
            (step_table.shape, F32),
        ],
        [pltpu.VMEM((LANES, LANES), F32)],
    )(frame_step, back, step_raw, step_table)
    ring = [lax.ppermute(proj, "head", [(i, (i + k) % 4) for i in range(4)]) for k in (1, 2, 3)]
    grad_write, grad_read = call(
        total_kernel, "total", [VMEM] * 4, [(write_proj.shape, BF16), (read_proj.shape, BF16)]
    )(proj, *ring)
    return (act, grad_write, grad_read, grad_pre, grad_table)


def solution(mesh):
    in_specs = (
        P("seq", "head"),
        P("seq", "head"),
        P("seq", None),
        P("seq", None),
        P("seq", "head"),
        P(None, "head"),
        P("head"),
        P(),
        P("seq"),
    )
    out_specs = (
        P("seq", "head"),
        P("seq", None),
        P("seq", None),
        P("seq", "head"),
        P(None, "head"),
    )
    return jax.shard_map(shards, mesh=mesh, in_specs=in_specs, out_specs=out_specs, check_vma=False)
```

time: 749 us -> 115 us (0.15)
  waiting for transfers between devices: 261 us -> 7.48 us
  blocking collectives: 299 us -> 65.8 us
  other arithmetic: 79.4 us -> 0 us
  starting transfers between devices: 57.4 us -> 9.11 us
  between operations: 16.3 us -> 0.79 us
  Pallas kernels: 0 us -> 14.5 us
  matrix products: 9.07 us -> 0 us
    psum x2 -> x0, blocking collectives: 261 us -> none  [the longest x1 246 us: shards(): grad_table = lax.psum(picked[:, None] * column[None, :], 'seq')]
    all_gather x2 -> x0, waiting for transfers between devices: 207 us -> none  [prefix(): gathered = jax.tree.map(lambda a: lax.all_gather(a, axis), part)]
    add x64 -> x0, other arithmetic: 75 us -> none  [the longest x63 75 us: combine_states(): jnp.exp(latter[0])[:, None, None] * earlier[1] + latter[1]]
    all_to_all x0 -> x2, blocking collectives: none -> 65.8 us  [the longest x1 38.7 us: shards(): recv = lax.all_to_all(send, 'seq', 0, 0, tiled=True)]
    all_to_all x8 -> x1, waiting for transfers between devices: 53.6 us -> 0.01 us  [shards(): lax.all_to_all(states, 'seq', 0, 0, tiled=True, axis_index_groups=STATE_G...]
    all_to_all x8 -> x1, starting transfers between devices: 57.3 us -> 4.13 us  [shards(): lax.all_to_all(states, 'seq', 0, 0, tiled=True, axis_index_groups=STATE_G...]
    all_gather x1 -> x0, blocking collectives: 38.3 us -> none  [prefix(): gathered = jax.tree.map(lambda a: lax.all_gather(a, axis), part)]
    unnamed x4 -> x48, local copies, waits for them, and re-layouts: 1.48 us -> 17.1 us
  transfers between devices with their start and end apart: 10 -> 6, of which waited for: 8 -> 4; matrix products, arithmetic and copies ran while one was open for 2% -> 1% of each run, Pallas kernels for 0% -> 2%
where the time goes in v1:
time: 115 us
  blocking collectives  65.8 us (57%)
  local copies, waits for them, and re-layouts  17.1 us (15%)
  Pallas kernels  14.5 us (13%)
  starting transfers between devices  9.11 us (8%)
  waiting for transfers between devices  7.48 us (7%)
    all_to_all x1, blocking collectives, shards(): recv = lax.all_to_all(send, 'seq', 0, 0, tiled=True)  38.7 us
    all_to_all x1, blocking collectives, shards(): back = lax.all_to_all(out, 'seq', 0, 0, tiled=True)  27.1 us
    unnamed x48, local copies, waits for them, and re-layouts  17.1 us
    pallas_call x1, Pallas kernels, shards(): call(outer_kernel, 'outer', [SMEM] + [VMEM] * 12, [((SEQ, SLOT_OUT, LANES...  4.74 us
    all_to_all x1, starting transfers between devices, shards(): lax.all_to_all(states, 'seq', 0, 0, tiled=True, axis_index_groups=STATE_G...  4.13 us
    pallas_call x1, Pallas kernels, shards(): call(unpack_kernel, 'unpack', [SMEM, VMEM, VMEM], [tokens] * 4 + [((PARTS...  3.8 us
    ppermute x3, waiting for transfers between devices, shards(): lax.ppermute(proj, 'head', [(i, (i + k) % 4) for i in range(4)])  3.8 us
    ppermute x3, starting transfers between devices, shards(): lax.ppermute(proj, 'head', [(i, (i + k) % 4) for i in range(4)])  3.61 us
  transfers between devices with their start and end apart: 6, of which 4 were waited for; matrix products, arithmetic and copies ran while one was open for 1% of the time, Pallas kernels for 2%

profile of v1, /device:TPU:1, one launch (start us, length us, event | category | flops | bytes accessed | tf_op | source)
XLA Modules:
  0.0 114.8 jit_solution(9927074374846844906)
XLA Ops:
  0.6 0.0 copy-start.18
  0.6 0.8 copy.14.raw_ref
  1.5 0.0 copy-start.16
  1.5 0.0 copy-start.17
  1.5 1.1 copy.15.table_ref
  2.6 0.0 copy-start.20
  2.6 0.0 copy-start.21
  2.6 0.6 copy-done.20
  3.2 0.0 copy-done.21
  3.2 0.7 pack.1
  4.0 0.0 copy-start.19
  4.0 38.7 %all_to_all.15.recv_ref = bf16[64,56,128]{2,1,0:T(8,128)(2,1)S(1)} all-to-all(bf16[64,56,128]{2,1,0:T(8,128)(2,1)S(1)} %pack.1), channel_id=1, replica_groups=mesh['seq'=64,'head'=4] {'seq'}, dimensions={0} | all-to-all | bytes 1835008 | tf_op jit(solution)/shard_map/all_to_all | solution.py:464
  42.7 0.3 collective-permute-start
  43.0 2.1 %collective-permute-done.swap_ref = bf16[64,56,128]{2,1,0:T(8,128)(2,1)S(1)} collective-permute-done((bf16[64,56,128]{2,1,0:T(8,128)(2,1)S(1)}, bf16[64,56,128]{2,1,0:T(8,128)(2,1)S(1)}, u32[]{:S(2)}, u32[]{:S(2)}) %collective-permute-start) | collective-permute-done | bytes 917536 | tf_op jit(solution)/shard_map/ppermute | solution.py:465
  45.1 3.8 %unpack.1 = (bf16[1024,128]{1,0:T(8,128)(2,1)S(1)}, bf16[1024,128]{1,0:T(8,128)(2,1)S(1)}, bf16[1024,128]{1,0:T(8,128)(2,1)S(1)}, bf16[1024,128]{1,0:T(8,128)(2,...) custom-call(f32[16]{0:T(128)S(1)} %copy-done.19, ...), custom_call_target="tpu_custom_call" | custom-call | tf_op jit(solution)/shard_map/unpack/pallas_call | solution.py:469
  49.0 0.7 copy-done
  49.7 0.7 copy-done.3
  50.4 0.7 copy-done.6
  51.1 0.7 copy-done.9
  51.8 0.7 copy-done.12
  52.5 4.1 %all-to-all-start.1 = ((bf16[8,136,128]{2,1,0:T(8,128)(2,1)}), bf16[8,136,128]{2,1,0:T(8,128)(2,1)S(1)}, u32[]{:S(2)}, u32[]{:S(2)}) async-start(bf16[8,136,128]{2,1,0:T(8,128)(2,1)} %get-tuple-element.26), calls=%async_computation.1 | async-start | bytes 557056 | tf_op jit(solution)/shard_map/all_to_all | solution.py:474
  56.6 1.0 copy-done.1
  57.6 0.9 copy-done.4
  58.5 0.9 copy-done.7
  59.5 0.9 copy-done.10
  60.4 0.9 copy-done.13
  61.4 2.7 %inner.1 = (f32[1024,128]{1,0:T(8,128)S(1)}, f32[1024,128]{1,0:T(8,128)S(1)}, f32[1024,128]{1,0:T(8,128)S(1)}, f32[128,128]{1,0:T(8,128)S(1)}) custom-call(bf16[1024,128]{1,0:T(8,128)(2,1)S(1)} %copy-done.4, bf16[1024,128]{1,0:T(8,128)(2,1)S(1)} %copy-done.7, bf16[1024,128]{1,0:T(8,128)(2,1)S(1)} %copy-done.10, bf16[1024,128]{1,0:T(8,128)(2,1)S(1)} %copy-done.13, ...), custom_call_target="tpu_custom_call" | custom-call | flops 1000000000 | bytes 4194304 | tf_op jit(solution)/shard_map/inner/pallas_call | solution.py:475
  64.0 0.0 all-to-all-done.1.recv_ref
  64.1 1.0 copy-done.2
  65.0 0.9 copy-done.5
  66.0 0.9 copy-done.8
  66.9 0.9 copy-done.11
  67.9 0.9 copy-done.14
  68.8 4.7 %outer.1 = (bf16[64,40,128]{2,1,0:T(8,128)(2,1)S(1)}, f32[1024,128]{1,0:T(8,128)S(1)}, f32[1024,128]{1,0:T(8,128)S(1)}) custom-call(f32[16]{0:T(128)S(1)} %copy-done.19, bf16[8,136,128]{2,1,0:T(8,128)(2,1)S(1)} %all-to-all-done.1.recv_ref, bf16[1024,128]{1,0:T(8,128)(2,1)S(1)} %copy-done.5, bf16[1024,128]{1,0:T(8,128)(2,1)S(1)} %copy-done.8, ...), custom_call_target="tpu_custom_call" | custom-call | tf_op jit(solution)/shard_map/outer/pallas_call | solution.py:479
  73.6 1.0 collective-permute-start.1
  74.6 1.5 %collective-permute-done.1.got_ref = f32[1024,128]{1,0:T(8,128)S(1)} collective-permute-done((f32[1024,128]{1,0:T(8,128)S(1)}, f32[1024,128]{1,0:T(8,128)S(1)}, u32[]{:S(2)}, u32[]{:S(2)}) %collective-permute-start.1) | collective-permute-done | bytes 524320 | tf_op jit(solution)/shard_map/ppermute | solution.py:484
  76.1 0.1 join.1
  76.2 27.1 %all_to_all.16.recv_ref = bf16[64,40,128]{2,1,0:T(8,128)(2,1)S(1)} all-to-all(bf16[64,40,128]{2,1,0:T(8,128)(2,1)S(1)} %join.1), channel_id=1, replica_groups=mesh['seq'=64,'head'=4] {'seq'}, dimensions={0} | all-to-all | bytes 1310720 | tf_op jit(solution)/shard_map/all_to_all | solution.py:486
  103.4 1.9 %finish.1 = (bf16[128,1024]{1,0:T(8,128)(2,1)}, bf16[128,256]{1,0:T(8,128)(2,1)S(1)}, f32[128,16]{1,0:T(8,128)S(1)}, f32[1000,16]{1,0:T(8,128)S(1)}) custom-call(s32[4]{0:T(128)S(1)} %copy-done.20, bf16[64,40,128]{2,1,0:T(8,128)(2,1)S(1)} %all_to_all.16.recv_ref, f32[128,16]{1,0:T(8,128)S(1)} %copy.14.raw_ref, f32[1000,16]{1,0:T(8,128)S(1)} %copy.15.table_ref), custom_call_target="tpu_custom_call" | custom-call | tf_op jit(solution)/shard_map/finish/pallas_call | solution.py:487
  105.3 2.5 %collective-permute-start.4 = (bf16[128,256]{1,0:T(8,128)(2,1)S(1)}, bf16[128,256]{1,0:T(8,128)(2,1)S(1)}, u32[]{:S(2)}, u32[]{:S(2)}) collective-permute-start(bf16[128,256]{1,0:T(8,128)(2,1)S(1)} %get-tuple-element.42.own_ref), channel_id=1, source_target_pairs={{0,3},{1,0},{2,1},{3,2},{4,7},{5,4},{6,5},{7,6},{8,11},{9,8},{10,9... | collective-permute-start | bytes 196616 | tf_op jit(solution)/shard_map/ppermute | solution.py:497
  107.8 0.5 collective-permute-start.3
  108.3 0.6 collective-permute-start.2
  108.9 0.7 copy.18
  109.6 0.8 copy.19
  110.4 0.0 collective-permute-done.4.three_ref
  110.4 2.1 %collective-permute-done.3.two_ref = bf16[128,256]{1,0:T(8,128)(2,1)S(1)} collective-permute-done((bf16[128,256]{1,0:T(8,128)(2,1)S(1)}, bf16[128,256]{1,0:T(8,128)(2,1)S(1)}, u32[]{:S(2)}, u32[]{:S(2)}) %collective-permute-start.3) | collective-permute-done | bytes 65568 | tf_op jit(solution)/shard_map/ppermute | solution.py:497
  112.4 1.7 %collective-permute-done.2.one_ref = bf16[128,256]{1,0:T(8,128)(2,1)S(1)} collective-permute-done((bf16[128,256]{1,0:T(8,128)(2,1)S(1)}, bf16[128,256]{1,0:T(8,128)(2,1)S(1)}, u32[]{:S(2)}, u32[]{:S(2)}) %collective-permute-start.2) | collective-permute-done | bytes 65568 | tf_op jit(solution)/shard_map/ppermute | solution.py:497
  114.2 0.7 total.1
  (21 shorter events, 0.0 us)
Async XLA Ops:
  0.6 2.0 %copy-start.18 = (bf16[128,128]{1,0:T(8,128)(2,1)S(1)}, bf16[128,128]{1,0:T(8,128)(2,1)}, u32[]{:S(2)}) copy-start(bf16[128,128]{1,0:T(8,128)(2,1)} %c_ref.1) | copy-start | bytes 98308
  1.4 1.2 %copy-start.15 = (bf16[128,1024]{1,0:T(8,128)(2,1)S(1)}, bf16[128,1024]{1,0:T(8,128)(2,1)}, u32[]{:S(2)}) copy-start(bf16[128,1024]{1,0:T(8,128)(2,1)} %x_ref.1) | copy-start | bytes 786436
  1.5 1.2 %copy-start.16 = (bf16[128,1024]{1,0:T(8,128)(2,1)S(1)}, bf16[128,1024]{1,0:T(8,128)(2,1)}, u32[]{:S(2)}) copy-start(bf16[128,1024]{1,0:T(8,128)(2,1)} %dy_ref.1) | copy-start | bytes 786436
  1.5 1.2 %copy-start.17 = (bf16[128,128]{1,0:T(8,128)(2,1)S(1)}, bf16[128,128]{1,0:T(8,128)(2,1)}, u32[]{:S(2)}) copy-start(bf16[128,128]{1,0:T(8,128)(2,1)} %b_ref.1) | copy-start | bytes 98308
  2.6 0.7 copy-start.20
  2.6 0.7 copy-start.21
  4.0 41.2 %copy-start.19 = (f32[16]{0:T(128)S(1)}, f32[16]{0:T(128)}, u32[]{:S(2)}) copy-start(f32[16]{0:T(128)} %decay_ref.3) | copy-start | bytes 196
  42.7 2.5 %collective-permute-start = (bf16[64,56,128]{2,1,0:T(8,128)(2,1)S(1)}, bf16[64,56,128]{2,1,0:T(8,128)(2,1)S(1)}, u32[]{:S(2)}, u32[]{:S(2)}) collective-permute-start(bf16[64,56,128]{2,1,0:T(8,128)(2,1)S(1)} %all_to_all.15.recv_ref), channel_id=1, source_target_pairs={{0,4},{4,0},{8,12},{12,8},{16,20},{20,16},{24,28},{28,24},{32,36},... | collective-permute-start | bytes 2752520 | tf_op jit(solution)/shard_map/ppermute | solution.py:465
  49.0 0.7 copy-start
  49.7 0.7 copy-start.3
  50.4 0.7 copy-start.6
  51.1 0.7 copy-start.9
  51.8 0.7 copy-start.12
  52.5 11.6 %all-to-all-start.1 = ((bf16[8,136,128]{2,1,0:T(8,128)(2,1)}), bf16[8,136,128]{2,1,0:T(8,128)(2,1)S(1)}, u32[]{:S(2)}, u32[]{:S(2)}) async-start(bf16[8,136,128]{2,1,0:T(8,128)(2,1)} %get-tuple-element.26), calls=%async_computation.1 | async-start | bytes 557056 | tf_op jit(solution)/shard_map/all_to_all | solution.py:474
  56.6 1.0 copy-start.1
  57.6 0.9 copy-start.4
  58.5 0.9 copy-start.7
  59.5 0.9 copy-start.10
  60.4 0.9 copy-start.13
  64.1 1.0 copy-start.2
  65.0 0.9 copy-start.5
  66.0 0.9 copy-start.8
  66.9 0.9 copy-start.11
  67.9 0.9 copy-start.14
  73.6 2.6 %collective-permute-start.1 = (f32[1024,128]{1,0:T(8,128)S(1)}, f32[1024,128]{1,0:T(8,128)S(1)}, u32[]{:S(2)}, u32[]{:S(2)}) collective-permute-start(f32[1024,128]{1,0:T(8,128)S(1)} %get-tuple-element.40), channel_id=1, source_target_pairs={{0,4},{4,0},{8,12},{12,8},{16,20},{20,16},{24,28},{28,24},{32,36},... | collective-permute-start | bytes 1572872 | tf_op jit(solution)/shard_map/ppermute | solution.py:484
  105.3 5.1 %collective-permute-start.4 = (bf16[128,256]{1,0:T(8,128)(2,1)S(1)}, bf16[128,256]{1,0:T(8,128)(2,1)S(1)}, u32[]{:S(2)}, u32[]{:S(2)}) collective-permute-start(bf16[128,256]{1,0:T(8,128)(2,1)S(1)} %get-tuple-element.42.own_ref), channel_id=1, source_target_pairs={{0,3},{1,0},{2,1},{3,2},{4,7},{5,4},{6,5},{7,6},{8,11},{9,8},{10,9... | collective-permute-start | bytes 196616 | tf_op jit(solution)/shard_map/ppermute | solution.py:497
  107.8 4.7 %collective-permute-start.3 = (bf16[128,256]{1,0:T(8,128)(2,1)S(1)}, bf16[128,256]{1,0:T(8,128)(2,1)S(1)}, u32[]{:S(2)}, u32[]{:S(2)}) collective-permute-start(bf16[128,256]{1,0:T(8,128)(2,1)S(1)} %get-tuple-element.42.own_ref), channel_id=1, source_target_pairs={{0,2},{1,3},{2,0},{3,1},{4,6},{5,7},{6,4},{7,5},{8,10},{9,11},{10,... | collective-permute-start | bytes 196616 | tf_op jit(solution)/shard_map/ppermute | solution.py:497
  108.3 5.9 %collective-permute-start.2 = (bf16[128,256]{1,0:T(8,128)(2,1)S(1)}, bf16[128,256]{1,0:T(8,128)(2,1)S(1)}, u32[]{:S(2)}, u32[]{:S(2)}) collective-permute-start(bf16[128,256]{1,0:T(8,128)(2,1)S(1)} %get-tuple-element.42.own_ref), channel_id=1, source_target_pairs={{0,1},{1,2},{2,3},{3,0},{4,5},{5,6},{6,7},{7,4},{8,9},{9,10},{10,1... | collective-permute-start | bytes 196616 | tf_op jit(solution)/shard_map/ppermute | solution.py:497

commit v2 on v1

v2 whole, which is shorter than its diff:
```python
import jax
import jax.numpy as jnp
from jax import lax
from jax.experimental import pallas as pl
from jax.experimental.pallas import tpu as pltpu
from jax.sharding import PartitionSpec as P

F32 = jnp.float32
BF16 = jnp.bfloat16
FRAME_TOK = 2048
TOK = 128
LANES = 128
SEQ = 64
PARTS = 8
PAIRS = 8
BLOCKS = 8
SLOT_IN = 56
SLOT_STATE = 136
SLOT_OUT = 40
LOCAL = BLOCKS * TOK
PARAMS = pltpu.CompilerParams(vmem_limit_bytes=32 * 1024 * 1024)


def place(part, pair):
    y, low = part // 2, part % 2
    high, core = pair // 2, pair % 2
    return y * 16 + (high * 2 + low) * 2 + core


def my_place():
    me = lax.axis_index("seq")
    part = (me // 16) * 2 + (me // 2) % 2
    pair = ((me // 4) % 4) * 2 + me % 2
    return part, pair, me % 2


STATE_GROUPS = [[place(part, pair) for part in range(PARTS)] for pair in range(PAIRS)]


def nn(a, b):
    return lax.dot_general(a, b, (((1,), (0,)), ((), ())), preferred_element_type=F32)


def nt(a, b):
    return lax.dot_general(a, b, (((1,), (1,)), ((), ())), preferred_element_type=F32)


def split(value):
    high = value.astype(BF16)
    return high, (value - high.astype(F32)).astype(BF16)


def lane_iota(rows):
    return lax.broadcasted_iota(jnp.int32, (rows, LANES), 1)


def heads_over_lanes(first, second, rows):
    return jnp.where(lane_iota(rows) < 64, first, second)


def softplus(value):
    return jnp.maximum(value, 0.0) + jnp.log1p(jnp.exp(-jnp.abs(value)))


def sigmoid(value):
    return 1.0 / (1.0 + jnp.exp(-value))


def shifted_steps(frame_ref, raw, table):
    frame_here = lax.axis_index("seq") * TOK // FRAME_TOK
    index = frame_ref[frame_here]
    columns = lax.broadcasted_iota(jnp.int32, table.shape, 1)
    shift = jnp.sum(jnp.where(columns == index, table, 0.0), axis=1, keepdims=True)
    return raw + shift


def pack_kernel(frame_ref, order_ref, *refs):
    sources, out_ref, targets, sems = refs[:6], refs[6], refs[7:13], refs[13]
    copies = [
        pltpu.make_async_copy(source, target, sems.at[i])
        for i, (source, target) in enumerate(zip(sources, targets))
    ]
    for copy in copies:
        copy.start()
    raw_ref, table_ref, b_ref, c_ref, x_ref, dy_ref = targets
    order = jnp.broadcast_to(order_ref[...].astype(F32), (TOK, TOK)).T
    lane = lane_iota(TOK)
    token = ((lane % 64) * 2 + lane // 64).astype(F32)
    steps = lax.broadcasted_iota(jnp.int32, (TOK, TOK), 0).astype(F32)
    position = jnp.sum(jnp.where(order == token, steps, 0.0), axis=0, keepdims=True)
    copies[0].wait()
    copies[1].wait()
    pre = shifted_steps(frame_ref, raw_ref[...], table_ref[...])
    delta = softplus(pre).astype(BF16).astype(F32)
    gate = sigmoid(pre)
    gate_high = gate.astype(BF16).astype(F32)
    gate_low = gate - gate_high
    for copy in copies[2:]:
        copy.wait()
    for pair in range(PAIRS):
        own = slice(2 * pair, 2 * pair + 2)
        rows = jnp.concatenate(
            [position, delta[own], gate_high[own], gate_low[own], jnp.zeros((1, LANES), F32)], axis=0
        ).astype(BF16)
        proj_ref = c_ref if pair % 2 else b_ref
        columns = slice(LANES * pair, LANES * pair + LANES)
        for part in range(PARTS):
            slot = place(part, pair)
            tokens = slice(16 * part, 16 * part + 16)
            out_ref[slot, 0:16, :] = x_ref[tokens, columns]
            out_ref[slot, 16:32, :] = dy_ref[tokens, columns]
            out_ref[slot, 32:48, :] = proj_ref[tokens, :]
            out_ref[slot, 48:56, :] = rows


def to_columns(first, second):
    head_one = jnp.concatenate([first, pltpu.roll(first, LANES - 1, 1)], axis=0)
    head_two = jnp.concatenate([pltpu.roll(second, 1, 1), second], axis=0)
    return jnp.where(lane_iota(TOK) % 2 == 0, head_one, head_two)


def slope_lanes(decay_ref, pair, rows):
    return jnp.where(lane_iota(rows) % 2 == 0, -decay_ref[2 * pair], -decay_ref[2 * pair + 1])


def block_lanes(columns, block, rows):
    j = 2 * block
    return heads_over_lanes(columns[:, j : j + 1], columns[:, j + 1 : j + 2], rows)


def block_rows(block):
    return slice(block * TOK, block * TOK + TOK)


def stack(value):
    return jnp.concatenate(split(value), axis=0)


def twice(value):
    return jnp.concatenate([value, value], axis=1)


def turned(value):
    return value.astype(F32).T.astype(BF16)


def twice_split(value):
    return jnp.concatenate(split(value), axis=1)


def spread(value, wide, target_ref, base):
    wide[...] = value.reshape(SEQ * 16, LANES)
    for row in range(16):
        start = base + row * 64
        target_ref[start : start + 64, :] = wide[pl.ds(row, 64, stride=16), :].astype(BF16)


def unpack_kernel(
    decay_ref, recv_ref, data_ref, proj_ref, weight_ref, wide, wide_two, wide_three, misc
):
    part, pair, core = my_place()
    spread(recv_ref[:, 0:16, :].astype(F32), wide, data_ref, 0)
    spread(recv_ref[:, 16:32, :].astype(F32), wide_two, data_ref, LOCAL)
    spread(recv_ref[:, 32:48, :].astype(F32), wide_three, proj_ref, 0)
    misc[...] = recv_ref[:, 48:56, :].astype(F32).reshape(SEQ * 8, LANES)
    shift = (LANES - 16 * part) % LANES

    def own_lanes(row):
        return pltpu.roll(misc[pl.ds(row, 64, stride=8), :], shift, 1)

    steps = to_columns(own_lanes(1), own_lanes(2))
    gates_high = to_columns(own_lanes(3), own_lanes(4))
    gates_low = to_columns(own_lanes(5), own_lanes(6))
    pos_rows = jnp.concatenate(
        [misc[pl.ds(part * 64 + 8 * block, 1), :] for block in range(BLOCKS)], axis=0
    )
    pos_cols = jnp.concatenate([pos_rows, jnp.zeros((LANES - BLOCKS, LANES), F32)], axis=0).T
    lane = lane_iota(TOK)
    steps_bf = steps.astype(BF16)
    sums = jnp.zeros((TOK, LANES), F32)
    for block in range(BLOCKS):
        later = (pos_cols[:, block : block + 1] >= pos_rows[block : block + 1, :]).astype(F32).astype(BF16)
        sums = jnp.where(lane // 2 == block, nn(later, steps_bf), sums)
    slopes = slope_lanes(decay_ref, pair, TOK)
    logs = sums * slopes
    totals = jnp.sum(steps, axis=0, keepdims=True) * slopes[:1]
    short = jnp.where(lane_iota(1) < 2 * BLOCKS, totals, 0.0)
    onward = short
    until = pltpu.roll(short, 2, 1)
    for reach in (2, 4, 8):
        onward = onward + pltpu.roll(onward, LANES - reach, 1)
        until = until + pltpu.roll(until, reach, 1)
    base = 2 * LOCAL
    data_ref[base : base + TOK, :] = steps_bf
    data_ref[base + TOK : base + 2 * TOK, :] = gates_high.astype(BF16)
    data_ref[base + 2 * TOK : base + 3 * TOK, :] = gates_low.astype(BF16)
    data_ref[base + 3 * TOK : base + 4 * TOK, :] = pos_cols.astype(BF16)
    whole = heads_over_lanes(onward[:, 0:1], onward[:, 1:2], 1)
    top = whole.astype(BF16).astype(F32)
    middle = (whole - top).astype(BF16).astype(F32)
    bottom = whole - top - middle
    tail = jnp.concatenate([top, middle, bottom, jnp.zeros((13, LANES), F32)], axis=0).astype(BF16)
    weight_ref[4 * LOCAL : 4 * LOCAL + 16, :] = tail
    weights = steps * jnp.exp(jnp.minimum(onward - logs, 0.0))
    starts = jnp.exp(jnp.minimum(logs + until, 0.0))
    for block in range(BLOCKS):
        rows = block_rows(block)
        later_rows = slice(LOCAL + block * TOK, LOCAL + block * TOK + TOK)
        first = block * 2 * TOK
        weight_ref[first : first + 2 * TOK, :] = stack(
            data_ref[rows, :].astype(F32) * block_lanes(weights, block, TOK)
        )
        first = 2 * LOCAL + block * 2 * TOK
        weight_ref[first : first + 2 * TOK, :] = stack(
            data_ref[later_rows, :].astype(F32) * block_lanes(starts, block, TOK)
        )


def states_kernel(mine_ref, swap_ref, weight_ref, data_ref, all_ref, send_ref, wide):
    part, pair, core = my_place()
    all_ref[0 : 2 * LOCAL, :] = data_ref[0 : 2 * LOCAL, :]
    all_ref[4 * LOCAL : 4 * LOCAL + 4 * TOK, :] = data_ref[2 * LOCAL : 2 * LOCAL + 4 * TOK, :]
    spread(swap_ref[:, 32:48, :].astype(F32), wide, all_ref, 3 * LOCAL)

    @pl.when(core == 0)
    def _():
        all_ref[2 * LOCAL : 3 * LOCAL, :] = mine_ref[...]

    @pl.when(core == 1)
    def _():
        all_ref[2 * LOCAL : 3 * LOCAL, :] = all_ref[3 * LOCAL : 4 * LOCAL, :]
        all_ref[3 * LOCAL : 4 * LOCAL, :] = mine_ref[...]

    state = jnp.zeros((LANES, LANES), F32)
    adjoint = jnp.zeros((LANES, LANES), F32)
    for block in range(BLOCKS):
        write = all_ref[2 * LOCAL + block * TOK : 2 * LOCAL + block * TOK + TOK, :]
        read = all_ref[3 * LOCAL + block * TOK : 3 * LOCAL + block * TOK + TOK, :]
        first = block * 2 * TOK
        state = state + nn(twice(turned(write)), weight_ref[first : first + 2 * TOK, :])
        first = 2 * LOCAL + block * 2 * TOK
        adjoint = adjoint + nn(twice(turned(read)), weight_ref[first : first + 2 * TOK, :])
    state = state.astype(BF16)
    adjoint = adjoint.astype(BF16)
    for slot in range(PARTS):
        after = slot > part

        @pl.when(after)
        def _():
            send_ref[slot, 0:128, :] = state

        @pl.when(jnp.logical_not(after))
        def _():
            send_ref[slot, 0:128, :] = adjoint

        send_ref[slot, 128:136, :] = weight_ref[4 * LOCAL : 4 * LOCAL + 16, :][:8]


def inner_kernel(decay_ref, all_ref, sums_ref, grad_ref, data_ref):
    part, pair, core = my_place()
    base = 4 * LOCAL
    steps_bf = all_ref[base : base + TOK, :]
    steps = steps_bf.astype(F32)
    pos_cols = all_ref[base + 3 * TOK : base + 4 * TOK, :].astype(F32)
    pos_rows = pos_cols.T[:8]
    grad_ref[2 * LOCAL : 2 * LOCAL + TOK, :] = steps
    grad_ref[2 * LOCAL + TOK : 2 * LOCAL + 2 * TOK, :] = (
        all_ref[base + TOK : base + 2 * TOK, :].astype(F32) + all_ref[base + 2 * TOK : base + 3 * TOK, :].astype(F32)
    )
    grad_ref[2 * LOCAL + 2 * TOK : 2 * LOCAL + 3 * TOK, :] = jnp.zeros((TOK, LANES), F32)
    lane = lane_iota(TOK)
    sums = jnp.zeros((TOK, LANES), F32)
    masks = 3 * LOCAL
    for block in range(BLOCKS):
        pos_col = pos_cols[:, block : block + 1]
        pos_row = pos_rows[block : block + 1, :]
        behind = (pos_col >= pos_row).astype(F32).astype(BF16)
        first = masks + block * 2 * TOK
        data_ref[first : first + TOK, :] = (pos_row >= pos_col).astype(F32).astype(BF16)
        data_ref[first + TOK : first + 2 * TOK, :] = behind
        sums = jnp.where(lane // 2 == block, nn(behind, steps_bf), sums)
    slopes = slope_lanes(decay_ref, pair, TOK)
    logs = sums * slopes
    log_rows = logs.T
    totals = jnp.sum(steps, axis=0, keepdims=True) * slopes[:1]
    starts = jnp.exp(logs)
    ends = steps * jnp.exp(totals - logs)
    data_ref[0:LOCAL, :] = all_ref[0:LOCAL, :]
    data_ref[LOCAL : 3 * LOCAL, :] = all_ref[2 * LOCAL : 4 * LOCAL, :]
    for block in range(BLOCKS):
        rows = block_rows(block)

        def piece(number):
            return all_ref[number * LOCAL + block * TOK : number * LOCAL + block * TOK + TOK, :]

        def sums_rows(number):
            return slice(number * LOCAL + block * TOK, number * LOCAL + block * TOK + TOK)

        x, dy, write, read = piece(0), piece(1), piece(2), piece(3)
        sums_ref[6 * LOCAL + block : 6 * LOCAL + block + 1, :] = block_lanes(totals, block, 1)
        end = block_lanes(ends, block, TOK)
        grad_ref[LOCAL + block * TOK : LOCAL + block * TOK + TOK, :] = end
        xe = x.astype(F32) * end
        ds = dy.astype(F32) * block_lanes(starts, block, TOK)
        first = block * 2 * TOK
        sums_ref[sums_rows(4), :] = ds
        sums_ref[sums_rows(5), :] = xe
        sums_ref[sums_rows(2), :] = nn(twice(turned(write)), stack(xe))
        sums_ref[sums_rows(3), :] = nn(twice(turned(read)), stack(ds))
        ahead = pos_rows[block : block + 1, :] >= pos_cols[:, block : block + 1]
        behind = data_ref[masks + first + TOK : masks + first + 2 * TOK, :]
        cross = nt(write, read)
        zero = jnp.zeros_like(dy)
        x_heads = (jnp.where(lane < 64, x, zero), jnp.where(lane < 64, zero, x))
        dy_stack = jnp.concatenate(
            [jnp.where(lane < 64, dy, zero), jnp.where(lane < 64, zero, dy)], axis=0
        )
        carry, mixed, seen = [], [], []
        for head in range(2):
            j = 2 * block + head
            gap = log_rows[j : j + 1, :] - logs[:, j : j + 1]
            decay = jnp.exp(jnp.where(ahead, gap, -1e30))
            carry.append(decay * cross)
            mixed.append(decay * (nt(x_heads[head], dy) * steps[:, j : j + 1]))
            seen.append(twice_split(mixed[head] * cross))
        crossed = nn(jnp.concatenate(seen, axis=0), jnp.concatenate([behind, behind], axis=0))
        for head in range(2):
            j = 2 * LOCAL + 2 * TOK + 2 * block + head
            own = jnp.where(ahead, crossed[head * TOK : head * TOK + TOK], 0.0)
            grad_ref[j : j + 1, :] = jnp.sum(own, axis=0, keepdims=True)
        high, low = split(jnp.concatenate(carry, axis=1))
        grad_ref[rows, :] = block_lanes(steps, block, TOK) * (nn(high, dy_stack) + nn(low, dy_stack))
        both = mixed[0] + mixed[1]
        sums_ref[sums_rows(0), :] = nn(twice_split(both), jnp.concatenate([read, read], axis=0))
        sums_ref[sums_rows(1), :] = nn(twice_split(both.T), jnp.concatenate([write, write], axis=0))


def outer_kernel(recv_ref, sums_ref, keep_ref, give_ref, all_ref, adj, wide_w, wide_r):
    part, pair, core = my_place()

    def arrive(slot, state):
        tail = recv_ref[slot, 128:136, :].astype(F32)
        total = tail[0:1] + tail[1:2] + tail[2:3]
        return state * jnp.exp(total) + recv_ref[slot, 0:128, :].astype(F32)

    zero = jnp.zeros((LANES, LANES), F32)
    state = lax.fori_loop(0, part, arrive, zero)
    adjoint = lax.fori_loop(0, PARTS - 1 - part, lambda k, a: arrive(PARTS - 1 - k, a), zero)
    keeps = jnp.exp(sums_ref[6 * LOCAL : 6 * LOCAL + 8, :])

    def sums_rows(number, block):
        return slice(number * LOCAL + block * TOK, number * LOCAL + block * TOK + TOK)

    for block in reversed(range(BLOCKS)):
        adj[block] = adjoint
        adjoint = adjoint * keeps[block : block + 1] + sums_ref[sums_rows(3, block), :]
    overlaps = []
    for block in range(BLOCKS):
        adjoint = adj[block]
        state_high, state_low = split(state)
        adj_high, adj_low = split(adjoint)
        first = block * 2 * TOK
        all_ref[4 * LOCAL + first : 4 * LOCAL + first + TOK, :] = state_high
        all_ref[4 * LOCAL + first + TOK : 4 * LOCAL + first + 2 * TOK, :] = state_low
        all_ref[6 * LOCAL + first : 6 * LOCAL + first + TOK, :] = adj_high
        all_ref[6 * LOCAL + first + TOK : 6 * LOCAL + first + 2 * TOK, :] = adj_low
        keep = keeps[block : block + 1]
        overlaps.append(jnp.sum(adjoint * state, axis=0, keepdims=True) * keep)
        ds_high, ds_low = split(sums_ref[sums_rows(4, block), :])
        xe_high, xe_low = split(sums_ref[sums_rows(5, block), :])
        all_ref[first : first + TOK, :] = ds_high
        all_ref[first + TOK : first + 2 * TOK, :] = ds_low
        all_ref[2 * LOCAL + first : 2 * LOCAL + first + TOK, :] = xe_high
        all_ref[2 * LOCAL + first + TOK : 2 * LOCAL + first + 2 * TOK, :] = xe_low
        gr = sums_ref[sums_rows(1, block), :] + (
            nt(jnp.concatenate([ds_high, ds_low], axis=1), twice(state_high)) + nt(ds_high, state_low)
        )
        gw = sums_ref[sums_rows(0, block), :] + (
            nt(jnp.concatenate([xe_high, xe_low], axis=1), twice(adj_high)) + nt(xe_high, adj_low)
        )
        for half in range(2):
            out_rows = pl.ds(2 * block + half, 64, stride=16)
            wide_w[out_rows, :] = gw[64 * half : 64 * half + 64]
            wide_r[out_rows, :] = gr[64 * half : 64 * half + 64]
        state = state * keep + sums_ref[sums_rows(2, block), :]
    overlaps = jnp.concatenate(overlaps, axis=0)
    top = overlaps.astype(BF16).astype(F32)
    middle = (overlaps - top).astype(BF16).astype(F32)
    bottom = overlaps - top - middle
    all_ref[8 * LOCAL : 8 * LOCAL + 32, :] = jnp.concatenate(
        [top, middle, bottom, jnp.zeros((8, LANES), F32)], axis=0
    ).astype(BF16)

    @pl.when(core == 0)
    def _():
        keep_ref[...] = wide_w[...]
        give_ref[...] = wide_r[...]

    @pl.when(core == 1)
    def _():
        keep_ref[...] = wide_r[...]
        give_ref[...] = wide_w[...]


def grads_kernel(decay_ref, data_ref, all_ref, grad_ref, out_ref, wide):
    part, pair, core = my_place()
    slopes = slope_lanes(decay_ref, pair, TOK)
    base = 2 * LOCAL
    steps = grad_ref[base : base + TOK, :]
    gates = grad_ref[base + TOK : base + 2 * TOK, :]
    lane = lane_iota(TOK)
    tail = all_ref[8 * LOCAL : 8 * LOCAL + 32, :].astype(F32)
    overlaps = tail[0:8] + tail[8:16] + tail[16:24]
    row_lane = lane_iota(8)
    row = lax.broadcasted_iota(jnp.int32, (8, LANES), 0)
    first = jnp.sum(jnp.where(row_lane < 64, overlaps, 0.0), axis=1, keepdims=True)
    second = jnp.sum(jnp.where(row_lane < 64, 0.0, overlaps), axis=1, keepdims=True)
    kept = jnp.where(row_lane == 2 * row, first, jnp.where(row_lane == 2 * row + 1, second, 0.0))
    log_grad = grad_ref[base + 2 * TOK : base + 3 * TOK, :].T + jnp.sum(kept, axis=0, keepdims=True)
    sub = lax.broadcasted_iota(jnp.int32, (2 * LANES, LANES), 0) % LANES // 64
    pick_lane = lax.broadcasted_iota(jnp.int32, (2 * LANES, LANES), 1)
    direct = jnp.zeros((TOK, LANES), F32)
    for block in range(BLOCKS):
        rows = block_rows(block)
        lo = block * 2 * TOK

        def both(number):
            start = number * LOCAL + lo
            return all_ref[start : start + TOK, :].astype(F32) + all_ref[start + TOK : start + 2 * TOK, :].astype(F32)

        x = data_ref[rows, :].astype(F32)
        write = data_ref[LOCAL + block * TOK : LOCAL + block * TOK + TOK, :]
        read = data_ref[2 * LOCAL + block * TOK : 2 * LOCAL + block * TOK + TOK, :]
        carried = nn(twice(write), all_ref[6 * LOCAL + lo : 6 * LOCAL + lo + 2 * TOK, :])
        recalled = nn(twice(read), all_ref[4 * LOCAL + lo : 4 * LOCAL + lo + 2 * TOK, :])
        act = grad_ref[rows, :] + grad_ref[LOCAL + block * TOK : LOCAL + block * TOK + TOK, :] * carried
        wide[pl.ds(2 * block, 64, stride=16), :] = act[:64]
        wide[pl.ds(2 * block + 1, 64, stride=16), :] = act[64:]
        products = jnp.concatenate([both(0) * recalled, both(2) * carried, x * act], axis=0)
        pick = (pick_lane == 2 * block + sub).astype(F32).astype(BF16)
        sums = nn(twice_split(products), pick)
        direct = direct + sums[2 * TOK :]
        ahead = data_ref[3 * LOCAL + lo : 3 * LOCAL + lo + TOK, :]
        behind = data_ref[3 * LOCAL + lo + TOK : 3 * LOCAL + lo + 2 * TOK, :]
        added = nn(twice(ahead), stack(sums[:TOK])) + nn(twice(behind), stack(sums[TOK : 2 * TOK]))
        log_grad = log_grad + jnp.where(lane // 2 == block, added, 0.0)

    grad_step = direct / steps + slopes * (log_grad - direct)
    grad_step = jnp.where(lane < 2 * BLOCKS, grad_step, 0.0).astype(BF16).astype(F32)
    grad_pre = grad_step * gates
    frames = []
    for frame in range(4):
        low_rows = slice(16 * frame, 16 * frame + 16)
        high_rows = slice(64 + 16 * frame, 80 + 16 * frame)
        frames.append(jnp.sum(grad_pre[low_rows] + grad_pre[high_rows], axis=0, keepdims=True))
    frames = jnp.concatenate(frames + [jnp.zeros((4, LANES), F32)], axis=0)
    frames_high = frames.astype(BF16).astype(F32)
    frames = frames_high + pltpu.roll(frames - frames_high, 64, 1)

    even = lane_iota(64) % 2 == 0
    top, bottom = grad_step[:64], grad_step[64:]
    shift = 16 * part
    row_one = pltpu.roll(jnp.where(even, top, pltpu.roll(bottom, 1, 1)), shift, 1)
    row_two = pltpu.roll(jnp.where(even, pltpu.roll(top, LANES - 1, 1), bottom), shift, 1)
    misc = jnp.concatenate(
        [
            row_one[:, None, :],
            row_two[:, None, :],
            jnp.broadcast_to(frames[None, :4, :], (SEQ, 4, LANES)),
            jnp.zeros((SEQ, 2, LANES), F32),
        ],
        axis=1,
    )
    out_ref[:, 0:16, :] = wide[...].reshape(SEQ, 16, LANES).astype(BF16)
    out_ref[:, 16:32, :] = jnp.zeros((SEQ, 16, LANES), BF16)
    out_ref[:, 32:40, :] = misc.astype(BF16)


def join_kernel(in_ref, keep_ref, got_ref, out_ref):
    out_ref[:, 0:16, :] = in_ref[:, 0:16, :]
    out_ref[:, 16:32, :] = (keep_ref[...] + got_ref[...]).reshape(SEQ, 16, LANES).astype(BF16)
    out_ref[:, 32:40, :] = in_ref[:, 32:40, :]


def proj_kernel(recv_ref, proj_ref, rest_ref):
    for part in range(PARTS):
        for core in range(2):
            total = recv_ref[place(part, core), 16:32, :].astype(F32)
            for high in range(1, 4):
                total = total + recv_ref[place(part, 2 * high + core), 16:32, :].astype(F32)
            proj_ref[16 * part : 16 * part + 16, LANES * core : LANES * core + LANES] = total.astype(BF16)
    rest_ref[:, 0:16, :] = recv_ref[:, 0:16, :]
    rest_ref[:, 16:24, :] = recv_ref[:, 32:40, :]


def finish_kernel(frame_ref, recv_ref, raw_ref, table_ref, act_ref, pre_ref, grad_ref, rows_ref):
    heads = raw_ref.shape[0]
    for pair in range(PAIRS):
        columns = slice(LANES * pair, LANES * pair + LANES)
        for part in range(PARTS):
            act_ref[16 * part : 16 * part + 16, columns] = recv_ref[place(part, pair), 0:16, :]
    lane = lane_iota(8)
    per_frame = jnp.zeros((8, LANES), F32)
    for pair in range(PAIRS):
        rows = recv_ref[place(0, pair), 16:24, :].astype(F32)
        for part in range(1, PARTS):
            rows = rows + recv_ref[place(part, pair), 16:24, :].astype(F32)
        rows_ref[2 * pair : 2 * pair + 2, :] = rows[0:2]
        rows = rows + pltpu.roll(rows, 64, 1)
        for head in range(2):
            inside = (lane < 2 * BLOCKS) & (lane % 2 == head)
            total = jnp.sum(jnp.where(inside, rows, 0.0), axis=1, keepdims=True)
            per_frame = jnp.where(lane == 2 * pair + head, total, per_frame)
    pre = shifted_steps(frame_ref, raw_ref[...], table_ref[...])
    pre_ref[...] = rows_ref[...] * sigmoid(pre)
    per_head = jnp.concatenate([per_frame, jnp.zeros((LANES - 8, LANES), F32)], axis=0).T
    steps = lax.broadcasted_iota(jnp.int32, grad_ref.shape, 1)
    grad = jnp.zeros(grad_ref.shape, F32)
    for frame in range(4):
        grad = grad + jnp.where(steps == frame_ref[frame], per_head[:heads, 2 + frame : 3 + frame], 0.0)
    grad_ref[...] = grad


def total_kernel(own_ref, one_ref, two_ref, three_ref, write_ref, read_ref):
    even = own_ref[...].astype(F32) + two_ref[...].astype(F32)
    odd = one_ref[...].astype(F32) + three_ref[...].astype(F32)
    total = (even + odd).astype(BF16)
    write_ref[...] = total[:, :LANES]
    read_ref[...] = total[:, LANES:]


VMEM = pl.BlockSpec(memory_space=pltpu.VMEM)
SMEM = pl.BlockSpec(memory_space=pltpu.SMEM)


def call(kernel, name, in_specs, out_shape, scratch=(), params=PARAMS):
    shapes = [jax.ShapeDtypeStruct(shape, dtype) for shape, dtype in out_shape]
    return pl.pallas_call(
        kernel,
        out_shape=shapes,
        in_specs=in_specs,
        out_specs=[VMEM] * len(shapes),
        scratch_shapes=list(scratch),
        compiler_params=params,
        name=name,
    )


def shards(
    activations, grad_out, write_proj, read_proj, step_raw, step_table, decay_rate, frame_step, scan_order
):
    raw, table = step_raw.T, step_table.T
    swap_core = [(i, i ^ 1) for i in range(SEQ)]
    hbm = pl.BlockSpec(memory_space=pltpu.HBM)
    sources = (raw, table, write_proj, read_proj, activations, grad_out)
    (send,) = call(
        pack_kernel, "pack", [SMEM, VMEM] + [hbm] * 6, [((SEQ, SLOT_IN, LANES), BF16)],
        [pltpu.VMEM(a.shape, a.dtype) for a in sources] + [pltpu.SemaphoreType.DMA((6,))],
        pltpu.CompilerParams(vmem_limit_bytes=62 * 1024 * 1024),
    )(frame_step, scan_order.reshape(1, TOK), *sources)
    recv = lax.all_to_all(send, "seq", 0, 0, tiled=True)
    swap = lax.ppermute(recv, "seq", swap_core)
    wide = pltpu.VMEM((LOCAL, LANES), F32)
    data, mine, weight = call(
        unpack_kernel, "unpack", [SMEM, VMEM],
        [((2 * LOCAL + 4 * TOK, LANES), BF16), ((LOCAL, LANES), BF16), ((4 * LOCAL + 16, LANES), BF16)],
        [wide] * 3 + [pltpu.VMEM((SEQ * 8, LANES), F32)],
    )(decay_rate, recv)
    data, states = call(
        states_kernel, "states", [VMEM] * 4,
        [((4 * LOCAL + 4 * TOK, LANES), BF16), ((PARTS, SLOT_STATE, LANES), BF16)], [wide],
    )(mine, swap, weight, data)
    states = lax.all_to_all(states, "seq", 0, 0, tiled=True, axis_index_groups=STATE_GROUPS)
    sums, grad, data = call(
        inner_kernel, "inner", [SMEM, VMEM],
        [
            ((6 * LOCAL + 8, LANES), F32),
            ((2 * LOCAL + 3 * TOK, LANES), F32),
            ((5 * LOCAL, LANES), BF16),
        ],
    )(decay_rate, data)
    keep, give, pairs = call(
        outer_kernel, "outer", [VMEM] * 2,
        [((LOCAL, LANES), F32)] * 2 + [((8 * LOCAL + 32, LANES), BF16)],
        [pltpu.VMEM((BLOCKS, LANES, LANES), F32)] + [wide] * 2,
    )(states, sums)
    got = lax.ppermute(give, "seq", swap_core)
    (out,) = call(
        grads_kernel, "grads", [SMEM] + [VMEM] * 3, [((SEQ, SLOT_OUT, LANES), BF16)], [wide]
    )(decay_rate, data, pairs, grad)
    (out,) = call(join_kernel, "join", [VMEM] * 3, [((SEQ, SLOT_OUT, LANES), BF16)])(out, keep, got)
    back = lax.all_to_all(out, "seq", 0, 0, tiled=True)
    proj, rest = call(
        proj_kernel, "proj", [VMEM], [((TOK, 2 * LANES), BF16), ((SEQ, 24, LANES), BF16)]
    )(back)
    ring = [lax.ppermute(proj, "head", [(i, (i + k) % 4) for i in range(4)]) for k in (1, 2, 3)]
    act, grad_pre, grad_table = call(
        finish_kernel, "finish", [SMEM] + [VMEM] * 3,
        [(activations.shape, BF16), (raw.shape, F32), (table.shape, F32)],
        [pltpu.VMEM((2 * PAIRS, LANES), F32)],
    )(frame_step, rest, raw, table)
    grad_write, grad_read = call(
        total_kernel, "total", [VMEM] * 4, [(write_proj.shape, BF16), (read_proj.shape, BF16)]
    )(proj, *ring)
    return (act, grad_write, grad_read, grad_pre.T, grad_table.T)


def solution(mesh):
    in_specs = (
        P("seq", "head"),
        P("seq", "head"),
        P("seq", None),
        P("seq", None),
        P("seq", "head"),
        P(None, "head"),
        P("head"),
        P(),
        P("seq"),
    )
    out_specs = (
        P("seq", "head"),
        P("seq", None),
        P("seq", None),
        P("seq", "head"),
        P(None, "head"),
    )
    return jax.shard_map(shards, mesh=mesh, in_specs=in_specs, out_specs=out_specs, check_vma=False)
```

time: 115 us -> 103 us (0.90)
  local copies, waits for them, and re-layouts: 17.1 us -> 4.44 us
  waiting for transfers between devices: 7.48 us -> 3.93 us
  Pallas kernels: 14.5 us -> 17.8 us
    unnamed x48 -> x20, local copies, waits for them, and re-layouts: 17.1 us -> 4.44 us
    pallas_call x4 -> x7, Pallas kernels: 11.9 us -> 15.5 us  [the longest x1 3.98 us: shards(): call(grads_kernel, 'grads', [SMEM] + [VMEM] * 3, [((SEQ, SLOT_OUT, LANES)...]
    ppermute x1, waiting for transfers between devices: 2.14 us -> 0.19 us  [shards(): swap = lax.ppermute(recv, 'seq', swap_core)]
    ppermute x1, waiting for transfers between devices: 1.54 us -> 0.01 us  [shards(): got = lax.ppermute(give, 'seq', swap_core)]
  transfers between devices with their start and end apart: 6 -> 6, of which waited for: 4 -> 3; matrix products, arithmetic and copies ran while one was open for 1% -> 0% of each run, Pallas kernels for 2% -> 11%
where the time goes in v2:
time: 103 us; the launch traced here: 102 us
  blocking collectives  65.9 us (64%)
  Pallas kernels  17.8 us (17%)
  starting transfers between devices  9.42 us (9%)
  local copies, waits for them, and re-layouts  4.44 us (4%)
  waiting for transfers between devices  3.93 us (4%)
    all_to_all x1, blocking collectives, shards(): recv = lax.all_to_all(send, 'seq', 0, 0, tiled=True)  38.9 us
    all_to_all x1, blocking collectives, shards(): back = lax.all_to_all(out, 'seq', 0, 0, tiled=True)  27 us
    unnamed x20, local copies, waits for them, and re-layouts  4.44 us
    all_to_all x1, starting transfers between devices, shards(): lax.all_to_all(states, 'seq', 0, 0, tiled=True, axis_index_groups=STATE_G...  4.14 us
    pallas_call x1, Pallas kernels, shards(): call(grads_kernel, 'grads', [SMEM] + [VMEM] * 3, [((SEQ, SLOT_OUT, LANES)...  3.98 us
    pallas_call x1, Pallas kernels, shards(): call(inner_kernel, 'inner', [SMEM, VMEM], [((6 * LOCAL + 8, LANES), F32),...  3.81 us
    ppermute x3, waiting for transfers between devices, shards(): lax.ppermute(proj, 'head', [(i, (i + k) % 4) for i in range(4)])  3.72 us
    ppermute x3, starting transfers between devices, shards(): lax.ppermute(proj, 'head', [(i, (i + k) % 4) for i in range(4)])  3.68 us
  transfers between devices with their start and end apart: 6, of which 3 were waited for; matrix products, arithmetic and copies ran while one was open for 0% of the time, Pallas kernels for 11%

profile of v2, /device:TPU:1, one launch (start us, length us, event | category | flops | bytes accessed | tf_op | source)
XLA Modules:
  0.0 102.2 jit_solution(4913676056847399147)
XLA Ops:
  0.6 2.9 %pack.1 = bf16[64,56,128]{2,1,0:T(8,128)(2,1)} custom-call(s32[4]{0:T(128)} %frame_ref.3, s32[1,128]{1,0:T(1,128)} %bitcast.9, f32[16,128]{1,0:T(8,128)} %bitcast.7, f32[16,1000]{1,0:T(8,128)} %bitcast.5, bf16[128,128]{1,0:T(8,128)(2,1)} %refs_2_.1, bf16[128,128]{1,0:T(8,128)(2,1)} %refs_3_.1, bf16[128,1024]{1,0:T(8,128)(2,1)} %refs_4_.1, ...), custom_call_target="tpu_custom_call" | custom-call | tf_op jit(solution)/shard_map/pack/pallas_call | solution.py:556
  3.6 0.0 copy-start.8
  3.6 38.9 %all_to_all.15.recv_ref = bf16[64,56,128]{2,1,0:T(8,128)(2,1)S(1)} all-to-all(bf16[64,56,128]{2,1,0:T(8,128)(2,1)} %pack.1), channel_id=1, replica_groups=mesh['seq'=64,'head'=4] {'seq'}, dimensions={0} | all-to-all | bytes 1835008 | tf_op jit(solution)/shard_map/all_to_all | solution.py:561
  42.5 0.3 collective-permute-start
  42.8 0.0 copy-done.8
  42.8 1.9 %unpack.1 = (bf16[2560,128]{1,0:T(8,128)(2,1)S(1)}, bf16[1024,128]{1,0:T(8,128)(2,1)S(1)}, bf16[4112,128]{1,0:T(8,128)(2,1)S(1)}) custom-call(f32[16]{0:T(128)S(1)} %copy-done.8, bf16[64,56,128]{2,1,0:T(8,128)(2,1)S(1)} %all_to_all.15.recv_ref), custom_call_target="tpu_custom_call" | custom-call | tf_op jit(solution)/shard_map/unpack/pallas_call | solution.py:564
  44.8 0.2 collective-permute-done.swap_ref
  45.0 1.6 %states.1 = (bf16[4608,128]{1,0:T(8,128)(2,1)S(1)}, bf16[8,136,128]{2,1,0:T(8,128)(2,1)}) custom-call(bf16[1024,128]{1,0:T(8,128)(2,1)S(1)} %get-tuple-element.23.mine_ref, bf16[64,56,128]{2,1,0:T(8,128)(2,1)S(1)} %collective-permute-done.swap_ref, bf16[4112,128]{1,0:T(8,128)(2,1)S(1)} %get-tuple-element.24.weight_ref, ...), custom_call_target="tpu_custom_call" | custom-call | tf_op jit(solution)/shard_map/states/pallas_call | solution.py:569
  46.5 0.0 copy-start.4
  46.5 1.0 %copy-done.4 = bf16[4608,128]{1,0:T(8,128)(2,1)} copy-done((bf16[4608,128]{1,0:T(8,128)(2,1)}, bf16[4608,128]{1,0:T(8,128)(2,1)S(1)}, u32[]{:S(2)}) %copy-start.4) | copy-done | bytes 1179672
  47.6 4.1 %all-to-all-start.1 = ((bf16[8,136,128]{2,1,0:T(8,128)(2,1)}), bf16[8,136,128]{2,1,0:T(8,128)(2,1)S(1)}, u32[]{:S(2)}, u32[]{:S(2)}) async-start(bf16[8,136,128]{2,1,0:T(8,128)(2,1)} %get-tuple-element.28), calls=%async_computation.1 | async-start | bytes 557056 | tf_op jit(solution)/shard_map/all_to_all | solution.py:573
  51.7 0.0 copy-start.5
  51.7 1.3 %copy-done.5 = bf16[4608,128]{1,0:T(8,128)(2,1)S(1)} copy-done((bf16[4608,128]{1,0:T(8,128)(2,1)S(1)}, bf16[4608,128]{1,0:T(8,128)(2,1)}, u32[]{:S(2)}) %copy-start.5) | copy-done | bytes 1179672
  53.0 3.8 %inner.1 = (f32[6152,128]{1,0:T(8,128)S(1)}, f32[2432,128]{1,0:T(8,128)S(1)}, bf16[5120,128]{1,0:T(8,128)(2,1)S(1)}) custom-call(f32[16]{0:T(128)S(1)} %copy-done.8, bf16[4608,128]{1,0:T(8,128)(2,1)S(1)} %copy-done.5), custom_call_target="tpu_custom_call" | custom-call | tf_op jit(solution)/shard_map/inner/pallas_call | solution.py:574
  56.8 0.0 copy-start
  56.8 1.1 %copy-done = bf16[5120,128]{1,0:T(8,128)(2,1)} copy-done((bf16[5120,128]{1,0:T(8,128)(2,1)}, bf16[5120,128]{1,0:T(8,128)(2,1)S(1)}, u32[]{:S(2)}) %copy-start) | copy-done | bytes 1310744
  57.9 0.0 copy-start.2
  57.9 1.0 %copy-done.2 = f32[2432,128]{1,0:T(8,128)} copy-done((f32[2432,128]{1,0:T(8,128)}, f32[2432,128]{1,0:T(8,128)S(1)}, u32[]{:S(2)}) %copy-start.2) | copy-done | bytes 1245208
  58.9 0.0 all-to-all-done.1.recv_ref
  58.9 0.0 copy-start.1
  58.9 0.0 copy-start.3
  58.9 1.2 %outer.1 = (f32[1024,128]{1,0:T(8,128)S(1)}, f32[1024,128]{1,0:T(8,128)S(1)}, bf16[8224,128]{1,0:T(8,128)(2,1)S(1)}) custom-call(bf16[8,136,128]{2,1,0:T(8,128)(2,1)S(1)} %all-to-all-done.1.recv_ref, f32[6152,128]{1,0:T(8,128)S(1)} %get-tuple-element.29.sums_ref), custom_call_target="tpu_custom_call" | custom-call | tf_op jit(solution)/shard_map/outer/pallas_call | solution.py:582
  60.1 1.3 %collective-permute-start.1 = (f32[1024,128]{1,0:T(8,128)S(1)}, f32[1024,128]{1,0:T(8,128)S(1)}, u32[]{:S(2)}, u32[]{:S(2)}) collective-permute-start(f32[1024,128]{1,0:T(8,128)S(1)} %get-tuple-element.33), channel_id=1, source_target_pairs={{0,4},{4,0},{8,12},{12,8},{16,20},{20,16},{24,28},{28,24},{32,36},... | collective-permute-start | bytes 1572872 | tf_op jit(solution)/shard_map/ppermute | solution.py:587
  61.4 0.0 copy-done.1
  61.4 0.0 copy-done.3
  61.4 4.0 %grads.1.in_ref = bf16[64,40,128]{2,1,0:T(8,128)(2,1)S(1)} custom-call(f32[16]{0:T(128)S(1)} %copy-done.8, bf16[5120,128]{1,0:T(8,128)(2,1)S(1)} %copy-done.1, bf16[8224,128]{1,0:T(8,128)(2,1)S(1)} %get-tuple-element.30.all_ref, f32[2432,128]{1,0:T(8,128)S(1)} %copy-done.3), custom_call_target="tpu_custom_call" | custom-call | tf_op jit(solution)/shard_map/grads/pallas_call | solution.py:588
  65.4 0.0 collective-permute-done.1.got_ref
  65.4 0.1 join.1
  65.5 0.0 copy-start.6
  65.5 0.0 copy-start.7
  65.5 0.0 copy-start.9
  65.5 27.0 %all_to_all.16.recv_ref = bf16[64,40,128]{2,1,0:T(8,128)(2,1)S(1)} all-to-all(bf16[64,40,128]{2,1,0:T(8,128)(2,1)S(1)} %join.1), channel_id=1, replica_groups=mesh['seq'=64,'head'=4] {'seq'}, dimensions={0} | all-to-all | bytes 1310720 | tf_op jit(solution)/shard_map/all_to_all | solution.py:592
  92.5 0.1 proj.1
  92.6 2.6 %collective-permute-start.4 = (bf16[128,256]{1,0:T(8,128)(2,1)S(1)}, bf16[128,256]{1,0:T(8,128)(2,1)S(1)}, u32[]{:S(2)}, u32[]{:S(2)}) collective-permute-start(bf16[128,256]{1,0:T(8,128)(2,1)S(1)} %get-tuple-element.36.own_ref), channel_id=1, source_target_pairs={{0,3},{1,0},{2,1},{3,2},{4,7},{5,4},{6,5},{7,6},{8,11},{9,8},{10,9... | collective-permute-start | bytes 196616 | tf_op jit(solution)/shard_map/ppermute | solution.py:596
  95.1 0.5 collective-permute-start.3
  95.7 0.6 collective-permute-start.2
  96.3 0.0 copy-done.6
  96.3 0.0 copy-done.7
  96.3 0.0 copy-done.9
  96.3 1.5 %finish.1 = (bf16[128,1024]{1,0:T(8,128)(2,1)}, f32[16,128]{1,0:T(8,128)}, f32[16,1000]{1,0:T(8,128)}) custom-call(s32[4]{0:T(128)S(1)} %copy-done.9, bf16[64,24,128]{2,1,0:T(8,128)(2,1)S(1)} %get-tuple-element.34.recv_ref, f32[16,128]{1,0:T(8,128)S(1)} %bitcast.8, f32[16,1000]{1,0:T(8,128)S(1)} %bitcast.6), custom_call_target="tpu_custom_call" | custom-call | tf_op jit(solution)/shard_map/finish/pallas_call | solution.py:597
  97.8 0.0 collective-permute-done.4.three_ref
  97.8 2.0 %collective-permute-done.3.two_ref = bf16[128,256]{1,0:T(8,128)(2,1)S(1)} collective-permute-done((bf16[128,256]{1,0:T(8,128)(2,1)S(1)}, bf16[128,256]{1,0:T(8,128)(2,1)S(1)}, u32[]{:S(2)}, u32[]{:S(2)}) %collective-permute-start.3) | collective-permute-done | bytes 65568 | tf_op jit(solution)/shard_map/ppermute | solution.py:596
  99.8 1.7 %collective-permute-done.2.one_ref = bf16[128,256]{1,0:T(8,128)(2,1)S(1)} collective-permute-done((bf16[128,256]{1,0:T(8,128)(2,1)S(1)}, bf16[128,256]{1,0:T(8,128)(2,1)S(1)}, u32[]{:S(2)}, u32[]{:S(2)}) %collective-permute-start.2) | collective-permute-done | bytes 65568 | tf_op jit(solution)/shard_map/ppermute | solution.py:596
  101.5 0.7 total.1
Async XLA Ops:
  3.6 39.3 %copy-start.8 = (f32[16]{0:T(128)S(1)}, f32[16]{0:T(128)}, u32[]{:S(2)}) copy-start(f32[16]{0:T(128)} %decay_ref.5) | copy-start | bytes 196
  42.5 2.5 %collective-permute-start = (bf16[64,56,128]{2,1,0:T(8,128)(2,1)S(1)}, bf16[64,56,128]{2,1,0:T(8,128)(2,1)S(1)}, u32[]{:S(2)}, u32[]{:S(2)}) collective-permute-start(bf16[64,56,128]{2,1,0:T(8,128)(2,1)S(1)} %all_to_all.15.recv_ref), channel_id=1, source_target_pairs={{0,4},{4,0},{8,12},{12,8},{16,20},{20,16},{24,28},{28,24},{32,36},... | collective-permute-start | bytes 2752520 | tf_op jit(solution)/shard_map/ppermute | solution.py:562
  46.5 1.0 %copy-start.4 = (bf16[4608,128]{1,0:T(8,128)(2,1)}, bf16[4608,128]{1,0:T(8,128)(2,1)S(1)}, u32[]{:S(2)}) copy-start(bf16[4608,128]{1,0:T(8,128)(2,1)S(1)} %get-tuple-element.26.all_ref) | copy-start | bytes 3538948
  47.6 11.4 %all-to-all-start.1 = ((bf16[8,136,128]{2,1,0:T(8,128)(2,1)}), bf16[8,136,128]{2,1,0:T(8,128)(2,1)S(1)}, u32[]{:S(2)}, u32[]{:S(2)}) async-start(bf16[8,136,128]{2,1,0:T(8,128)(2,1)} %get-tuple-element.28), calls=%async_computation.1 | async-start | bytes 557056 | tf_op jit(solution)/shard_map/all_to_all | solution.py:573
  51.7 1.3 %copy-start.5 = (bf16[4608,128]{1,0:T(8,128)(2,1)S(1)}, bf16[4608,128]{1,0:T(8,128)(2,1)}, u32[]{:S(2)}) copy-start(bf16[4608,128]{1,0:T(8,128)(2,1)} %copy-done.4) | copy-start | bytes 3538948
  56.8 1.1 %copy-start = (bf16[5120,128]{1,0:T(8,128)(2,1)}, bf16[5120,128]{1,0:T(8,128)(2,1)S(1)}, u32[]{:S(2)}) copy-start(bf16[5120,128]{1,0:T(8,128)(2,1)S(1)} %get-tuple-element.27.data_ref) | copy-start | bytes 3932164
  57.9 1.0 %copy-start.2 = (f32[2432,128]{1,0:T(8,128)}, f32[2432,128]{1,0:T(8,128)S(1)}, u32[]{:S(2)}) copy-start(f32[2432,128]{1,0:T(8,128)S(1)} %get-tuple-element.31.grad_ref) | copy-start | bytes 3735556
  58.9 2.5 %copy-start.1 = (bf16[5120,128]{1,0:T(8,128)(2,1)S(1)}, bf16[5120,128]{1,0:T(8,128)(2,1)}, u32[]{:S(2)}) copy-start(bf16[5120,128]{1,0:T(8,128)(2,1)} %copy-done) | copy-start | bytes 3932164
  58.9 2.5 %copy-start.3 = (f32[2432,128]{1,0:T(8,128)S(1)}, f32[2432,128]{1,0:T(8,128)}, u32[]{:S(2)}) copy-start(f32[2432,128]{1,0:T(8,128)} %copy-done.2) | copy-start | bytes 3735556
  60.1 5.3 %collective-permute-start.1 = (f32[1024,128]{1,0:T(8,128)S(1)}, f32[1024,128]{1,0:T(8,128)S(1)}, u32[]{:S(2)}, u32[]{:S(2)}) collective-permute-start(f32[1024,128]{1,0:T(8,128)S(1)} %get-tuple-element.33), channel_id=1, source_target_pairs={{0,4},{4,0},{8,12},{12,8},{16,20},{20,16},{24,28},{28,24},{32,36},... | collective-permute-start | bytes 1572872 | tf_op jit(solution)/shard_map/ppermute | solution.py:587
  65.5 30.7 %copy-start.6 = (f32[1000,16]{0,1:T(8,128)S(1)}, f32[1000,16]{0,1:T(8,128)}, u32[]{:S(2)}) copy-start(f32[1000,16]{0,1:T(8,128)} %param.14) | copy-start | bytes 192004
  65.5 30.7 %copy-start.7 = (f32[128,16]{0,1:T(8,128)S(1)}, f32[128,16]{0,1:T(8,128)}, u32[]{:S(2)}) copy-start(f32[128,16]{0,1:T(8,128)} %param.13) | copy-start | bytes 24580
  65.5 30.7 %copy-start.9 = (s32[4]{0:T(128)S(1)}, s32[4]{0:T(128)}, u32[]{:S(2)}) copy-start(s32[4]{0:T(128)} %frame_ref.3) | copy-start | bytes 52
  92.6 5.2 %collective-permute-start.4 = (bf16[128,256]{1,0:T(8,128)(2,1)S(1)}, bf16[128,256]{1,0:T(8,128)(2,1)S(1)}, u32[]{:S(2)}, u32[]{:S(2)}) collective-permute-start(bf16[128,256]{1,0:T(8,128)(2,1)S(1)} %get-tuple-element.36.own_ref), channel_id=1, source_target_pairs={{0,3},{1,0},{2,1},{3,2},{4,7},{5,4},{6,5},{7,6},{8,11},{9,8},{10,9... | collective-permute-start | bytes 196616 | tf_op jit(solution)/shard_map/ppermute | solution.py:596
  95.1 4.7 %collective-permute-start.3 = (bf16[128,256]{1,0:T(8,128)(2,1)S(1)}, bf16[128,256]{1,0:T(8,128)(2,1)S(1)}, u32[]{:S(2)}, u32[]{:S(2)}) collective-permute-start(bf16[128,256]{1,0:T(8,128)(2,1)S(1)} %get-tuple-element.36.own_ref), channel_id=1, source_target_pairs={{0,2},{1,3},{2,0},{3,1},{4,6},{5,7},{6,4},{7,5},{8,10},{9,11},{10,... | collective-permute-start | bytes 196616 | tf_op jit(solution)/shard_map/ppermute | solution.py:596
  95.7 5.9 %collective-permute-start.2 = (bf16[128,256]{1,0:T(8,128)(2,1)S(1)}, bf16[128,256]{1,0:T(8,128)(2,1)S(1)}, u32[]{:S(2)}, u32[]{:S(2)}) collective-permute-start(bf16[128,256]{1,0:T(8,128)(2,1)S(1)} %get-tuple-element.36.own_ref), channel_id=1, source_target_pairs={{0,1},{1,2},{2,3},{3,0},{4,5},{5,6},{6,7},{7,4},{8,9},{9,10},{10,1... | collective-permute-start | bytes 196616 | tf_op jit(solution)/shard_map/ppermute | solution.py:596

commit v3 on v2

--- a/solution.py
+++ b/solution.py
@@ -200,46 +200,47 @@
     middle = (whole - top).astype(BF16).astype(F32)
     bottom = whole - top - middle
     tail = jnp.concatenate([top, middle, bottom, jnp.zeros((13, LANES), F32)], axis=0).astype(BF16)
-    weight_ref[4 * LOCAL : 4 * LOCAL + 16, :] = tail
+    weight_ref[2 * LOCAL : 2 * LOCAL + 16, :] = tail
     weights = steps * jnp.exp(jnp.minimum(onward - logs, 0.0))
     starts = jnp.exp(jnp.minimum(logs + until, 0.0))
     for block in range(BLOCKS):
         rows = block_rows(block)
         later_rows = slice(LOCAL + block * TOK, LOCAL + block * TOK + TOK)
-        first = block * 2 * TOK
-        weight_ref[first : first + 2 * TOK, :] = stack(
+        weight_ref[rows, :] = (
             data_ref[rows, :].astype(F32) * block_lanes(weights, block, TOK)
-        )
-        first = 2 * LOCAL + block * 2 * TOK
-        weight_ref[first : first + 2 * TOK, :] = stack(
+        ).astype(BF16)
+        weight_ref[later_rows, :] = (
             data_ref[later_rows, :].astype(F32) * block_lanes(starts, block, TOK)
-        )
-
-
-def states_kernel(mine_ref, swap_ref, weight_ref, data_ref, all_ref, send_ref, wide):
+        ).astype(BF16)
+
+
+def gather_kernel(mine_ref, swap_ref, data_ref, all_ref, wide):
     part, pair, core = my_place()
     all_ref[0 : 2 * LOCAL, :] = data_ref[0 : 2 * LOCAL, :]
     all_ref[4 * LOCAL : 4 * LOCAL + 4 * TOK, :] = data_ref[2 * LOCAL : 2 * LOCAL + 4 * TOK, :]
-    spread(swap_ref[:, 32:48, :].astype(F32), wide, all_ref, 3 * LOCAL)
 
     @pl.when(core == 0)
     def _():
         all_ref[2 * LOCAL : 3 * LOCAL, :] = mine_ref[...]
+        spread(swap_ref[:, 32:48, :].astype(F32), wide, all_ref, 3 * LOCAL)
 
     @pl.when(core == 1)
     def _():
-        all_ref[2 * LOCAL : 3 * LOCAL, :] = all_ref[3 * LOCAL : 4 * LOCAL, :]
         all_ref[3 * LOCAL : 4 * LOCAL, :] = mine_ref[...]
-
+        spread(swap_ref[:, 32:48, :].astype(F32), wide, all_ref, 2 * LOCAL)
+
+
+def states_kernel(all_ref, weight_ref, send_ref):
+    part, pair, core = my_place()
     state = jnp.zeros((LANES, LANES), F32)
     adjoint = jnp.zeros((LANES, LANES), F32)
-    for block in range(BLOCKS):
-        write = all_ref[2 * LOCAL + block * TOK : 2 * LOCAL + block * TOK + TOK, :]
-        read = all_ref[3 * LOCAL + block * TOK : 3 * LOCAL + block * TOK + TOK, :]
-        first = block * 2 * TOK
-        state = state + nn(twice(turned(write)), weight_ref[first : first + 2 * TOK, :])
-        first = 2 * LOCAL + block * 2 * TOK
-        adjoint = adjoint + nn(twice(turned(read)), weight_ref[first : first + 2 * TOK, :])
+    for block in range(0, BLOCKS, 2):
+        rows = slice(block * TOK, block * TOK + 2 * TOK)
+        later_rows = slice(LOCAL + block * TOK, LOCAL + block * TOK + 2 * TOK)
+        write = all_ref[2 * LOCAL + block * TOK : 2 * LOCAL + block * TOK + 2 * TOK, :]
+        read = all_ref[3 * LOCAL + block * TOK : 3 * LOCAL + block * TOK + 2 * TOK, :]
+        state = state + nn(turned(write), weight_ref[rows, :])
+        adjoint = adjoint + nn(turned(read), weight_ref[later_rows, :])
     state = state.astype(BF16)
     adjoint = adjoint.astype(BF16)
     for slot in range(PARTS):
@@ -253,40 +254,32 @@
         def _():
             send_ref[slot, 0:128, :] = adjoint
 
-        send_ref[slot, 128:136, :] = weight_ref[4 * LOCAL : 4 * LOCAL + 16, :][:8]
-
-
-def inner_kernel(decay_ref, all_ref, sums_ref, grad_ref, data_ref):
+        send_ref[slot, 128:136, :] = weight_ref[2 * LOCAL : 2 * LOCAL + 16, :][:8]
+
+
+def inner_kernel(decay_ref, all_ref, sums_ref, grad_ref):
     part, pair, core = my_place()
     base = 4 * LOCAL
     steps_bf = all_ref[base : base + TOK, :]
     steps = steps_bf.astype(F32)
     pos_cols = all_ref[base + 3 * TOK : base + 4 * TOK, :].astype(F32)
     pos_rows = pos_cols.T[:8]
-    grad_ref[2 * LOCAL : 2 * LOCAL + TOK, :] = steps
-    grad_ref[2 * LOCAL + TOK : 2 * LOCAL + 2 * TOK, :] = (
-        all_ref[base + TOK : base + 2 * TOK, :].astype(F32) + all_ref[base + 2 * TOK : base + 3 * TOK, :].astype(F32)
-    )
-    grad_ref[2 * LOCAL + 2 * TOK : 2 * LOCAL + 3 * TOK, :] = jnp.zeros((TOK, LANES), F32)
+    grad_ref[LOCAL + 2 * TOK : LOCAL + 3 * TOK, :] = jnp.zeros((TOK, LANES), F32)
     lane = lane_iota(TOK)
     sums = jnp.zeros((TOK, LANES), F32)
-    masks = 3 * LOCAL
-    for block in range(BLOCKS):
-        pos_col = pos_cols[:, block : block + 1]
-        pos_row = pos_rows[block : block + 1, :]
-        behind = (pos_col >= pos_row).astype(F32).astype(BF16)
-        first = masks + block * 2 * TOK
-        data_ref[first : first + TOK, :] = (pos_row >= pos_col).astype(F32).astype(BF16)
-        data_ref[first + TOK : first + 2 * TOK, :] = behind
-        sums = jnp.where(lane // 2 == block, nn(behind, steps_bf), sums)
+    masks = []
+    for block in range(BLOCKS):
+        behind = pos_cols[:, block : block + 1] >= pos_rows[block : block + 1, :]
+        masks.append(behind.astype(F32).astype(BF16))
+        sums = jnp.where(lane // 2 == block, nn(masks[block], steps_bf), sums)
     slopes = slope_lanes(decay_ref, pair, TOK)
     logs = sums * slopes
     log_rows = logs.T
     totals = jnp.sum(steps, axis=0, keepdims=True) * slopes[:1]
     starts = jnp.exp(logs)
     ends = steps * jnp.exp(totals - logs)
-    data_ref[0:LOCAL, :] = all_ref[0:LOCAL, :]
-    data_ref[LOCAL : 3 * LOCAL, :] = all_ref[2 * LOCAL : 4 * LOCAL, :]
+    grad_ref[LOCAL : LOCAL + TOK, :] = ends
+    grad_ref[LOCAL + TOK : LOCAL + 2 * TOK, :] = starts
     for block in range(BLOCKS):
         rows = block_rows(block)
 
@@ -297,18 +290,9 @@
             return slice(number * LOCAL + block * TOK, number * LOCAL + block * TOK + TOK)
 
         x, dy, write, read = piece(0), piece(1), piece(2), piece(3)
-        sums_ref[6 * LOCAL + block : 6 * LOCAL + block + 1, :] = block_lanes(totals, block, 1)
-        end = block_lanes(ends, block, TOK)
-        grad_ref[LOCAL + block * TOK : LOCAL + block * TOK + TOK, :] = end
-        xe = x.astype(F32) * end
-        ds = dy.astype(F32) * block_lanes(starts, block, TOK)
-        first = block * 2 * TOK
-        sums_ref[sums_rows(4), :] = ds
-        sums_ref[sums_rows(5), :] = xe
-        sums_ref[sums_rows(2), :] = nn(twice(turned(write)), stack(xe))
-        sums_ref[sums_rows(3), :] = nn(twice(turned(read)), stack(ds))
+        sums_ref[2 * LOCAL + block : 2 * LOCAL + block + 1, :] = block_lanes(totals, block, 1)
         ahead = pos_rows[block : block + 1, :] >= pos_cols[:, block : block + 1]
-        behind = data_ref[masks + first + TOK : masks + first + 2 * TOK, :]
+        behind = masks[block]
         cross = nt(write, read)
         zero = jnp.zeros_like(dy)
         x_heads = (jnp.where(lane < 64, x, zero), jnp.where(lane < 64, zero, x))
@@ -325,7 +309,7 @@
             seen.append(twice_split(mixed[head] * cross))
         crossed = nn(jnp.concatenate(seen, axis=0), jnp.concatenate([behind, behind], axis=0))
         for head in range(2):
-            j = 2 * LOCAL + 2 * TOK + 2 * block + head
+            j = LOCAL + 2 * TOK + 2 * block + head
             own = jnp.where(ahead, crossed[head * TOK : head * TOK + TOK], 0.0)
             grad_ref[j : j + 1, :] = jnp.sum(own, axis=0, keepdims=True)
         high, low = split(jnp.concatenate(carry, axis=1))
@@ -335,7 +319,7 @@
         sums_ref[sums_rows(1), :] = nn(twice_split(both.T), jnp.concatenate([write, write], axis=0))
 
 
-def outer_kernel(recv_ref, sums_ref, keep_ref, give_ref, all_ref, adj, wide_w, wide_r):
+def outer_kernel(recv_ref, sums_ref, data_ref, grad_ref, keep_ref, give_ref, all_ref, adj, wide_w, wide_r):
     part, pair, core = my_place()
 
     def arrive(slot, state):
@@ -346,14 +330,27 @@
     zero = jnp.zeros((LANES, LANES), F32)
     state = lax.fori_loop(0, part, arrive, zero)
     adjoint = lax.fori_loop(0, PARTS - 1 - part, lambda k, a: arrive(PARTS - 1 - k, a), zero)
-    keeps = jnp.exp(sums_ref[6 * LOCAL : 6 * LOCAL + 8, :])
+    keeps = jnp.exp(sums_ref[2 * LOCAL : 2 * LOCAL + 8, :])
 
     def sums_rows(number, block):
         return slice(number * LOCAL + block * TOK, number * LOCAL + block * TOK + TOK)
 
+    ends = grad_ref[LOCAL : LOCAL + TOK, :]
+    starts = grad_ref[LOCAL + TOK : LOCAL + 2 * TOK, :]
+
+    def data_rows(number, block):
+        return slice(number * LOCAL + block * TOK, number * LOCAL + block * TOK + TOK)
+
+    gains, ds, xe = [], [], []
+    for block in range(BLOCKS):
+        xe.append(split(data_ref[data_rows(0, block), :].astype(F32) * block_lanes(ends, block, TOK)))
+        ds.append(split(data_ref[data_rows(1, block), :].astype(F32) * block_lanes(starts, block, TOK)))
+        write = twice(turned(data_ref[data_rows(2, block), :]))
+        read = twice(turned(data_ref[data_rows(3, block), :]))
+        gains.append((nn(write, jnp.concatenate(xe[block], axis=0)), nn(read, jnp.concatenate(ds[block], axis=0))))
     for block in reversed(range(BLOCKS)):
         adj[block] = adjoint
-        adjoint = adjoint * keeps[block : block + 1] + sums_ref[sums_rows(3, block), :]
+        adjoint = adjoint * keeps[block : block + 1] + gains[block][1]
     overlaps = []
     for block in range(BLOCKS):
         adjoint = adj[block]
@@ -366,8 +363,8 @@
         all_ref[6 * LOCAL + first + TOK : 6 * LOCAL + first + 2 * TOK, :] = adj_low
         keep = keeps[block : block + 1]
         overlaps.append(jnp.sum(adjoint * state, axis=0, keepdims=True) * keep)
-        ds_high, ds_low = split(sums_ref[sums_rows(4, block), :])
-        xe_high, xe_low = split(sums_ref[sums_rows(5, block), :])
+        ds_high, ds_low = ds[block]
+        xe_high, xe_low = xe[block]
         all_ref[first : first + TOK, :] = ds_high
         all_ref[first + TOK : first + 2 * TOK, :] = ds_low
         all_ref[2 * LOCAL + first : 2 * LOCAL + first + TOK, :] = xe_high
@@ -382,7 +379,7 @@
             out_rows = pl.ds(2 * block + half, 64, stride=16)
             wide_w[out_rows, :] = gw[64 * half : 64 * half + 64]
             wide_r[out_rows, :] = gr[64 * half : 64 * half + 64]
-        state = state * keep + sums_ref[sums_rows(2, block), :]
+        state = state * keep + gains[block][0]
     overlaps = jnp.concatenate(overlaps, axis=0)
     top = overlaps.astype(BF16).astype(F32)
     middle = (overlaps - top).astype(BF16).astype(F32)
@@ -402,12 +399,15 @@
         give_ref[...] = wide_w[...]
 
 
-def grads_kernel(decay_ref, data_ref, all_ref, grad_ref, out_ref, wide):
+def grads_kernel(decay_ref, data_ref, all_ref, grad_ref, out_ref, wide, misc):
     part, pair, core = my_place()
     slopes = slope_lanes(decay_ref, pair, TOK)
-    base = 2 * LOCAL
-    steps = grad_ref[base : base + TOK, :]
-    gates = grad_ref[base + TOK : base + 2 * TOK, :]
+    base = 4 * LOCAL
+    steps = data_ref[base : base + TOK, :].astype(F32)
+    gates = data_ref[base + TOK : base + 2 * TOK, :].astype(F32) + data_ref[base + 2 * TOK : base + 3 * TOK, :].astype(F32)
+    pos_cols = data_ref[base + 3 * TOK : base + 4 * TOK, :].astype(F32)
+    pos_rows = pos_cols.T[:8]
+    ends = grad_ref[LOCAL : LOCAL + TOK, :]
     lane = lane_iota(TOK)
     tail = all_ref[8 * LOCAL : 8 * LOCAL + 32, :].astype(F32)
     overlaps = tail[0:8] + tail[8:16] + tail[16:24]
@@ -416,10 +416,9 @@
     first = jnp.sum(jnp.where(row_lane < 64, overlaps, 0.0), axis=1, keepdims=True)
     second = jnp.sum(jnp.where(row_lane < 64, 0.0, overlaps), axis=1, keepdims=True)
     kept = jnp.where(row_lane == 2 * row, first, jnp.where(row_lane == 2 * row + 1, second, 0.0))
-    log_grad = grad_ref[base + 2 * TOK : base + 3 * TOK, :].T + jnp.sum(kept, axis=0, keepdims=True)
     sub = lax.broadcasted_iota(jnp.int32, (2 * LANES, LANES), 0) % LANES // 64
     pick_lane = lax.broadcasted_iota(jnp.int32, (2 * LANES, LANES), 1)
-    direct = jnp.zeros((TOK, LANES), F32)
+    per_head = jnp.zeros((3 * TOK, LANES), F32)
     for block in range(BLOCKS):
         rows = block_rows(block)
         lo = block * 2 * TOK
@@ -429,22 +428,32 @@
             return all_ref[start : start + TOK, :].astype(F32) + all_ref[start + TOK : start + 2 * TOK, :].astype(F32)
 
         x = data_ref[rows, :].astype(F32)
-        write = data_ref[LOCAL + block * TOK : LOCAL + block * TOK + TOK, :]
-        read = data_ref[2 * LOCAL + block * TOK : 2 * LOCAL + block * TOK + TOK, :]
+        write = data_ref[2 * LOCAL + block * TOK : 2 * LOCAL + block * TOK + TOK, :]
+        read = data_ref[3 * LOCAL + block * TOK : 3 * LOCAL + block * TOK + TOK, :]
         carried = nn(twice(write), all_ref[6 * LOCAL + lo : 6 * LOCAL + lo + 2 * TOK, :])
         recalled = nn(twice(read), all_ref[4 * LOCAL + lo : 4 * LOCAL + lo + 2 * TOK, :])
-        act = grad_ref[rows, :] + grad_ref[LOCAL + block * TOK : LOCAL + block * TOK + TOK, :] * carried
+        act = grad_ref[rows, :] + block_lanes(ends, block, TOK) * carried
         wide[pl.ds(2 * block, 64, stride=16), :] = act[:64]
         wide[pl.ds(2 * block + 1, 64, stride=16), :] = act[64:]
         products = jnp.concatenate([both(0) * recalled, both(2) * carried, x * act], axis=0)
         pick = (pick_lane == 2 * block + sub).astype(F32).astype(BF16)
-        sums = nn(twice_split(products), pick)
-        direct = direct + sums[2 * TOK :]
-        ahead = data_ref[3 * LOCAL + lo : 3 * LOCAL + lo + TOK, :]
-        behind = data_ref[3 * LOCAL + lo + TOK : 3 * LOCAL + lo + 2 * TOK, :]
-        added = nn(twice(ahead), stack(sums[:TOK])) + nn(twice(behind), stack(sums[TOK : 2 * TOK]))
-        log_grad = log_grad + jnp.where(lane // 2 == block, added, 0.0)
-
+        per_head = per_head + nn(twice_split(products), pick)
+
+    direct = per_head[2 * TOK :]
+    read_high, read_low = split(per_head[:TOK].T[: 2 * BLOCKS])
+    write_part = per_head[TOK : 2 * TOK].T[: 2 * BLOCKS]
+    write_high, write_low = split(write_part)
+    vectors = jnp.concatenate([read_high, read_low, write_high, write_low], axis=0)
+    log_rows = grad_ref[LOCAL + 2 * TOK : LOCAL + 2 * TOK + 2 * BLOCKS, :]
+    log_rows = log_rows + write_part + jnp.sum(write_part, axis=1, keepdims=True)
+    owner = lax.broadcasted_iota(jnp.int32, (2 * BLOCKS, LANES), 0) // 2
+    for block in range(BLOCKS):
+        behind = (pos_cols[:, block : block + 1] >= pos_rows[block : block + 1, :]).astype(F32).astype(BF16)
+        sums = nn(vectors, behind)
+        added = (sums[0:16] + sums[16:32]) - (sums[32:48] + sums[48:64])
+        log_rows = log_rows + jnp.where(owner == block, added, 0.0)
+    log_grad = jnp.concatenate([log_rows, jnp.zeros((TOK - 2 * BLOCKS, LANES), F32)], axis=0).T
+    log_grad = log_grad + jnp.sum(kept, axis=0, keepdims=True)
     grad_step = direct / steps + slopes * (log_grad - direct)
     grad_step = jnp.where(lane < 2 * BLOCKS, grad_step, 0.0).astype(BF16).astype(F32)
     grad_pre = grad_step * gates
@@ -462,18 +471,14 @@
     shift = 16 * part
     row_one = pltpu.roll(jnp.where(even, top, pltpu.roll(bottom, 1, 1)), shift, 1)
     row_two = pltpu.roll(jnp.where(even, pltpu.roll(top, LANES - 1, 1), bottom), shift, 1)
-    misc = jnp.concatenate(
-        [
-            row_one[:, None, :],
-            row_two[:, None, :],
-            jnp.broadcast_to(frames[None, :4, :], (SEQ, 4, LANES)),
-            jnp.zeros((SEQ, 2, LANES), F32),
-        ],
-        axis=1,
-    )
+    misc[...] = jnp.zeros((SEQ * 8, LANES), F32)
+    misc[pl.ds(0, 64, stride=8), :] = row_one
+    misc[pl.ds(1, 64, stride=8), :] = row_two
+    for frame in range(4):
+        misc[pl.ds(2 + frame, 64, stride=8), :] = jnp.broadcast_to(frames[frame : frame + 1], (SEQ, LANES))
     out_ref[:, 0:16, :] = wide[...].reshape(SEQ, 16, LANES).astype(BF16)
     out_ref[:, 16:32, :] = jnp.zeros((SEQ, 16, LANES), BF16)
-    out_ref[:, 32:40, :] = misc.astype(BF16)
+    out_ref[:, 32:40, :] = misc[...].reshape(SEQ, 8, LANES).astype(BF16)
 
 
 def join_kernel(in_ref, keep_ref, got_ref, out_ref):
@@ -561,32 +566,32 @@
     recv = lax.all_to_all(send, "seq", 0, 0, tiled=True)
     swap = lax.ppermute(recv, "seq", swap_core)
     wide = pltpu.VMEM((LOCAL, LANES), F32)
+    bundle = ((4 * LOCAL + 4 * TOK, LANES), BF16)
+    sums = ((LOCAL, LANES), F32)
     data, mine, weight = call(
         unpack_kernel, "unpack", [SMEM, VMEM],
-        [((2 * LOCAL + 4 * TOK, LANES), BF16), ((LOCAL, LANES), BF16), ((4 * LOCAL + 16, LANES), BF16)],
+        [((2 * LOCAL + 4 * TOK, LANES), BF16), ((LOCAL, LANES), BF16), ((2 * LOCAL + 16, LANES), BF16)],
         [wide] * 3 + [pltpu.VMEM((SEQ * 8, LANES), F32)],
     )(decay_rate, recv)
-    data, states = call(
-        states_kernel, "states", [VMEM] * 4,
-        [((4 * LOCAL + 4 * TOK, LANES), BF16), ((PARTS, SLOT_STATE, LANES), BF16)], [wide],
-    )(mine, swap, weight, data)
+    (data,) = call(gather_kernel, "gather", [VMEM] * 3, [bundle], [wide])(mine, swap, data)
+    (states,) = call(states_kernel, "states", [VMEM] * 2, [((PARTS, SLOT_STATE, LANES), BF16)])(data, weight)
     states = lax.all_to_all(states, "seq", 0, 0, tiled=True, axis_index_groups=STATE_GROUPS)
-    sums, grad, data = call(
+    inner, grad = call(
         inner_kernel, "inner", [SMEM, VMEM],
         [
-            ((6 * LOCAL + 8, LANES), F32),
-            ((2 * LOCAL + 3 * TOK, LANES), F32),
-            ((5 * LOCAL, LANES), BF16),
+            ((2 * LOCAL + 8, LANES), F32),
+            ((LOCAL + 3 * TOK, LANES), F32),
         ],
     )(decay_rate, data)
     keep, give, pairs = call(
-        outer_kernel, "outer", [VMEM] * 2,
-        [((LOCAL, LANES), F32)] * 2 + [((8 * LOCAL + 32, LANES), BF16)],
+        outer_kernel, "outer", [VMEM] * 4,
+        [sums] * 2 + [((8 * LOCAL + 32, LANES), BF16)],
         [pltpu.VMEM((BLOCKS, LANES, LANES), F32)] + [wide] * 2,
-    )(states, sums)
+    )(states, inner, data, grad)
     got = lax.ppermute(give, "seq", swap_core)
     (out,) = call(
-        grads_kernel, "grads", [SMEM] + [VMEM] * 3, [((SEQ, SLOT_OUT, LANES), BF16)], [wide]
+        grads_kernel, "grads", [SMEM] + [VMEM] * 3, [((SEQ, SLOT_OUT, LANES), BF16)],
+        [wide, pltpu.VMEM((SEQ * 8, LANES), F32)],
     )(decay_rate, data, pairs, grad)
     (out,) = call(join_kernel, "join", [VMEM] * 3, [((SEQ, SLOT_OUT, LANES), BF16)])(out, keep, got)
     back = lax.all_to_all(out, "seq", 0, 0, tiled=True)

time: 103 us -> 98.7 us (0.958)
  local copies, waits for them, and re-layouts: 4.44 us -> 0.03 us
  waiting for transfers between devices: 3.93 us -> 7.83 us
  blocking collectives: 65.9 us -> 63.8 us
  Pallas kernels: 17.8 us -> 16.4 us
    unnamed x20 -> x8, local copies, waits for them, and re-layouts: 4.44 us -> 0.03 us
    all_to_all x1, waiting for transfers between devices: 0.01 us -> 3.94 us  [shards(): lax.all_to_all(states, 'seq', 0, 0, tiled=True, axis_index_groups=STATE_G...]
    all_to_all x1, blocking collectives: 27 us -> 24.9 us  [shards(): back = lax.all_to_all(out, 'seq', 0, 0, tiled=True)]
    pallas_call x1, Pallas kernels: 3.98 us -> 2.45 us  [shards(): call(grads_kernel, 'grads', [SMEM] + [VMEM] * 3, [((SEQ, SLOT_OUT, LANES)...]
    pallas_call x3 -> x4, Pallas kernels: 6.59 us -> 6.8 us  [the longest x1 3.17 us: shards(): call(inner_kernel, 'inner', [SMEM, VMEM], [((2 * LOCAL + 8, LANES), F32),...]
  transfers between devices with their start and end apart: 6 -> 6, of which waited for: 3 -> 4; matrix products, arithmetic and copies ran while one was open for 0% -> 0% of each run, Pallas kernels for 11% -> 9%
where the time goes in v3:
time: 98.7 us; the launch traced here: 98.3 us
  blocking collectives  63.8 us (65%)
  Pallas kernels  16.4 us (17%)
  starting transfers between devices  9.52 us (10%)
  waiting for transfers between devices  7.83 us (8%)
    all_to_all x1, blocking collectives, shards(): recv = lax.all_to_all(send, 'seq', 0, 0, tiled=True)  38.9 us
    all_to_all x1, blocking collectives, shards(): back = lax.all_to_all(out, 'seq', 0, 0, tiled=True)  24.9 us
    all_to_all x1, starting transfers between devices, shards(): lax.all_to_all(states, 'seq', 0, 0, tiled=True, axis_index_groups=STATE_G...  4.13 us
    all_to_all x1, waiting for transfers between devices, shards(): lax.all_to_all(states, 'seq', 0, 0, tiled=True, axis_index_groups=STATE_G...  3.94 us
    ppermute x3, waiting for transfers between devices, shards(): lax.ppermute(proj, 'head', [(i, (i + k) % 4) for i in range(4)])  3.7 us
    ppermute x3, starting transfers between devices, shards(): lax.ppermute(proj, 'head', [(i, (i + k) % 4) for i in range(4)])  3.69 us
    pallas_call x1, Pallas kernels, shards(): call(inner_kernel, 'inner', [SMEM, VMEM], [((2 * LOCAL + 8, LANES), F32),...  3.17 us
    pallas_call x1, Pallas kernels, shards(): call(pack_kernel, 'pack', [SMEM, VMEM] + [hbm] * 6, [((SEQ, SLOT_IN, LANE...  2.9 us
  transfers between devices with their start and end apart: 6, of which 4 were waited for; matrix products, arithmetic and copies ran while one was open for 0% of the time, Pallas kernels for 9%

profile of v3, /device:TPU:1, one launch (start us, length us, event | category | flops | bytes accessed | tf_op | source)
XLA Modules:
  0.0 98.3 jit_solution(7410399291232189222)
XLA Ops:
  0.6 2.9 %pack.1 = bf16[64,56,128]{2,1,0:T(8,128)(2,1)} custom-call(s32[4]{0:T(128)} %frame_ref.3, s32[1,128]{1,0:T(1,128)} %bitcast.9, f32[16,128]{1,0:T(8,128)} %bitcast.7, f32[16,1000]{1,0:T(8,128)} %bitcast.5, bf16[128,128]{1,0:T(8,128)(2,1)} %refs_2_.1, bf16[128,128]{1,0:T(8,128)(2,1)} %refs_3_.1, bf16[128,1024]{1,0:T(8,128)(2,1)} %refs_4_.1, ...), custom_call_target="tpu_custom_call" | custom-call | tf_op jit(solution)/shard_map/pack/pallas_call | solution.py:561
  3.5 0.0 copy-start.2
  3.6 38.9 %all_to_all.15.recv_ref = bf16[64,56,128]{2,1,0:T(8,128)(2,1)S(1)} all-to-all(bf16[64,56,128]{2,1,0:T(8,128)(2,1)} %pack.1), channel_id=1, replica_groups=mesh['seq'=64,'head'=4] {'seq'}, dimensions={0} | all-to-all | bytes 1835008 | tf_op jit(solution)/shard_map/all_to_all | solution.py:566
  42.5 0.3 collective-permute-start
  42.8 0.0 copy-done.2
  42.8 1.9 %unpack.1 = (bf16[2560,128]{1,0:T(8,128)(2,1)S(1)}, bf16[1024,128]{1,0:T(8,128)(2,1)S(1)}, bf16[2064,128]{1,0:T(8,128)(2,1)S(1)}) custom-call(f32[16]{0:T(128)S(1)} %copy-done.2, bf16[64,56,128]{2,1,0:T(8,128)(2,1)S(1)} %all_to_all.15.recv_ref), custom_call_target="tpu_custom_call" | custom-call | tf_op jit(solution)/shard_map/unpack/pallas_call | solution.py:571
  44.8 0.2 collective-permute-done.swap_ref
  44.9 0.3 gather.1.all_ref.data_ref
  45.2 1.1 %states.1 = bf16[8,136,128]{2,1,0:T(8,128)(2,1)} custom-call(bf16[4608,128]{1,0:T(8,128)(2,1)S(1)} %gather.1.all_ref.data_ref, bf16[2064,128]{1,0:T(8,128)(2,1)S(1)} %get-tuple-element.22.weight_ref), custom_call_target="tpu_custom_call" | custom-call | tf_op jit(solution)/shard_map/states/pallas_call | solution.py:577
  46.3 4.1 %all-to-all-start.1 = ((bf16[8,136,128]{2,1,0:T(8,128)(2,1)}), bf16[8,136,128]{2,1,0:T(8,128)(2,1)S(1)}, u32[]{:S(2)}, u32[]{:S(2)}) async-start(bf16[8,136,128]{2,1,0:T(8,128)(2,1)} %states.1), calls=%async_computation.1 | async-start | bytes 557056 | tf_op jit(solution)/shard_map/all_to_all | solution.py:578
  50.4 3.2 %inner.1 = (f32[2056,128]{1,0:T(8,128)S(1)}, f32[1408,128]{1,0:T(8,128)S(1)}) custom-call(f32[16]{0:T(128)S(1)} %copy-done.2, bf16[4608,128]{1,0:T(8,128)(2,1)S(1)} %gather.1.all_ref.data_ref), custom_call_target="tpu_custom_call" | custom-call | tf_op jit(solution)/shard_map/inner/pallas_call | solution.py:579
  53.6 3.9 %all-to-all-done.1.recv_ref = bf16[8,136,128]{2,1,0:T(8,128)(2,1)S(1)} async-done(((bf16[8,136,128]{2,1,0:T(8,128)(2,1)}), bf16[8,136,128]{2,1,0:T(8,128)(2,1)S(1)}, u32[]{:S(2)}, u32[]{:S(2)}) %all-to-all-start.1) | async-done | bytes 278560 | tf_op jit(solution)/shard_map/all_to_all | solution.py:578
  57.6 2.2 %outer.1 = (f32[1024,128]{1,0:T(8,128)S(1)}, f32[1024,128]{1,0:T(8,128)S(1)}, bf16[8224,128]{1,0:T(8,128)(2,1)S(1)}) custom-call(bf16[8,136,128]{2,1,0:T(8,128)(2,1)S(1)} %all-to-all-done.1.recv_ref, f32[2056,128]{1,0:T(8,128)S(1)} %get-tuple-element.23.sums_ref, bf16[4608,128]{1,0:T(8,128)(2,1)S(1)} %gather.1.all_ref.data_ref, ...), custom_call_target="tpu_custom_call" | custom-call | tf_op jit(solution)/shard_map/outer/pallas_call | solution.py:586
  59.8 1.4 %collective-permute-start.1 = (f32[1024,128]{1,0:T(8,128)S(1)}, f32[1024,128]{1,0:T(8,128)S(1)}, u32[]{:S(2)}, u32[]{:S(2)}) collective-permute-start(f32[1024,128]{1,0:T(8,128)S(1)} %get-tuple-element.27), channel_id=1, source_target_pairs={{0,4},{4,0},{8,12},{12,8},{16,20},{20,16},{24,28},{28,24},{32,36},... | collective-permute-start | bytes 1572872 | tf_op jit(solution)/shard_map/ppermute | solution.py:591
  61.2 2.5 %grads.1.in_ref = bf16[64,40,128]{2,1,0:T(8,128)(2,1)S(1)} custom-call(f32[16]{0:T(128)S(1)} %copy-done.2, bf16[4608,128]{1,0:T(8,128)(2,1)S(1)} %gather.1.all_ref.data_ref, bf16[8224,128]{1,0:T(8,128)(2,1)S(1)} %get-tuple-element.25.all_ref, f32[1408,128]{1,0:T(8,128)S(1)} %get-tuple-element.24.grad_ref), custom_call_target="tpu_custom_call" | custom-call | tf_op jit(solution)/shard_map/grads/pallas_call | solution.py:592
  63.6 0.0 collective-permute-done.1.got_ref
  63.7 0.1 join.1
  63.8 0.0 copy-start
  63.8 0.0 copy-start.1
  63.8 0.0 copy-start.3
  63.8 24.9 %all_to_all.16.recv_ref = bf16[64,40,128]{2,1,0:T(8,128)(2,1)S(1)} all-to-all(bf16[64,40,128]{2,1,0:T(8,128)(2,1)S(1)} %join.1), channel_id=1, replica_groups=mesh['seq'=64,'head'=4] {'seq'}, dimensions={0} | all-to-all | bytes 1310720 | tf_op jit(solution)/shard_map/all_to_all | solution.py:597
  88.7 0.1 proj.1
  88.7 2.6 %collective-permute-start.4 = (bf16[128,256]{1,0:T(8,128)(2,1)S(1)}, bf16[128,256]{1,0:T(8,128)(2,1)S(1)}, u32[]{:S(2)}, u32[]{:S(2)}) collective-permute-start(bf16[128,256]{1,0:T(8,128)(2,1)S(1)} %get-tuple-element.30.own_ref), channel_id=1, source_target_pairs={{0,3},{1,0},{2,1},{3,2},{4,7},{5,4},{6,5},{7,6},{8,11},{9,8},{10,9... | collective-permute-start | bytes 196616 | tf_op jit(solution)/shard_map/ppermute | solution.py:601
  91.3 0.5 collective-permute-start.3
  91.8 0.6 collective-permute-start.2
  92.4 0.0 copy-done
  92.4 0.0 copy-done.1
  92.4 0.0 copy-done.3
  92.4 1.5 %finish.1 = (bf16[128,1024]{1,0:T(8,128)(2,1)}, f32[16,128]{1,0:T(8,128)}, f32[16,1000]{1,0:T(8,128)}) custom-call(s32[4]{0:T(128)S(1)} %copy-done.3, bf16[64,24,128]{2,1,0:T(8,128)(2,1)S(1)} %get-tuple-element.28.recv_ref, f32[16,128]{1,0:T(8,128)S(1)} %bitcast.8, f32[16,1000]{1,0:T(8,128)S(1)} %bitcast.6), custom_call_target="tpu_custom_call" | custom-call | tf_op jit(solution)/shard_map/finish/pallas_call | solution.py:602
  94.0 0.0 collective-permute-done.4.three_ref
  94.0 2.0 %collective-permute-done.3.two_ref = bf16[128,256]{1,0:T(8,128)(2,1)S(1)} collective-permute-done((bf16[128,256]{1,0:T(8,128)(2,1)S(1)}, bf16[128,256]{1,0:T(8,128)(2,1)S(1)}, u32[]{:S(2)}, u32[]{:S(2)}) %collective-permute-start.3) | collective-permute-done | bytes 65568 | tf_op jit(solution)/shard_map/ppermute | solution.py:601
  95.9 1.7 %collective-permute-done.2.one_ref = bf16[128,256]{1,0:T(8,128)(2,1)S(1)} collective-permute-done((bf16[128,256]{1,0:T(8,128)(2,1)S(1)}, bf16[128,256]{1,0:T(8,128)(2,1)S(1)}, u32[]{:S(2)}, u32[]{:S(2)}) %collective-permute-start.2) | collective-permute-done | bytes 65568 | tf_op jit(solution)/shard_map/ppermute | solution.py:601
  97.7 0.7 total.1
Async XLA Ops:
  3.5 39.3 %copy-start.2 = (f32[16]{0:T(128)S(1)}, f32[16]{0:T(128)}, u32[]{:S(2)}) copy-start(f32[16]{0:T(128)} %decay_ref.5) | copy-start | bytes 196
  42.5 2.5 %collective-permute-start = (bf16[64,56,128]{2,1,0:T(8,128)(2,1)S(1)}, bf16[64,56,128]{2,1,0:T(8,128)(2,1)S(1)}, u32[]{:S(2)}, u32[]{:S(2)}) collective-permute-start(bf16[64,56,128]{2,1,0:T(8,128)(2,1)S(1)} %all_to_all.15.recv_ref), channel_id=1, source_target_pairs={{0,4},{4,0},{8,12},{12,8},{16,20},{20,16},{24,28},{28,24},{32,36},... | collective-permute-start | bytes 2752520 | tf_op jit(solution)/shard_map/ppermute | solution.py:567
  46.3 11.3 %all-to-all-start.1 = ((bf16[8,136,128]{2,1,0:T(8,128)(2,1)}), bf16[8,136,128]{2,1,0:T(8,128)(2,1)S(1)}, u32[]{:S(2)}, u32[]{:S(2)}) async-start(bf16[8,136,128]{2,1,0:T(8,128)(2,1)} %states.1), calls=%async_computation.1 | async-start | bytes 557056 | tf_op jit(solution)/shard_map/all_to_all | solution.py:578
  59.8 3.8 %collective-permute-start.1 = (f32[1024,128]{1,0:T(8,128)S(1)}, f32[1024,128]{1,0:T(8,128)S(1)}, u32[]{:S(2)}, u32[]{:S(2)}) collective-permute-start(f32[1024,128]{1,0:T(8,128)S(1)} %get-tuple-element.27), channel_id=1, source_target_pairs={{0,4},{4,0},{8,12},{12,8},{16,20},{20,16},{24,28},{28,24},{32,36},... | collective-permute-start | bytes 1572872 | tf_op jit(solution)/shard_map/ppermute | solution.py:591
  63.8 28.7 %copy-start = (f32[1000,16]{0,1:T(8,128)S(1)}, f32[1000,16]{0,1:T(8,128)}, u32[]{:S(2)}) copy-start(f32[1000,16]{0,1:T(8,128)} %param.14) | copy-start | bytes 192004
  63.8 28.6 %copy-start.1 = (f32[128,16]{0,1:T(8,128)S(1)}, f32[128,16]{0,1:T(8,128)}, u32[]{:S(2)}) copy-start(f32[128,16]{0,1:T(8,128)} %param.13) | copy-start | bytes 24580
  63.8 28.6 %copy-start.3 = (s32[4]{0:T(128)S(1)}, s32[4]{0:T(128)}, u32[]{:S(2)}) copy-start(s32[4]{0:T(128)} %frame_ref.3) | copy-start | bytes 52
  88.7 5.2 %collective-permute-start.4 = (bf16[128,256]{1,0:T(8,128)(2,1)S(1)}, bf16[128,256]{1,0:T(8,128)(2,1)S(1)}, u32[]{:S(2)}, u32[]{:S(2)}) collective-permute-start(bf16[128,256]{1,0:T(8,128)(2,1)S(1)} %get-tuple-element.30.own_ref), channel_id=1, source_target_pairs={{0,3},{1,0},{2,1},{3,2},{4,7},{5,4},{6,5},{7,6},{8,11},{9,8},{10,9... | collective-permute-start | bytes 196616 | tf_op jit(solution)/shard_map/ppermute | solution.py:601
  91.3 4.7 %collective-permute-start.3 = (bf16[128,256]{1,0:T(8,128)(2,1)S(1)}, bf16[128,256]{1,0:T(8,128)(2,1)S(1)}, u32[]{:S(2)}, u32[]{:S(2)}) collective-permute-start(bf16[128,256]{1,0:T(8,128)(2,1)S(1)} %get-tuple-element.30.own_ref), channel_id=1, source_target_pairs={{0,2},{1,3},{2,0},{3,1},{4,6},{5,7},{6,4},{7,5},{8,10},{9,11},{10,... | collective-permute-start | bytes 196616 | tf_op jit(solution)/shard_map/ppermute | solution.py:601
  91.8 5.9 %collective-permute-start.2 = (bf16[128,256]{1,0:T(8,128)(2,1)S(1)}, bf16[128,256]{1,0:T(8,128)(2,1)S(1)}, u32[]{:S(2)}, u32[]{:S(2)}) collective-permute-start(bf16[128,256]{1,0:T(8,128)(2,1)S(1)} %get-tuple-element.30.own_ref), channel_id=1, source_target_pairs={{0,1},{1,2},{2,3},{3,0},{4,5},{5,6},{6,7},{7,4},{8,9},{9,10},{10,1... | collective-permute-start | bytes 196616 | tf_op jit(solution)/shard_map/ppermute | solution.py:601

commit v4 on v3

--- a/solution.py
+++ b/solution.py
@@ -74,28 +74,29 @@
     return raw + shift
 
 
-def pack_kernel(frame_ref, order_ref, *refs):
-    sources, out_ref, targets, sems = refs[:6], refs[6], refs[7:13], refs[13]
+def pack_kernel(*refs):
+    sources, out_ref, targets, sems = refs[:8], refs[8], refs[9:17], refs[17]
     copies = [
         pltpu.make_async_copy(source, target, sems.at[i])
         for i, (source, target) in enumerate(zip(sources, targets))
     ]
     for copy in copies:
         copy.start()
-    raw_ref, table_ref, b_ref, c_ref, x_ref, dy_ref = targets
+    order_ref, frame_ref, raw_ref, table_ref, b_ref, c_ref, x_ref, dy_ref = targets
+    copies[0].wait()
     order = jnp.broadcast_to(order_ref[...].astype(F32), (TOK, TOK)).T
     lane = lane_iota(TOK)
     token = ((lane % 64) * 2 + lane // 64).astype(F32)
     steps = lax.broadcasted_iota(jnp.int32, (TOK, TOK), 0).astype(F32)
     position = jnp.sum(jnp.where(order == token, steps, 0.0), axis=0, keepdims=True)
-    copies[0].wait()
-    copies[1].wait()
+    for copy in copies[1:4]:
+        copy.wait()
     pre = shifted_steps(frame_ref, raw_ref[...], table_ref[...])
     delta = softplus(pre).astype(BF16).astype(F32)
     gate = sigmoid(pre)
     gate_high = gate.astype(BF16).astype(F32)
     gate_low = gate - gate_high
-    for copy in copies[2:]:
+    for copy in copies[4:]:
         copy.wait()
     for pair in range(PAIRS):
         own = slice(2 * pair, 2 * pair + 2)
@@ -120,7 +121,11 @@
 
 
 def slope_lanes(decay_ref, pair, rows):
-    return jnp.where(lane_iota(rows) % 2 == 0, -decay_ref[2 * pair], -decay_ref[2 * pair + 1])
+    rates = decay_ref[...]
+    lane = lax.broadcasted_iota(jnp.int32, rates.shape, 1)
+    first = jnp.sum(jnp.where(lane == 2 * pair, rates, 0.0), axis=1, keepdims=True)
+    second = jnp.sum(jnp.where(lane == 2 * pair + 1, rates, 0.0), axis=1, keepdims=True)
+    return jnp.where(lane_iota(rows) % 2 == 0, -first, -second)
 
 
 def block_lanes(columns, block, rows):
@@ -153,6 +158,10 @@
     for row in range(16):
         start = base + row * 64
         target_ref[start : start + 64, :] = wide[pl.ds(row, 64, stride=16), :].astype(BF16)
+
+
+def cut_kernel(recv_ref, proj_ref):
+    proj_ref[...] = recv_ref[:, 32:48, :]
 
 
 def unpack_kernel(
@@ -222,12 +231,12 @@
     @pl.when(core == 0)
     def _():
         all_ref[2 * LOCAL : 3 * LOCAL, :] = mine_ref[...]
-        spread(swap_ref[:, 32:48, :].astype(F32), wide, all_ref, 3 * LOCAL)
+        spread(swap_ref[...].astype(F32), wide, all_ref, 3 * LOCAL)
 
     @pl.when(core == 1)
     def _():
         all_ref[3 * LOCAL : 4 * LOCAL, :] = mine_ref[...]
-        spread(swap_ref[:, 32:48, :].astype(F32), wide, all_ref, 2 * LOCAL)
+        spread(swap_ref[...].astype(F32), wide, all_ref, 2 * LOCAL)
 
 
 def states_kernel(all_ref, weight_ref, send_ref):
@@ -322,14 +331,24 @@
 def outer_kernel(recv_ref, sums_ref, data_ref, grad_ref, keep_ref, give_ref, all_ref, adj, wide_w, wide_r):
     part, pair, core = my_place()
 
-    def arrive(slot, state):
+    totals = []
+    for slot in range(PARTS):
         tail = recv_ref[slot, 128:136, :].astype(F32)
-        total = tail[0:1] + tail[1:2] + tail[2:3]
-        return state * jnp.exp(total) + recv_ref[slot, 0:128, :].astype(F32)
-
-    zero = jnp.zeros((LANES, LANES), F32)
-    state = lax.fori_loop(0, part, arrive, zero)
-    adjoint = lax.fori_loop(0, PARTS - 1 - part, lambda k, a: arrive(PARTS - 1 - k, a), zero)
+        totals.append(tail[0:1] + tail[1:2] + tail[2:3])
+    zero = jnp.zeros((1, LANES), F32)
+    state = jnp.zeros((LANES, LANES), F32)
+    adjoint = jnp.zeros((LANES, LANES), F32)
+    after, before = zero, zero
+    weights = [None] * PARTS
+    for slot in reversed(range(PARTS)):
+        weights[slot] = jnp.where(slot < part, jnp.exp(after), zero)
+        after = after + jnp.where(slot < part, totals[slot], zero)
+    for slot in range(PARTS):
+        weight = jnp.where(slot > part, jnp.exp(before), zero)
+        before = before + jnp.where(slot > part, totals[slot], zero)
+        sent = recv_ref[slot, 0:128, :].astype(F32)
+        state = state + weights[slot] * sent
+        adjoint = adjoint + weight * sent
     keeps = jnp.exp(sums_ref[2 * LOCAL : 2 * LOCAL + 8, :])
 
     def sums_rows(number, block):
@@ -555,34 +574,38 @@
     activations, grad_out, write_proj, read_proj, step_raw, step_table, decay_rate, frame_step, scan_order
 ):
     raw, table = step_raw.T, step_table.T
+    rates = decay_rate.reshape(1, decay_rate.shape[0])
     swap_core = [(i, i ^ 1) for i in range(SEQ)]
     hbm = pl.BlockSpec(memory_space=pltpu.HBM)
-    sources = (raw, table, write_proj, read_proj, activations, grad_out)
+    order = scan_order.reshape(1, TOK)
+    sources = (order, frame_step, raw, table, write_proj, read_proj, activations, grad_out)
     (send,) = call(
-        pack_kernel, "pack", [SMEM, VMEM] + [hbm] * 6, [((SEQ, SLOT_IN, LANES), BF16)],
-        [pltpu.VMEM(a.shape, a.dtype) for a in sources] + [pltpu.SemaphoreType.DMA((6,))],
+        pack_kernel, "pack", [hbm] * 8, [((SEQ, SLOT_IN, LANES), BF16)],
+        [(pltpu.SMEM if a is frame_step else pltpu.VMEM)(a.shape, a.dtype) for a in sources]
+        + [pltpu.SemaphoreType.DMA((8,))],
         pltpu.CompilerParams(vmem_limit_bytes=62 * 1024 * 1024),
-    )(frame_step, scan_order.reshape(1, TOK), *sources)
+    )(*sources)
     recv = lax.all_to_all(send, "seq", 0, 0, tiled=True)
-    swap = lax.ppermute(recv, "seq", swap_core)
+    (proj,) = call(cut_kernel, "cut", [VMEM], [((SEQ, 16, LANES), BF16)])(recv)
+    swap = lax.ppermute(proj, "seq", swap_core)
     wide = pltpu.VMEM((LOCAL, LANES), F32)
     bundle = ((4 * LOCAL + 4 * TOK, LANES), BF16)
     sums = ((LOCAL, LANES), F32)
     data, mine, weight = call(
-        unpack_kernel, "unpack", [SMEM, VMEM],
+        unpack_kernel, "unpack", [VMEM] * 2,
         [((2 * LOCAL + 4 * TOK, LANES), BF16), ((LOCAL, LANES), BF16), ((2 * LOCAL + 16, LANES), BF16)],
         [wide] * 3 + [pltpu.VMEM((SEQ * 8, LANES), F32)],
-    )(decay_rate, recv)
+    )(rates, recv)
     (data,) = call(gather_kernel, "gather", [VMEM] * 3, [bundle], [wide])(mine, swap, data)
     (states,) = call(states_kernel, "states", [VMEM] * 2, [((PARTS, SLOT_STATE, LANES), BF16)])(data, weight)
     states = lax.all_to_all(states, "seq", 0, 0, tiled=True, axis_index_groups=STATE_GROUPS)
     inner, grad = call(
-        inner_kernel, "inner", [SMEM, VMEM],
+        inner_kernel, "inner", [VMEM] * 2,
         [
             ((2 * LOCAL + 8, LANES), F32),
             ((LOCAL + 3 * TOK, LANES), F32),
         ],
-    )(decay_rate, data)
+    )(rates, data)
     keep, give, pairs = call(
         outer_kernel, "outer", [VMEM] * 4,
         [sums] * 2 + [((8 * LOCAL + 32, LANES), BF16)],
@@ -590,9 +613,9 @@
     )(states, inner, data, grad)
     got = lax.ppermute(give, "seq", swap_core)
     (out,) = call(
-        grads_kernel, "grads", [SMEM] + [VMEM] * 3, [((SEQ, SLOT_OUT, LANES), BF16)],
+        grads_kernel, "grads", [VMEM] * 4, [((SEQ, SLOT_OUT, LANES), BF16)],
         [wide, pltpu.VMEM((SEQ * 8, LANES), F32)],
-    )(decay_rate, data, pairs, grad)
+    )(rates, data, pairs, grad)
     (out,) = call(join_kernel, "join", [VMEM] * 3, [((SEQ, SLOT_OUT, LANES), BF16)])(out, keep, got)
     back = lax.all_to_all(out, "seq", 0, 0, tiled=True)
     proj, rest = call(

time: 98.7 us -> 96.9 us (0.982)
  Pallas kernels: 16.4 us -> 14 us
    pallas_call x4 -> x5, Pallas kernels: 10.5 us -> 8.22 us  [the longest x1 2.56 us: shards(): call(inner_kernel, 'inner', [VMEM] * 2, [((2 * LOCAL + 8, LANES), F32), (...]
  transfers between devices with their start and end apart: 6 -> 6, of which waited for: 4 -> 3; matrix products, arithmetic and copies ran while one was open for 0% -> 0% of each run, Pallas kernels for 9% -> 8%
where the time goes in v4:
time: 96.9 us; the launch traced here: 96.5 us
  blocking collectives  64.1 us (66%)
  Pallas kernels  14 us (14%)
  starting transfers between devices  9.66 us (10%)
  waiting for transfers between devices  7.91 us (8%)
    all_to_all x1, blocking collectives, shards(): recv = lax.all_to_all(send, 'seq', 0, 0, tiled=True)  38.9 us
    all_to_all x1, blocking collectives, shards(): back = lax.all_to_all(out, 'seq', 0, 0, tiled=True)  25.2 us
    all_to_all x1, waiting for transfers between devices, shards(): lax.all_to_all(states, 'seq', 0, 0, tiled=True, axis_index_groups=STATE_G...  4.19 us
    all_to_all x1, starting transfers between devices, shards(): lax.all_to_all(states, 'seq', 0, 0, tiled=True, axis_index_groups=STATE_G...  3.81 us
    ppermute x3, waiting for transfers between devices, shards(): lax.ppermute(proj, 'head', [(i, (i + k) % 4) for i in range(4)])  3.72 us
    ppermute x3, starting transfers between devices, shards(): lax.ppermute(proj, 'head', [(i, (i + k) % 4) for i in range(4)])  3.68 us
    pallas_call x1, Pallas kernels, shards(): call(inner_kernel, 'inner', [VMEM] * 2, [((2 * LOCAL + 8, LANES), F32), (...  2.56 us
    pallas_call x1, Pallas kernels, shards(): call(pack_kernel, 'pack', [hbm] * 8, [((SEQ, SLOT_IN, LANES), BF16)], [(p...  2.27 us
  transfers between devices with their start and end apart: 6, of which 3 were waited for; matrix products, arithmetic and copies ran while one was open for 0% of the time, Pallas kernels for 8%

profile of v4, /device:TPU:1, one launch (start us, length us, event | category | flops | bytes accessed | tf_op | source)
XLA Modules:
  0.0 96.5 jit_solution(3435719101803996013)
XLA Ops:
  0.6 2.3 %pack.1 = bf16[64,56,128]{2,1,0:T(8,128)(2,1)} custom-call(s32[1,128]{1,0:T(1,128)} %bitcast.13, s32[4]{0:T(128)} %frame_ref.1, f32[16,128]{1,0:T(8,128)} %bitcast.8, f32[16,1000]{1,0:T(8,128)} %bitcast.6, bf16[128,128]{1,0:T(8,128)(2,1)} %refs_4_.1, bf16[128,128]{1,0:T(8,128)(2,1)} %refs_5_.1, bf16[128,1024]{1,0:T(8,128)(2,1)} %refs_6_.1, ...), custom_call_target="tpu_custom_call" | custom-call | tf_op jit(solution)/shard_map/pack/pallas_call | solution.py:582
  2.9 0.0 copy-start.2
  2.9 38.9 %all_to_all.15.recv_ref = bf16[64,56,128]{2,1,0:T(8,128)(2,1)S(1)} all-to-all(bf16[64,56,128]{2,1,0:T(8,128)(2,1)} %pack.1), channel_id=1, replica_groups=mesh['seq'=64,'head'=4] {'seq'}, dimensions={0} | all-to-all | bytes 1835008 | tf_op jit(solution)/shard_map/all_to_all | solution.py:588
  41.9 0.4 collective-permute-start
  42.3 0.0 copy-done.2
  42.3 1.5 %unpack.1 = (bf16[2560,128]{1,0:T(8,128)(2,1)S(1)}, bf16[1024,128]{1,0:T(8,128)(2,1)S(1)}, bf16[2064,128]{1,0:T(8,128)(2,1)S(1)}) custom-call(f32[1,16]{1,0:T(1,128)S(1)} %bitcast.10, bf16[64,56,128]{2,1,0:T(8,128)(2,1)S(1)} %all_to_all.15.recv_ref), custom_call_target="tpu_custom_call" | custom-call | tf_op jit(solution)/shard_map/unpack/pallas_call | solution.py:594
  43.8 0.0 collective-permute-done.swap_ref
  43.8 0.3 gather.1.all_ref.data_ref
  44.0 1.1 %states.1 = bf16[8,136,128]{2,1,0:T(8,128)(2,1)} custom-call(bf16[4608,128]{1,0:T(8,128)(2,1)S(1)} %gather.1.all_ref.data_ref, bf16[2064,128]{1,0:T(8,128)(2,1)S(1)} %get-tuple-element.22.weight_ref), custom_call_target="tpu_custom_call" | custom-call | tf_op jit(solution)/shard_map/states/pallas_call | solution.py:600
  45.2 3.8 %all-to-all-start.1 = ((bf16[8,136,128]{2,1,0:T(8,128)(2,1)}), bf16[8,136,128]{2,1,0:T(8,128)(2,1)S(1)}, u32[]{:S(2)}, u32[]{:S(2)}) async-start(bf16[8,136,128]{2,1,0:T(8,128)(2,1)} %states.1), calls=%async_computation.1 | async-start | bytes 557056 | tf_op jit(solution)/shard_map/all_to_all | solution.py:601
  49.0 2.6 %inner.1 = (f32[2056,128]{1,0:T(8,128)S(1)}, f32[1408,128]{1,0:T(8,128)S(1)}) custom-call(f32[1,16]{1,0:T(1,128)S(1)} %bitcast.11, bf16[4608,128]{1,0:T(8,128)(2,1)S(1)} %gather.1.all_ref.data_ref), custom_call_target="tpu_custom_call" | custom-call | tf_op jit(solution)/shard_map/inner/pallas_call | solution.py:602
  51.5 4.2 %all-to-all-done.1.recv_ref = bf16[8,136,128]{2,1,0:T(8,128)(2,1)S(1)} async-done(((bf16[8,136,128]{2,1,0:T(8,128)(2,1)}), bf16[8,136,128]{2,1,0:T(8,128)(2,1)S(1)}, u32[]{:S(2)}, u32[]{:S(2)}) %all-to-all-start.1) | async-done | bytes 278560 | tf_op jit(solution)/shard_map/all_to_all | solution.py:601
  55.7 2.1 %outer.1 = (f32[1024,128]{1,0:T(8,128)S(1)}, f32[1024,128]{1,0:T(8,128)S(1)}, bf16[8224,128]{1,0:T(8,128)(2,1)S(1)}) custom-call(bf16[8,136,128]{2,1,0:T(8,128)(2,1)S(1)} %all-to-all-done.1.recv_ref, f32[2056,128]{1,0:T(8,128)S(1)} %get-tuple-element.23.sums_ref, bf16[4608,128]{1,0:T(8,128)(2,1)S(1)} %gather.1.all_ref.data_ref, ...), custom_call_target="tpu_custom_call" | custom-call | tf_op jit(solution)/shard_map/outer/pallas_call | solution.py:609
  57.8 1.7 %collective-permute-start.1 = (f32[1024,128]{1,0:T(8,128)S(1)}, f32[1024,128]{1,0:T(8,128)S(1)}, u32[]{:S(2)}, u32[]{:S(2)}) collective-permute-start(f32[1024,128]{1,0:T(8,128)S(1)} %get-tuple-element.27), channel_id=1, source_target_pairs={{0,4},{4,0},{8,12},{12,8},{16,20},{20,16},{24,28},{28,24},{32,36},... | collective-permute-start | bytes 1572872 | tf_op jit(solution)/shard_map/ppermute | solution.py:614
  59.6 1.9 %grads.1.in_ref = bf16[64,40,128]{2,1,0:T(8,128)(2,1)S(1)} custom-call(f32[1,16]{1,0:T(1,128)S(1)} %bitcast.12, bf16[4608,128]{1,0:T(8,128)(2,1)S(1)} %gather.1.all_ref.data_ref, bf16[8224,128]{1,0:T(8,128)(2,1)S(1)} %get-tuple-element.25.all_ref, f32[1408,128]{1,0:T(8,128)S(1)} %get-tuple-element.24.grad_ref), custom_call_target="tpu_custom_call" | custom-call | tf_op jit(solution)/shard_map/grads/pallas_call | solution.py:615
  61.5 0.0 collective-permute-done.1.got_ref
  61.5 0.1 join.1
  61.6 0.0 copy-start
  61.6 0.0 copy-start.1
  61.6 0.0 copy-start.3
  61.6 25.2 %all_to_all.16.recv_ref = bf16[64,40,128]{2,1,0:T(8,128)(2,1)S(1)} all-to-all(bf16[64,40,128]{2,1,0:T(8,128)(2,1)S(1)} %join.1), channel_id=1, replica_groups=mesh['seq'=64,'head'=4] {'seq'}, dimensions={0} | all-to-all | bytes 1310720 | tf_op jit(solution)/shard_map/all_to_all | solution.py:620
  86.8 0.1 proj.1
  86.9 2.5 %collective-permute-start.4 = (bf16[128,256]{1,0:T(8,128)(2,1)S(1)}, bf16[128,256]{1,0:T(8,128)(2,1)S(1)}, u32[]{:S(2)}, u32[]{:S(2)}) collective-permute-start(bf16[128,256]{1,0:T(8,128)(2,1)S(1)} %get-tuple-element.30.own_ref), channel_id=1, source_target_pairs={{0,3},{1,0},{2,1},{3,2},{4,7},{5,4},{6,5},{7,6},{8,11},{9,8},{10,9... | collective-permute-start | bytes 196616 | tf_op jit(solution)/shard_map/ppermute | solution.py:624
  89.4 0.5 collective-permute-start.3
  90.0 0.6 collective-permute-start.2
  90.6 0.0 copy-done
  90.6 0.0 copy-done.1
  90.6 0.0 copy-done.3
  90.6 1.5 %finish.1 = (bf16[128,1024]{1,0:T(8,128)(2,1)}, f32[16,128]{1,0:T(8,128)}, f32[16,1000]{1,0:T(8,128)}) custom-call(s32[4]{0:T(128)S(1)} %copy-done.3, bf16[64,24,128]{2,1,0:T(8,128)(2,1)S(1)} %get-tuple-element.28.recv_ref, f32[16,128]{1,0:T(8,128)S(1)} %bitcast.9, f32[16,1000]{1,0:T(8,128)S(1)} %bitcast.7), custom_call_target="tpu_custom_call" | custom-call | tf_op jit(solution)/shard_map/finish/pallas_call | solution.py:625
  92.1 0.0 collective-permute-done.4.three_ref
  92.1 2.0 %collective-permute-done.3.two_ref = bf16[128,256]{1,0:T(8,128)(2,1)S(1)} collective-permute-done((bf16[128,256]{1,0:T(8,128)(2,1)S(1)}, bf16[128,256]{1,0:T(8,128)(2,1)S(1)}, u32[]{:S(2)}, u32[]{:S(2)}) %collective-permute-start.3) | collective-permute-done | bytes 65568 | tf_op jit(solution)/shard_map/ppermute | solution.py:624
  94.1 1.7 %collective-permute-done.2.one_ref = bf16[128,256]{1,0:T(8,128)(2,1)S(1)} collective-permute-done((bf16[128,256]{1,0:T(8,128)(2,1)S(1)}, bf16[128,256]{1,0:T(8,128)(2,1)S(1)}, u32[]{:S(2)}, u32[]{:S(2)}) %collective-permute-start.2) | collective-permute-done | bytes 65568 | tf_op jit(solution)/shard_map/ppermute | solution.py:624
  95.8 0.7 total.1
  (1 shorter events, 0.0 us)
Async XLA Ops:
  2.9 39.4 %copy-start.2 = (f32[16]{0:T(128)S(1)}, f32[16]{0:T(128)}, u32[]{:S(2)}) copy-start(f32[16]{0:T(128)} %param.15) | copy-start | bytes 196
  41.9 1.9 %collective-permute-start = (bf16[64,16,128]{2,1,0:T(8,128)(2,1)S(1)}, bf16[64,16,128]{2,1,0:T(8,128)(2,1)S(1)}, u32[]{:S(2)}, u32[]{:S(2)}) collective-permute-start(bf16[64,16,128]{2,1,0:T(8,128)(2,1)S(1)} %cut.1), channel_id=1, source_target_pairs={{0,4},{4,0},{8,12},{12,8},{16,20},{20,16},{24,28},{28,24},{32,36},... | collective-permute-start | bytes 786440 | tf_op jit(solution)/shard_map/ppermute | solution.py:590
  45.2 10.6 %all-to-all-start.1 = ((bf16[8,136,128]{2,1,0:T(8,128)(2,1)}), bf16[8,136,128]{2,1,0:T(8,128)(2,1)S(1)}, u32[]{:S(2)}, u32[]{:S(2)}) async-start(bf16[8,136,128]{2,1,0:T(8,128)(2,1)} %states.1), calls=%async_computation.1 | async-start | bytes 557056 | tf_op jit(solution)/shard_map/all_to_all | solution.py:601
  57.8 3.7 %collective-permute-start.1 = (f32[1024,128]{1,0:T(8,128)S(1)}, f32[1024,128]{1,0:T(8,128)S(1)}, u32[]{:S(2)}, u32[]{:S(2)}) collective-permute-start(f32[1024,128]{1,0:T(8,128)S(1)} %get-tuple-element.27), channel_id=1, source_target_pairs={{0,4},{4,0},{8,12},{12,8},{16,20},{20,16},{24,28},{28,24},{32,36},... | collective-permute-start | bytes 1572872 | tf_op jit(solution)/shard_map/ppermute | solution.py:614
  61.6 29.0 %copy-start = (f32[1000,16]{0,1:T(8,128)S(1)}, f32[1000,16]{0,1:T(8,128)}, u32[]{:S(2)}) copy-start(f32[1000,16]{0,1:T(8,128)} %param.14) | copy-start | bytes 192004
  61.6 29.0 %copy-start.1 = (f32[128,16]{0,1:T(8,128)S(1)}, f32[128,16]{0,1:T(8,128)}, u32[]{:S(2)}) copy-start(f32[128,16]{0,1:T(8,128)} %param.13) | copy-start | bytes 24580
  61.6 29.0 %copy-start.3 = (s32[4]{0:T(128)S(1)}, s32[4]{0:T(128)}, u32[]{:S(2)}) copy-start(s32[4]{0:T(128)} %frame_ref.1) | copy-start | bytes 52
  86.9 5.2 %collective-permute-start.4 = (bf16[128,256]{1,0:T(8,128)(2,1)S(1)}, bf16[128,256]{1,0:T(8,128)(2,1)S(1)}, u32[]{:S(2)}, u32[]{:S(2)}) collective-permute-start(bf16[128,256]{1,0:T(8,128)(2,1)S(1)} %get-tuple-element.30.own_ref), channel_id=1, source_target_pairs={{0,3},{1,0},{2,1},{3,2},{4,7},{5,4},{6,5},{7,6},{8,11},{9,8},{10,9... | collective-permute-start | bytes 196616 | tf_op jit(solution)/shard_map/ppermute | solution.py:624
  89.4 4.7 %collective-permute-start.3 = (bf16[128,256]{1,0:T(8,128)(2,1)S(1)}, bf16[128,256]{1,0:T(8,128)(2,1)S(1)}, u32[]{:S(2)}, u32[]{:S(2)}) collective-permute-start(bf16[128,256]{1,0:T(8,128)(2,1)S(1)} %get-tuple-element.30.own_ref), channel_id=1, source_target_pairs={{0,2},{1,3},{2,0},{3,1},{4,6},{5,7},{6,4},{7,5},{8,10},{9,11},{10,... | collective-permute-start | bytes 196616 | tf_op jit(solution)/shard_map/ppermute | solution.py:624
  90.0 5.9 %collective-permute-start.2 = (bf16[128,256]{1,0:T(8,128)(2,1)S(1)}, bf16[128,256]{1,0:T(8,128)(2,1)S(1)}, u32[]{:S(2)}, u32[]{:S(2)}) collective-permute-start(bf16[128,256]{1,0:T(8,128)(2,1)S(1)} %get-tuple-element.30.own_ref), channel_id=1, source_target_pairs={{0,1},{1,2},{2,3},{3,0},{4,5},{5,6},{6,7},{7,4},{8,9},{9,10},{10,1... | collective-permute-start | bytes 196616 | tf_op jit(solution)/shard_map/ppermute | solution.py:624

commit v5 on v4

--- a/solution.py
+++ b/solution.py
@@ -75,7 +75,7 @@
 
 
 def pack_kernel(*refs):
-    sources, out_ref, targets, sems = refs[:8], refs[8], refs[9:17], refs[17]
+    sources, sent_ref, targets, out_ref, sems = refs[:8], refs[8], refs[9:17], refs[17], refs[18]
     copies = [
         pltpu.make_async_copy(source, target, sems.at[i])
         for i, (source, target) in enumerate(zip(sources, targets))
@@ -98,20 +98,31 @@
     gate_low = gate - gate_high
     for copy in copies[4:]:
         copy.wait()
+    rows = []
     for pair in range(PAIRS):
         own = slice(2 * pair, 2 * pair + 2)
-        rows = jnp.concatenate(
-            [position, delta[own], gate_high[own], gate_low[own], jnp.zeros((1, LANES), F32)], axis=0
-        ).astype(BF16)
-        proj_ref = c_ref if pair % 2 else b_ref
-        columns = slice(LANES * pair, LANES * pair + LANES)
-        for part in range(PARTS):
-            slot = place(part, pair)
+        rows.append(
+            jnp.concatenate(
+                [position, delta[own], gate_high[own], gate_low[own], jnp.zeros((1, LANES), F32)], axis=0
+            ).astype(BF16)
+        )
+    leaving = []
+    for quarter in range(4):
+        for part in (2 * quarter, 2 * quarter + 1):
             tokens = slice(16 * part, 16 * part + 16)
-            out_ref[slot, 0:16, :] = x_ref[tokens, columns]
-            out_ref[slot, 16:32, :] = dy_ref[tokens, columns]
-            out_ref[slot, 32:48, :] = proj_ref[tokens, :]
-            out_ref[slot, 48:56, :] = rows
+            for pair in range(PAIRS):
+                proj_ref = c_ref if pair % 2 else b_ref
+                columns = slice(LANES * pair, LANES * pair + LANES)
+                slot = place(part, pair)
+                out_ref[slot, 0:16, :] = x_ref[tokens, columns]
+                out_ref[slot, 16:32, :] = dy_ref[tokens, columns]
+                out_ref[slot, 32:48, :] = proj_ref[tokens, :]
+                out_ref[slot, 48:56, :] = rows[pair]
+        slots = pl.ds(16 * quarter, 16)
+        leaving.append(pltpu.make_async_copy(out_ref.at[slots], sent_ref.at[slots], sems.at[8 + quarter]))
+        leaving[quarter].start()
+    for copy in leaving:
+        copy.wait()
 
 
 def to_columns(first, second):
@@ -328,7 +339,7 @@
         sums_ref[sums_rows(1), :] = nn(twice_split(both.T), jnp.concatenate([write, write], axis=0))
 
 
-def outer_kernel(recv_ref, sums_ref, data_ref, grad_ref, keep_ref, give_ref, all_ref, adj, wide_w, wide_r):
+def outer_kernel(recv_ref, sums_ref, data_ref, grad_ref, keep_ref, give_ref, all_ref, adj):
     part, pair, core = my_place()
 
     totals = []
@@ -394,10 +405,13 @@
         gw = sums_ref[sums_rows(0, block), :] + (
             nt(jnp.concatenate([xe_high, xe_low], axis=1), twice(adj_high)) + nt(xe_high, adj_low)
         )
+        kept = jnp.where(core == 0, gw, gr)
+        given = jnp.where(core == 0, gr, gw)
         for half in range(2):
             out_rows = pl.ds(2 * block + half, 64, stride=16)
-            wide_w[out_rows, :] = gw[64 * half : 64 * half + 64]
-            wide_r[out_rows, :] = gr[64 * half : 64 * half + 64]
+            own_rows = slice(64 * half, 64 * half + 64)
+            keep_ref[out_rows, :] = kept[own_rows]
+            give_ref[out_rows, :] = given[own_rows]
         state = state * keep + gains[block][0]
     overlaps = jnp.concatenate(overlaps, axis=0)
     top = overlaps.astype(BF16).astype(F32)
@@ -406,16 +420,6 @@
     all_ref[8 * LOCAL : 8 * LOCAL + 32, :] = jnp.concatenate(
         [top, middle, bottom, jnp.zeros((8, LANES), F32)], axis=0
     ).astype(BF16)
-
-    @pl.when(core == 0)
-    def _():
-        keep_ref[...] = wide_w[...]
-        give_ref[...] = wide_r[...]
-
-    @pl.when(core == 1)
-    def _():
-        keep_ref[...] = wide_r[...]
-        give_ref[...] = wide_w[...]
 
 
 def grads_kernel(decay_ref, data_ref, all_ref, grad_ref, out_ref, wide, misc):
@@ -481,7 +485,7 @@
         low_rows = slice(16 * frame, 16 * frame + 16)
         high_rows = slice(64 + 16 * frame, 80 + 16 * frame)
         frames.append(jnp.sum(grad_pre[low_rows] + grad_pre[high_rows], axis=0, keepdims=True))
-    frames = jnp.concatenate(frames + [jnp.zeros((4, LANES), F32)], axis=0)
+    frames = sum(pltpu.roll(jnp.where(lane_iota(1) < 16, row, 0.0), 16 * i, 1) for i, row in enumerate(frames))
     frames_high = frames.astype(BF16).astype(F32)
     frames = frames_high + pltpu.roll(frames - frames_high, 64, 1)
 
@@ -493,28 +497,28 @@
     misc[...] = jnp.zeros((SEQ * 8, LANES), F32)
     misc[pl.ds(0, 64, stride=8), :] = row_one
     misc[pl.ds(1, 64, stride=8), :] = row_two
-    for frame in range(4):
-        misc[pl.ds(2 + frame, 64, stride=8), :] = jnp.broadcast_to(frames[frame : frame + 1], (SEQ, LANES))
+    misc[pl.ds(2, 64, stride=8), :] = jnp.broadcast_to(frames, (SEQ, LANES))
     out_ref[:, 0:16, :] = wide[...].reshape(SEQ, 16, LANES).astype(BF16)
     out_ref[:, 16:32, :] = jnp.zeros((SEQ, 16, LANES), BF16)
     out_ref[:, 32:40, :] = misc[...].reshape(SEQ, 8, LANES).astype(BF16)
 
 
 def join_kernel(in_ref, keep_ref, got_ref, out_ref):
-    out_ref[:, 0:16, :] = in_ref[:, 0:16, :]
-    out_ref[:, 16:32, :] = (keep_ref[...] + got_ref[...]).reshape(SEQ, 16, LANES).astype(BF16)
-    out_ref[:, 32:40, :] = in_ref[:, 32:40, :]
+    out_ref[:, 0:4] = in_ref[:, 0:16, :].reshape(SEQ, 4, 4, LANES)
+    proj = (keep_ref[...] + got_ref[...]).reshape(SEQ, 16, LANES).astype(BF16)
+    out_ref[:, 4:8] = proj.reshape(SEQ, 4, 4, LANES)
+    out_ref[:, 8:9] = in_ref[:, 32:40, :].reshape(SEQ, 2, 4, LANES)[:, 0:1]
 
 
 def proj_kernel(recv_ref, proj_ref, rest_ref):
     for part in range(PARTS):
         for core in range(2):
-            total = recv_ref[place(part, core), 16:32, :].astype(F32)
+            total = recv_ref[place(part, core), 4:8].reshape(16, LANES).astype(F32)
             for high in range(1, 4):
-                total = total + recv_ref[place(part, 2 * high + core), 16:32, :].astype(F32)
+                total = total + recv_ref[place(part, 2 * high + core), 4:8].reshape(16, LANES).astype(F32)
             proj_ref[16 * part : 16 * part + 16, LANES * core : LANES * core + LANES] = total.astype(BF16)
-    rest_ref[:, 0:16, :] = recv_ref[:, 0:16, :]
-    rest_ref[:, 16:24, :] = recv_ref[:, 32:40, :]
+    rest_ref[:, 0:4] = recv_ref[:, 0:4]
+    rest_ref[:, 4:5] = recv_ref[:, 8:9]
 
 
 def finish_kernel(frame_ref, recv_ref, raw_ref, table_ref, act_ref, pre_ref, grad_ref, rows_ref):
@@ -522,26 +526,33 @@
     for pair in range(PAIRS):
         columns = slice(LANES * pair, LANES * pair + LANES)
         for part in range(PARTS):
-            act_ref[16 * part : 16 * part + 16, columns] = recv_ref[place(part, pair), 0:16, :]
+            act_ref[16 * part : 16 * part + 16, columns] = recv_ref[place(part, pair), 0:4].reshape(16, LANES)
     lane = lane_iota(8)
-    per_frame = jnp.zeros((8, LANES), F32)
+    row = lax.broadcasted_iota(jnp.int32, (8, LANES), 0)
+    sums = []
     for pair in range(PAIRS):
-        rows = recv_ref[place(0, pair), 16:24, :].astype(F32)
+        rows = recv_ref[place(0, pair), 4:5].reshape(4, LANES).astype(F32)
         for part in range(1, PARTS):
-            rows = rows + recv_ref[place(part, pair), 16:24, :].astype(F32)
+            rows = rows + recv_ref[place(part, pair), 4:5].reshape(4, LANES).astype(F32)
         rows_ref[2 * pair : 2 * pair + 2, :] = rows[0:2]
-        rows = rows + pltpu.roll(rows, 64, 1)
+        sums.append(rows[2:3])
+    sums = jnp.concatenate(sums, axis=0)
+    sums = sums + pltpu.roll(sums, 64, 1)
+    per_frame = []
+    for frame in range(4):
+        total = jnp.zeros((8, LANES), F32)
         for head in range(2):
-            inside = (lane < 2 * BLOCKS) & (lane % 2 == head)
-            total = jnp.sum(jnp.where(inside, rows, 0.0), axis=1, keepdims=True)
-            per_frame = jnp.where(lane == 2 * pair + head, total, per_frame)
+            inside = (lane // 16 == frame) & (lane % 2 == head)
+            part_sum = jnp.sum(jnp.where(inside, sums, 0.0), axis=1, keepdims=True)
+            total = jnp.where(lane == 2 * row + head, part_sum, total)
+        per_frame.append(jnp.sum(total, axis=0, keepdims=True))
     pre = shifted_steps(frame_ref, raw_ref[...], table_ref[...])
     pre_ref[...] = rows_ref[...] * sigmoid(pre)
-    per_head = jnp.concatenate([per_frame, jnp.zeros((LANES - 8, LANES), F32)], axis=0).T
+    per_head = jnp.concatenate(per_frame + [jnp.zeros((LANES - 4, LANES), F32)], axis=0).T
     steps = lax.broadcasted_iota(jnp.int32, grad_ref.shape, 1)
     grad = jnp.zeros(grad_ref.shape, F32)
     for frame in range(4):
-        grad = grad + jnp.where(steps == frame_ref[frame], per_head[:heads, 2 + frame : 3 + frame], 0.0)
+        grad = grad + jnp.where(steps == frame_ref[frame], per_head[:heads, frame : frame + 1], 0.0)
     grad_ref[...] = grad
 
 
@@ -557,13 +568,13 @@
 SMEM = pl.BlockSpec(memory_space=pltpu.SMEM)
 
 
-def call(kernel, name, in_specs, out_shape, scratch=(), params=PARAMS):
+def call(kernel, name, in_specs, out_shape, scratch=(), params=PARAMS, out=VMEM):
     shapes = [jax.ShapeDtypeStruct(shape, dtype) for shape, dtype in out_shape]
     return pl.pallas_call(
         kernel,
         out_shape=shapes,
         in_specs=in_specs,
-        out_specs=[VMEM] * len(shapes),
+        out_specs=[out] * len(shapes),
         scratch_shapes=list(scratch),
         compiler_params=params,
         name=name,
@@ -582,8 +593,8 @@
     (send,) = call(
         pack_kernel, "pack", [hbm] * 8, [((SEQ, SLOT_IN, LANES), BF16)],
         [(pltpu.SMEM if a is frame_step else pltpu.VMEM)(a.shape, a.dtype) for a in sources]
-        + [pltpu.SemaphoreType.DMA((8,))],
-        pltpu.CompilerParams(vmem_limit_bytes=62 * 1024 * 1024),
+        + [pltpu.VMEM((SEQ, SLOT_IN, LANES), BF16), pltpu.SemaphoreType.DMA((12,))],
+        pltpu.CompilerParams(vmem_limit_bytes=62 * 1024 * 1024), hbm,
     )(*sources)
     recv = lax.all_to_all(send, "seq", 0, 0, tiled=True)
     (proj,) = call(cut_kernel, "cut", [VMEM], [((SEQ, 16, LANES), BF16)])(recv)
@@ -609,17 +620,17 @@
     keep, give, pairs = call(
         outer_kernel, "outer", [VMEM] * 4,
         [sums] * 2 + [((8 * LOCAL + 32, LANES), BF16)],
-        [pltpu.VMEM((BLOCKS, LANES, LANES), F32)] + [wide] * 2,
+        [pltpu.VMEM((BLOCKS, LANES, LANES), F32)],
     )(states, inner, data, grad)
     got = lax.ppermute(give, "seq", swap_core)
     (out,) = call(
         grads_kernel, "grads", [VMEM] * 4, [((SEQ, SLOT_OUT, LANES), BF16)],
         [wide, pltpu.VMEM((SEQ * 8, LANES), F32)],
     )(rates, data, pairs, grad)
-    (out,) = call(join_kernel, "join", [VMEM] * 3, [((SEQ, SLOT_OUT, LANES), BF16)])(out, keep, got)
+    (out,) = call(join_kernel, "join", [VMEM] * 3, [((SEQ, 9, 4, LANES), BF16)])(out, keep, got)
     back = lax.all_to_all(out, "seq", 0, 0, tiled=True)
     proj, rest = call(
-        proj_kernel, "proj", [VMEM], [((TOK, 2 * LANES), BF16), ((SEQ, 24, LANES), BF16)]
+        proj_kernel, "proj", [VMEM], [((TOK, 2 * LANES), BF16), ((SEQ, 5, 4, LANES), BF16)]
     )(back)
     ring = [lax.ppermute(proj, "head", [(i, (i + k) % 4) for i in range(4)]) for k in (1, 2, 3)]
     act, grad_pre, grad_table = call(

time: 96.9 us -> 95.3 us (0.983)
  blocking collectives: 64.1 us -> 62.7 us
    all_to_all x1, blocking collectives: 25.2 us -> 23.8 us  [shards(): back = lax.all_to_all(out, 'seq', 0, 0, tiled=True)]
where the time goes in v5:
time: 95.3 us; the launch traced here: 95 us
  blocking collectives  62.7 us (66%)
  Pallas kernels  14.2 us (15%)
  starting transfers between devices  9.67 us (10%)
  waiting for transfers between devices  7.6 us (8%)
    all_to_all x1, blocking collectives, shards(): recv = lax.all_to_all(send, 'seq', 0, 0, tiled=True)  38.9 us
    all_to_all x1, blocking collectives, shards(): back = lax.all_to_all(out, 'seq', 0, 0, tiled=True)  23.8 us
    all_to_all x1, waiting for transfers between devices, shards(): lax.all_to_all(states, 'seq', 0, 0, tiled=True, axis_index_groups=STATE_G...  4.19 us
    all_to_all x1, starting transfers between devices, shards(): lax.all_to_all(states, 'seq', 0, 0, tiled=True, axis_index_groups=STATE_G...  3.83 us
    ppermute x3, starting transfers between devices, shards(): lax.ppermute(proj, 'head', [(i, (i + k) % 4) for i in range(4)])  3.68 us
    ppermute x3, waiting for transfers between devices, shards(): lax.ppermute(proj, 'head', [(i, (i + k) % 4) for i in range(4)])  3.4 us
    pallas_call x1, Pallas kernels, shards(): call(inner_kernel, 'inner', [VMEM] * 2, [((2 * LOCAL + 8, LANES), F32), (...  2.56 us
    pallas_call x1, Pallas kernels, shards(): call(pack_kernel, 'pack', [hbm] * 8, [((SEQ, SLOT_IN, LANES), BF16)], [(p...  2.2 us
  transfers between devices with their start and end apart: 6, of which 3 were waited for; matrix products, arithmetic and copies ran while one was open for 0% of the time, Pallas kernels for 8%

profile of v5, /device:TPU:1, one launch (start us, length us, event | category | flops | bytes accessed | tf_op | source)
XLA Modules:
  0.0 95.0 jit_solution(6408179933929523663)
XLA Ops:
  0.6 2.2 %pack.1 = bf16[64,56,128]{2,1,0:T(8,128)(2,1)} custom-call(s32[1,128]{1,0:T(1,128)} %bitcast.13, s32[4]{0:T(128)} %frame_ref.1, f32[16,128]{1,0:T(8,128)} %bitcast.8, f32[16,1000]{1,0:T(8,128)} %bitcast.6, bf16[128,128]{1,0:T(8,128)(2,1)} %refs_4_.1, bf16[128,128]{1,0:T(8,128)(2,1)} %refs_5_.1, bf16[128,1024]{1,0:T(8,128)(2,1)} %refs_6_.1, ...), custom_call_target="tpu_custom_call" | custom-call | tf_op jit(solution)/shard_map/pack/pallas_call | solution.py:593
  2.8 0.0 copy-start.2
  2.9 38.9 %all_to_all.15.recv_ref = bf16[64,56,128]{2,1,0:T(8,128)(2,1)S(1)} all-to-all(bf16[64,56,128]{2,1,0:T(8,128)(2,1)} %pack.1), channel_id=1, replica_groups=mesh['seq'=64,'head'=4] {'seq'}, dimensions={0} | all-to-all | bytes 1835008 | tf_op jit(solution)/shard_map/all_to_all | solution.py:599
  41.8 0.4 collective-permute-start
  42.2 0.0 copy-done.2
  42.2 1.5 %unpack.1 = (bf16[2560,128]{1,0:T(8,128)(2,1)S(1)}, bf16[1024,128]{1,0:T(8,128)(2,1)S(1)}, bf16[2064,128]{1,0:T(8,128)(2,1)S(1)}) custom-call(f32[1,16]{1,0:T(1,128)S(1)} %bitcast.10, bf16[64,56,128]{2,1,0:T(8,128)(2,1)S(1)} %all_to_all.15.recv_ref), custom_call_target="tpu_custom_call" | custom-call | tf_op jit(solution)/shard_map/unpack/pallas_call | solution.py:605
  43.7 0.0 collective-permute-done.swap_ref
  43.7 0.3 gather.1.all_ref.data_ref
  44.0 1.1 %states.1 = bf16[8,136,128]{2,1,0:T(8,128)(2,1)} custom-call(bf16[4608,128]{1,0:T(8,128)(2,1)S(1)} %gather.1.all_ref.data_ref, bf16[2064,128]{1,0:T(8,128)(2,1)S(1)} %get-tuple-element.22.weight_ref), custom_call_target="tpu_custom_call" | custom-call | tf_op jit(solution)/shard_map/states/pallas_call | solution.py:611
  45.1 3.8 %all-to-all-start.1 = ((bf16[8,136,128]{2,1,0:T(8,128)(2,1)}), bf16[8,136,128]{2,1,0:T(8,128)(2,1)S(1)}, u32[]{:S(2)}, u32[]{:S(2)}) async-start(bf16[8,136,128]{2,1,0:T(8,128)(2,1)} %states.1), calls=%async_computation.1 | async-start | bytes 557056 | tf_op jit(solution)/shard_map/all_to_all | solution.py:612
  48.9 2.6 %inner.1 = (f32[2056,128]{1,0:T(8,128)S(1)}, f32[1408,128]{1,0:T(8,128)S(1)}) custom-call(f32[1,16]{1,0:T(1,128)S(1)} %bitcast.11, bf16[4608,128]{1,0:T(8,128)(2,1)S(1)} %gather.1.all_ref.data_ref), custom_call_target="tpu_custom_call" | custom-call | tf_op jit(solution)/shard_map/inner/pallas_call | solution.py:613
  51.5 4.2 %all-to-all-done.1.recv_ref = bf16[8,136,128]{2,1,0:T(8,128)(2,1)S(1)} async-done(((bf16[8,136,128]{2,1,0:T(8,128)(2,1)}), bf16[8,136,128]{2,1,0:T(8,128)(2,1)S(1)}, u32[]{:S(2)}, u32[]{:S(2)}) %all-to-all-start.1) | async-done | bytes 278560 | tf_op jit(solution)/shard_map/all_to_all | solution.py:612
  55.7 2.1 %outer.1 = (f32[1024,128]{1,0:T(8,128)S(1)}, f32[1024,128]{1,0:T(8,128)S(1)}, bf16[8224,128]{1,0:T(8,128)(2,1)S(1)}) custom-call(bf16[8,136,128]{2,1,0:T(8,128)(2,1)S(1)} %all-to-all-done.1.recv_ref, f32[2056,128]{1,0:T(8,128)S(1)} %get-tuple-element.23.sums_ref, bf16[4608,128]{1,0:T(8,128)(2,1)S(1)} %gather.1.all_ref.data_ref, ...), custom_call_target="tpu_custom_call" | custom-call | tf_op jit(solution)/shard_map/outer/pallas_call | solution.py:620
  57.8 1.7 %collective-permute-start.1 = (f32[1024,128]{1,0:T(8,128)S(1)}, f32[1024,128]{1,0:T(8,128)S(1)}, u32[]{:S(2)}, u32[]{:S(2)}) collective-permute-start(f32[1024,128]{1,0:T(8,128)S(1)} %get-tuple-element.27), channel_id=1, source_target_pairs={{0,4},{4,0},{8,12},{12,8},{16,20},{20,16},{24,28},{28,24},{32,36},... | collective-permute-start | bytes 1572872 | tf_op jit(solution)/shard_map/ppermute | solution.py:625
  59.5 1.9 %grads.1.in_ref = bf16[64,40,128]{2,1,0:T(8,128)(2,1)S(1)} custom-call(f32[1,16]{1,0:T(1,128)S(1)} %bitcast.12, bf16[4608,128]{1,0:T(8,128)(2,1)S(1)} %gather.1.all_ref.data_ref, bf16[8224,128]{1,0:T(8,128)(2,1)S(1)} %get-tuple-element.25.all_ref, f32[1408,128]{1,0:T(8,128)S(1)} %get-tuple-element.24.grad_ref), custom_call_target="tpu_custom_call" | custom-call | tf_op jit(solution)/shard_map/grads/pallas_call | solution.py:626
  61.5 0.0 collective-permute-done.1.got_ref
  61.5 0.2 join.1
  61.7 0.0 copy-start
  61.7 0.0 copy-start.1
  61.7 0.0 copy-start.3
  61.7 23.8 %all_to_all.16.recv_ref = bf16[64,9,4,128]{3,2,1,0:T(4,128)(2,1)S(1)} all-to-all(bf16[64,9,4,128]{3,2,1,0:T(4,128)(2,1)S(1)} %join.1), channel_id=1, replica_groups=mesh['seq'=64,'head'=4] {'seq'}, dimensions={0} | all-to-all | bytes 1179648 | tf_op jit(solution)/shard_map/all_to_all | solution.py:631
  85.6 0.1 proj.1
  85.7 2.6 %collective-permute-start.4 = (bf16[128,256]{1,0:T(8,128)(2,1)S(1)}, bf16[128,256]{1,0:T(8,128)(2,1)S(1)}, u32[]{:S(2)}, u32[]{:S(2)}) collective-permute-start(bf16[128,256]{1,0:T(8,128)(2,1)S(1)} %get-tuple-element.30.own_ref), channel_id=1, source_target_pairs={{0,3},{1,0},{2,1},{3,2},{4,7},{5,4},{6,5},{7,6},{8,11},{9,8},{10,9... | collective-permute-start | bytes 196616 | tf_op jit(solution)/shard_map/ppermute | solution.py:635
  88.2 0.5 collective-permute-start.3
  88.7 0.6 collective-permute-start.2
  89.3 0.0 copy-done
  89.3 0.0 copy-done.1
  89.3 0.0 copy-done.3
  89.3 1.6 %finish.1 = (bf16[128,1024]{1,0:T(8,128)(2,1)}, f32[16,128]{1,0:T(8,128)}, f32[16,1000]{1,0:T(8,128)}) custom-call(s32[4]{0:T(128)S(1)} %copy-done.3, bf16[64,5,4,128]{3,2,1,0:T(4,128)(2,1)S(1)} %get-tuple-element.28.recv_ref, f32[16,128]{1,0:T(8,128)S(1)} %bitcast.9, f32[16,1000]{1,0:T(8,128)S(1)} %bitcast.7), custom_call_target="tpu_custom_call" | custom-call | tf_op jit(solution)/shard_map/finish/pallas_call | solution.py:636
  90.9 0.0 collective-permute-done.4.three_ref
  90.9 2.0 %collective-permute-done.3.two_ref = bf16[128,256]{1,0:T(8,128)(2,1)S(1)} collective-permute-done((bf16[128,256]{1,0:T(8,128)(2,1)S(1)}, bf16[128,256]{1,0:T(8,128)(2,1)S(1)}, u32[]{:S(2)}, u32[]{:S(2)}) %collective-permute-start.3) | collective-permute-done | bytes 65568 | tf_op jit(solution)/shard_map/ppermute | solution.py:635
  92.9 1.4 %collective-permute-done.2.one_ref = bf16[128,256]{1,0:T(8,128)(2,1)S(1)} collective-permute-done((bf16[128,256]{1,0:T(8,128)(2,1)S(1)}, bf16[128,256]{1,0:T(8,128)(2,1)S(1)}, u32[]{:S(2)}, u32[]{:S(2)}) %collective-permute-start.2) | collective-permute-done | bytes 65568 | tf_op jit(solution)/shard_map/ppermute | solution.py:635
  94.3 0.7 total.1
  (1 shorter events, 0.0 us)
Async XLA Ops:
  2.8 39.4 %copy-start.2 = (f32[16]{0:T(128)S(1)}, f32[16]{0:T(128)}, u32[]{:S(2)}) copy-start(f32[16]{0:T(128)} %param.15) | copy-start | bytes 196
  41.8 1.9 %collective-permute-start = (bf16[64,16,128]{2,1,0:T(8,128)(2,1)S(1)}, bf16[64,16,128]{2,1,0:T(8,128)(2,1)S(1)}, u32[]{:S(2)}, u32[]{:S(2)}) collective-permute-start(bf16[64,16,128]{2,1,0:T(8,128)(2,1)S(1)} %cut.1), channel_id=1, source_target_pairs={{0,4},{4,0},{8,12},{12,8},{16,20},{20,16},{24,28},{28,24},{32,36},... | collective-permute-start | bytes 786440 | tf_op jit(solution)/shard_map/ppermute | solution.py:601
  45.1 10.6 %all-to-all-start.1 = ((bf16[8,136,128]{2,1,0:T(8,128)(2,1)}), bf16[8,136,128]{2,1,0:T(8,128)(2,1)S(1)}, u32[]{:S(2)}, u32[]{:S(2)}) async-start(bf16[8,136,128]{2,1,0:T(8,128)(2,1)} %states.1), calls=%async_computation.1 | async-start | bytes 557056 | tf_op jit(solution)/shard_map/all_to_all | solution.py:612
  57.8 3.7 %collective-permute-start.1 = (f32[1024,128]{1,0:T(8,128)S(1)}, f32[1024,128]{1,0:T(8,128)S(1)}, u32[]{:S(2)}, u32[]{:S(2)}) collective-permute-start(f32[1024,128]{1,0:T(8,128)S(1)} %get-tuple-element.27), channel_id=1, source_target_pairs={{0,4},{4,0},{8,12},{12,8},{16,20},{20,16},{24,28},{28,24},{32,36},... | collective-permute-start | bytes 1572872 | tf_op jit(solution)/shard_map/ppermute | solution.py:625
  61.7 27.6 %copy-start = (f32[1000,16]{0,1:T(8,128)S(1)}, f32[1000,16]{0,1:T(8,128)}, u32[]{:S(2)}) copy-start(f32[1000,16]{0,1:T(8,128)} %param.14) | copy-start | bytes 192004
  61.7 27.6 %copy-start.1 = (f32[128,16]{0,1:T(8,128)S(1)}, f32[128,16]{0,1:T(8,128)}, u32[]{:S(2)}) copy-start(f32[128,16]{0,1:T(8,128)} %param.13) | copy-start | bytes 24580
  61.7 27.6 %copy-start.3 = (s32[4]{0:T(128)S(1)}, s32[4]{0:T(128)}, u32[]{:S(2)}) copy-start(s32[4]{0:T(128)} %frame_ref.1) | copy-start | bytes 52
  85.7 5.3 %collective-permute-start.4 = (bf16[128,256]{1,0:T(8,128)(2,1)S(1)}, bf16[128,256]{1,0:T(8,128)(2,1)S(1)}, u32[]{:S(2)}, u32[]{:S(2)}) collective-permute-start(bf16[128,256]{1,0:T(8,128)(2,1)S(1)} %get-tuple-element.30.own_ref), channel_id=1, source_target_pairs={{0,3},{1,0},{2,1},{3,2},{4,7},{5,4},{6,5},{7,6},{8,11},{9,8},{10,9... | collective-permute-start | bytes 196616 | tf_op jit(solution)/shard_map/ppermute | solution.py:635
  88.2 4.7 %collective-permute-start.3 = (bf16[128,256]{1,0:T(8,128)(2,1)S(1)}, bf16[128,256]{1,0:T(8,128)(2,1)S(1)}, u32[]{:S(2)}, u32[]{:S(2)}) collective-permute-start(bf16[128,256]{1,0:T(8,128)(2,1)S(1)} %get-tuple-element.30.own_ref), channel_id=1, source_target_pairs={{0,2},{1,3},{2,0},{3,1},{4,6},{5,7},{6,4},{7,5},{8,10},{9,11},{10,... | collective-permute-start | bytes 196616 | tf_op jit(solution)/shard_map/ppermute | solution.py:635
  88.7 5.6 %collective-permute-start.2 = (bf16[128,256]{1,0:T(8,128)(2,1)S(1)}, bf16[128,256]{1,0:T(8,128)(2,1)S(1)}, u32[]{:S(2)}, u32[]{:S(2)}) collective-permute-start(bf16[128,256]{1,0:T(8,128)(2,1)S(1)} %get-tuple-element.30.own_ref), channel_id=1, source_target_pairs={{0,1},{1,2},{2,3},{3,0},{4,5},{5,6},{6,7},{7,4},{8,9},{9,10},{10,1... | collective-permute-start | bytes 196616 | tf_op jit(solution)/shard_map/ppermute | solution.py:635

commit v6 on v5

--- a/solution.py
+++ b/solution.py
@@ -14,7 +14,6 @@
 PARTS = 8
 PAIRS = 8
 BLOCKS = 8
-SLOT_IN = 56
 SLOT_STATE = 136
 SLOT_OUT = 40
 LOCAL = BLOCKS * TOK
@@ -75,7 +74,7 @@
 
 
 def pack_kernel(*refs):
-    sources, sent_ref, targets, out_ref, sems = refs[:8], refs[8], refs[9:17], refs[17], refs[18]
+    sources, sent_ref, targets, out_ref, misc, sems = refs[:8], refs[8], refs[9:17], refs[17], refs[18], refs[19]
     copies = [
         pltpu.make_async_copy(source, target, sems.at[i])
         for i, (source, target) in enumerate(zip(sources, targets))
@@ -98,14 +97,23 @@
     gate_low = gate - gate_high
     for copy in copies[4:]:
         copy.wait()
-    rows = []
-    for pair in range(PAIRS):
-        own = slice(2 * pair, 2 * pair + 2)
-        rows.append(
-            jnp.concatenate(
-                [position, delta[own], gate_high[own], gate_low[own], jnp.zeros((1, LANES), F32)], axis=0
-            ).astype(BF16)
-        )
+    row = lax.broadcasted_iota(jnp.int32, pre.shape, 0) % 2
+    group = lax.broadcasted_iota(jnp.int32, pre.shape, 1) // 16
+    turns = []
+    for kind, value in enumerate((delta, gate_high, gate_low)):
+        first = pltpu.roll(value, 32 * kind, 1) if kind else value
+        turns.append(jnp.where(row == 0, first, pltpu.roll(value, 32 * kind + 16, 1)))
+    misc[...] = jnp.zeros((SEQ * 4, LANES), F32)
+    misc[pl.ds(0, SEQ, stride=4), :] = jnp.broadcast_to(position, (SEQ, LANES))
+    for part in range(PARTS):
+        mixed = jnp.zeros(pre.shape, F32)
+        for kind in range(3):
+            mixed = mixed + jnp.where(group == (part + 2 * kind + row) % 8, turns[kind], 0.0)
+        mixed = mixed + pltpu.roll(mixed, mixed.shape[0] - 1, 0)
+        for pair in range(PAIRS):
+            spot = 4 * place(part, pair) + 1
+            misc[spot : spot + 1, :] = mixed[2 * pair : 2 * pair + 1]
+    out_ref[:, 12:13] = misc[...].astype(BF16).reshape(SEQ, 1, 4, LANES)
     leaving = []
     for quarter in range(4):
         for part in (2 * quarter, 2 * quarter + 1):
@@ -114,10 +122,9 @@
                 proj_ref = c_ref if pair % 2 else b_ref
                 columns = slice(LANES * pair, LANES * pair + LANES)
                 slot = place(part, pair)
-                out_ref[slot, 0:16, :] = x_ref[tokens, columns]
-                out_ref[slot, 16:32, :] = dy_ref[tokens, columns]
-                out_ref[slot, 32:48, :] = proj_ref[tokens, :]
-                out_ref[slot, 48:56, :] = rows[pair]
+                out_ref[slot, 0:4] = x_ref[tokens, columns].reshape(4, 4, LANES)
+                out_ref[slot, 4:8] = dy_ref[tokens, columns].reshape(4, 4, LANES)
+                out_ref[slot, 8:12] = proj_ref[tokens, :].reshape(4, 4, LANES)
         slots = pl.ds(16 * quarter, 16)
         leaving.append(pltpu.make_async_copy(out_ref.at[slots], sent_ref.at[slots], sems.at[8 + quarter]))
         leaving[quarter].start()
@@ -172,27 +179,27 @@
 
 
 def cut_kernel(recv_ref, proj_ref):
-    proj_ref[...] = recv_ref[:, 32:48, :]
+    proj_ref[...] = recv_ref[:, 8:12]
 
 
 def unpack_kernel(
     decay_ref, recv_ref, data_ref, proj_ref, weight_ref, wide, wide_two, wide_three, misc
 ):
     part, pair, core = my_place()
-    spread(recv_ref[:, 0:16, :].astype(F32), wide, data_ref, 0)
-    spread(recv_ref[:, 16:32, :].astype(F32), wide_two, data_ref, LOCAL)
-    spread(recv_ref[:, 32:48, :].astype(F32), wide_three, proj_ref, 0)
-    misc[...] = recv_ref[:, 48:56, :].astype(F32).reshape(SEQ * 8, LANES)
-    shift = (LANES - 16 * part) % LANES
-
-    def own_lanes(row):
-        return pltpu.roll(misc[pl.ds(row, 64, stride=8), :], shift, 1)
-
-    steps = to_columns(own_lanes(1), own_lanes(2))
-    gates_high = to_columns(own_lanes(3), own_lanes(4))
-    gates_low = to_columns(own_lanes(5), own_lanes(6))
+    misc[...] = recv_ref[:, 12:13].reshape(SEQ * 4, LANES).astype(F32)
+    mixed = pltpu.roll(misc[pl.ds(1, SEQ, stride=4), :], (LANES - 16 * part) % LANES, 1)
+
+    def own_lanes(number):
+        return pltpu.roll(mixed, LANES - 16 * number, 1) if number else mixed
+
+    steps = to_columns(own_lanes(0), own_lanes(1))
+    gates_high = to_columns(own_lanes(2), own_lanes(3))
+    gates_low = to_columns(own_lanes(4), own_lanes(5))
+    spread(recv_ref[:, 0:4].reshape(SEQ, 16, LANES).astype(F32), wide, data_ref, 0)
+    spread(recv_ref[:, 4:8].reshape(SEQ, 16, LANES).astype(F32), wide_two, data_ref, LOCAL)
+    spread(recv_ref[:, 8:12].reshape(SEQ, 16, LANES).astype(F32), wide_three, proj_ref, 0)
     pos_rows = jnp.concatenate(
-        [misc[pl.ds(part * 64 + 8 * block, 1), :] for block in range(BLOCKS)], axis=0
+        [misc[pl.ds(part * 32 + 4 * block, 1), :] for block in range(BLOCKS)], axis=0
     )
     pos_cols = jnp.concatenate([pos_rows, jnp.zeros((LANES - BLOCKS, LANES), F32)], axis=0).T
     lane = lane_iota(TOK)
@@ -242,12 +249,12 @@
     @pl.when(core == 0)
     def _():
         all_ref[2 * LOCAL : 3 * LOCAL, :] = mine_ref[...]
-        spread(swap_ref[...].astype(F32), wide, all_ref, 3 * LOCAL)
+        spread(swap_ref[...].reshape(SEQ, 16, LANES).astype(F32), wide, all_ref, 3 * LOCAL)
 
     @pl.when(core == 1)
     def _():
         all_ref[3 * LOCAL : 4 * LOCAL, :] = mine_ref[...]
-        spread(swap_ref[...].astype(F32), wide, all_ref, 2 * LOCAL)
+        spread(swap_ref[...].reshape(SEQ, 16, LANES).astype(F32), wide, all_ref, 2 * LOCAL)
 
 
 def states_kernel(all_ref, weight_ref, send_ref):
@@ -591,13 +598,17 @@
     order = scan_order.reshape(1, TOK)
     sources = (order, frame_step, raw, table, write_proj, read_proj, activations, grad_out)
     (send,) = call(
-        pack_kernel, "pack", [hbm] * 8, [((SEQ, SLOT_IN, LANES), BF16)],
+        pack_kernel, "pack", [hbm] * 8, [((SEQ, 13, 4, LANES), BF16)],
         [(pltpu.SMEM if a is frame_step else pltpu.VMEM)(a.shape, a.dtype) for a in sources]
-        + [pltpu.VMEM((SEQ, SLOT_IN, LANES), BF16), pltpu.SemaphoreType.DMA((12,))],
+        + [
+            pltpu.VMEM((SEQ, 13, 4, LANES), BF16),
+            pltpu.VMEM((SEQ * 4, LANES), F32),
+            pltpu.SemaphoreType.DMA((12,)),
+        ],
         pltpu.CompilerParams(vmem_limit_bytes=62 * 1024 * 1024), hbm,
     )(*sources)
     recv = lax.all_to_all(send, "seq", 0, 0, tiled=True)
-    (proj,) = call(cut_kernel, "cut", [VMEM], [((SEQ, 16, LANES), BF16)])(recv)
+    (proj,) = call(cut_kernel, "cut", [VMEM], [((SEQ, 4, 4, LANES), BF16)])(recv)
     swap = lax.ppermute(proj, "seq", swap_core)
     wide = pltpu.VMEM((LOCAL, LANES), F32)
     bundle = ((4 * LOCAL + 4 * TOK, LANES), BF16)
@@ -605,7 +616,7 @@
     data, mine, weight = call(
         unpack_kernel, "unpack", [VMEM] * 2,
         [((2 * LOCAL + 4 * TOK, LANES), BF16), ((LOCAL, LANES), BF16), ((2 * LOCAL + 16, LANES), BF16)],
-        [wide] * 3 + [pltpu.VMEM((SEQ * 8, LANES), F32)],
+        [wide] * 3 + [pltpu.VMEM((SEQ * 4, LANES), F32)],
     )(rates, recv)
     (data,) = call(gather_kernel, "gather", [VMEM] * 3, [bundle], [wide])(mine, swap, data)
     (states,) = call(states_kernel, "states", [VMEM] * 2, [((PARTS, SLOT_STATE, LANES), BF16)])(data, weight)

time: 95.3 us -> 94.1 us (0.987)
  blocking collectives: 62.7 us -> 61.3 us
    all_to_all x1, blocking collectives: 38.9 us -> 37.5 us  [shards(): recv = lax.all_to_all(send, 'seq', 0, 0, tiled=True)]
where the time goes in v6:
time: 94.1 us; the launch traced here: 93.8 us
  blocking collectives  61.3 us (65%)
  Pallas kernels  14.5 us (15%)
  starting transfers between devices  9.67 us (10%)
  waiting for transfers between devices  7.6 us (8%)
    all_to_all x1, blocking collectives, shards(): recv = lax.all_to_all(send, 'seq', 0, 0, tiled=True)  37.5 us
    all_to_all x1, blocking collectives, shards(): back = lax.all_to_all(out, 'seq', 0, 0, tiled=True)  23.8 us
    all_to_all x1, waiting for transfers between devices, shards(): lax.all_to_all(states, 'seq', 0, 0, tiled=True, axis_index_groups=STATE_G...  4.25 us
    all_to_all x1, starting transfers between devices, shards(): lax.all_to_all(states, 'seq', 0, 0, tiled=True, axis_index_groups=STATE_G...  3.84 us
    ppermute x3, starting transfers between devices, shards(): lax.ppermute(proj, 'head', [(i, (i + k) % 4) for i in range(4)])  3.69 us
    ppermute x3, waiting for transfers between devices, shards(): lax.ppermute(proj, 'head', [(i, (i + k) % 4) for i in range(4)])  3.34 us
    pallas_call x1, Pallas kernels, shards(): call(inner_kernel, 'inner', [VMEM] * 2, [((2 * LOCAL + 8, LANES), F32), (...  2.56 us
    pallas_call x1, Pallas kernels, shards(): call(pack_kernel, 'pack', [hbm] * 8, [((SEQ, 13, 4, LANES), BF16)], [(plt...  2.28 us
  transfers between devices with their start and end apart: 6, of which 3 were waited for; matrix products, arithmetic and copies ran while one was open for 0% of the time, Pallas kernels for 8%

profile of v6, /device:TPU:1, one launch (start us, length us, event | category | flops | bytes accessed | tf_op | source)
XLA Modules:
  0.0 93.8 jit_solution(1574324591867795547)
XLA Ops:
  0.6 2.3 %pack.1 = bf16[64,13,4,128]{3,2,1,0:T(4,128)(2,1)} custom-call(s32[1,128]{1,0:T(1,128)} %bitcast.13, s32[4]{0:T(128)} %frame_ref.1, f32[16,128]{1,0:T(8,128)} %bitcast.8, f32[16,1000]{1,0:T(8,128)} %bitcast.6, bf16[128,128]{1,0:T(8,128)(2,1)} %refs_4_.1, bf16[128,128]{1,0:T(8,128)(2,1)} %refs_5_.1, bf16[128,1024]{1,0:T(8,128)(2,1)} %refs_6_.1, ...), custom_call_target="tpu_custom_call" | custom-call | tf_op jit(solution)/shard_map/pack/pallas_call | solution.py:600
  2.9 0.0 copy-start.2
  2.9 37.5 %all_to_all.15.recv_ref = bf16[64,13,4,128]{3,2,1,0:T(4,128)(2,1)S(1)} all-to-all(bf16[64,13,4,128]{3,2,1,0:T(4,128)(2,1)} %pack.1), channel_id=1, replica_groups=mesh['seq'=64,'head'=4] {'seq'}, dimensions={0} | all-to-all | bytes 1703936 | tf_op jit(solution)/shard_map/all_to_all | solution.py:610
  40.5 0.5 collective-permute-start
  40.9 0.0 copy-done.2
  40.9 1.6 %unpack.1 = (bf16[2560,128]{1,0:T(8,128)(2,1)S(1)}, bf16[1024,128]{1,0:T(8,128)(2,1)S(1)}, bf16[2064,128]{1,0:T(8,128)(2,1)S(1)}) custom-call(f32[1,16]{1,0:T(1,128)S(1)} %bitcast.10, bf16[64,13,4,128]{3,2,1,0:T(4,128)(2,1)S(1)} %all_to_all.15.recv_ref), custom_call_target="tpu_custom_call" | custom-call | tf_op jit(solution)/shard_map/unpack/pallas_call | solution.py:616
  42.5 0.0 collective-permute-done.swap_ref
  42.6 0.3 gather.1.all_ref.data_ref
  42.9 1.1 %states.1 = bf16[8,136,128]{2,1,0:T(8,128)(2,1)} custom-call(bf16[4608,128]{1,0:T(8,128)(2,1)S(1)} %gather.1.all_ref.data_ref, bf16[2064,128]{1,0:T(8,128)(2,1)S(1)} %get-tuple-element.22.weight_ref), custom_call_target="tpu_custom_call" | custom-call | tf_op jit(solution)/shard_map/states/pallas_call | solution.py:622
  44.0 3.8 %all-to-all-start.1 = ((bf16[8,136,128]{2,1,0:T(8,128)(2,1)}), bf16[8,136,128]{2,1,0:T(8,128)(2,1)S(1)}, u32[]{:S(2)}, u32[]{:S(2)}) async-start(bf16[8,136,128]{2,1,0:T(8,128)(2,1)} %states.1), calls=%async_computation.1 | async-start | bytes 557056 | tf_op jit(solution)/shard_map/all_to_all | solution.py:623
  47.8 2.6 %inner.1 = (f32[2056,128]{1,0:T(8,128)S(1)}, f32[1408,128]{1,0:T(8,128)S(1)}) custom-call(f32[1,16]{1,0:T(1,128)S(1)} %bitcast.11, bf16[4608,128]{1,0:T(8,128)(2,1)S(1)} %gather.1.all_ref.data_ref), custom_call_target="tpu_custom_call" | custom-call | tf_op jit(solution)/shard_map/inner/pallas_call | solution.py:624
  50.4 4.3 %all-to-all-done.1.recv_ref = bf16[8,136,128]{2,1,0:T(8,128)(2,1)S(1)} async-done(((bf16[8,136,128]{2,1,0:T(8,128)(2,1)}), bf16[8,136,128]{2,1,0:T(8,128)(2,1)S(1)}, u32[]{:S(2)}, u32[]{:S(2)}) %all-to-all-start.1) | async-done | bytes 278560 | tf_op jit(solution)/shard_map/all_to_all | solution.py:623
  54.6 2.1 %outer.1 = (f32[1024,128]{1,0:T(8,128)S(1)}, f32[1024,128]{1,0:T(8,128)S(1)}, bf16[8224,128]{1,0:T(8,128)(2,1)S(1)}) custom-call(bf16[8,136,128]{2,1,0:T(8,128)(2,1)S(1)} %all-to-all-done.1.recv_ref, f32[2056,128]{1,0:T(8,128)S(1)} %get-tuple-element.23.sums_ref, bf16[4608,128]{1,0:T(8,128)(2,1)S(1)} %gather.1.all_ref.data_ref, ...), custom_call_target="tpu_custom_call" | custom-call | tf_op jit(solution)/shard_map/outer/pallas_call | solution.py:631
  56.8 1.7 %collective-permute-start.1 = (f32[1024,128]{1,0:T(8,128)S(1)}, f32[1024,128]{1,0:T(8,128)S(1)}, u32[]{:S(2)}, u32[]{:S(2)}) collective-permute-start(f32[1024,128]{1,0:T(8,128)S(1)} %get-tuple-element.27), channel_id=1, source_target_pairs={{0,4},{4,0},{8,12},{12,8},{16,20},{20,16},{24,28},{28,24},{32,36},... | collective-permute-start | bytes 1572872 | tf_op jit(solution)/shard_map/ppermute | solution.py:636
  58.4 1.9 %grads.1.in_ref = bf16[64,40,128]{2,1,0:T(8,128)(2,1)S(1)} custom-call(f32[1,16]{1,0:T(1,128)S(1)} %bitcast.12, bf16[4608,128]{1,0:T(8,128)(2,1)S(1)} %gather.1.all_ref.data_ref, bf16[8224,128]{1,0:T(8,128)(2,1)S(1)} %get-tuple-element.25.all_ref, f32[1408,128]{1,0:T(8,128)S(1)} %get-tuple-element.24.grad_ref), custom_call_target="tpu_custom_call" | custom-call | tf_op jit(solution)/shard_map/grads/pallas_call | solution.py:637
  60.4 0.0 collective-permute-done.1.got_ref
  60.4 0.2 join.1
  60.6 0.0 copy-start
  60.6 0.0 copy-start.1
  60.6 0.0 copy-start.3
  60.7 23.8 %all_to_all.16.recv_ref = bf16[64,9,4,128]{3,2,1,0:T(4,128)(2,1)S(1)} all-to-all(bf16[64,9,4,128]{3,2,1,0:T(4,128)(2,1)S(1)} %join.1), channel_id=1, replica_groups=mesh['seq'=64,'head'=4] {'seq'}, dimensions={0} | all-to-all | bytes 1179648 | tf_op jit(solution)/shard_map/all_to_all | solution.py:642
  84.4 0.1 proj.1
  84.5 2.6 %collective-permute-start.4 = (bf16[128,256]{1,0:T(8,128)(2,1)S(1)}, bf16[128,256]{1,0:T(8,128)(2,1)S(1)}, u32[]{:S(2)}, u32[]{:S(2)}) collective-permute-start(bf16[128,256]{1,0:T(8,128)(2,1)S(1)} %get-tuple-element.30.own_ref), channel_id=1, source_target_pairs={{0,3},{1,0},{2,1},{3,2},{4,7},{5,4},{6,5},{7,6},{8,11},{9,8},{10,9... | collective-permute-start | bytes 196616 | tf_op jit(solution)/shard_map/ppermute | solution.py:646
  87.1 0.5 collective-permute-start.3
  87.6 0.6 collective-permute-start.2
  88.2 0.0 copy-done
  88.2 0.0 copy-done.1
  88.2 0.0 copy-done.3
  88.2 1.6 %finish.1 = (bf16[128,1024]{1,0:T(8,128)(2,1)}, f32[16,128]{1,0:T(8,128)}, f32[16,1000]{1,0:T(8,128)}) custom-call(s32[4]{0:T(128)S(1)} %copy-done.3, bf16[64,5,4,128]{3,2,1,0:T(4,128)(2,1)S(1)} %get-tuple-element.28.recv_ref, f32[16,128]{1,0:T(8,128)S(1)} %bitcast.9, f32[16,1000]{1,0:T(8,128)S(1)} %bitcast.7), custom_call_target="tpu_custom_call" | custom-call | tf_op jit(solution)/shard_map/finish/pallas_call | solution.py:647
  89.8 0.0 collective-permute-done.4.three_ref
  89.8 2.0 %collective-permute-done.3.two_ref = bf16[128,256]{1,0:T(8,128)(2,1)S(1)} collective-permute-done((bf16[128,256]{1,0:T(8,128)(2,1)S(1)}, bf16[128,256]{1,0:T(8,128)(2,1)S(1)}, u32[]{:S(2)}, u32[]{:S(2)}) %collective-permute-start.3) | collective-permute-done | bytes 65568 | tf_op jit(solution)/shard_map/ppermute | solution.py:646
  91.7 1.4 %collective-permute-done.2.one_ref = bf16[128,256]{1,0:T(8,128)(2,1)S(1)} collective-permute-done((bf16[128,256]{1,0:T(8,128)(2,1)S(1)}, bf16[128,256]{1,0:T(8,128)(2,1)S(1)}, u32[]{:S(2)}, u32[]{:S(2)}) %collective-permute-start.2) | collective-permute-done | bytes 65568 | tf_op jit(solution)/shard_map/ppermute | solution.py:646
  93.1 0.7 total.1
  (1 shorter events, 0.0 us)
Async XLA Ops:
  2.9 38.0 %copy-start.2 = (f32[16]{0:T(128)S(1)}, f32[16]{0:T(128)}, u32[]{:S(2)}) copy-start(f32[16]{0:T(128)} %param.15) | copy-start | bytes 196
  40.5 2.1 %collective-permute-start = (bf16[64,4,4,128]{3,2,1,0:T(4,128)(2,1)S(1)}, bf16[64,4,4,128]{3,2,1,0:T(4,128)(2,1)S(1)}, u32[]{:S(2)}, u32[]{:S(2)}) collective-permute-start(bf16[64,4,4,128]{3,2,1,0:T(4,128)(2,1)S(1)} %cut.1), channel_id=1, source_target_pairs={{0,4},{4,0},{8,12},{12,8},{16,20},{20,16},{24,28},{28,24},{32,36},... | collective-permute-start | bytes 786440 | tf_op jit(solution)/shard_map/ppermute | solution.py:612
  44.0 10.7 %all-to-all-start.1 = ((bf16[8,136,128]{2,1,0:T(8,128)(2,1)}), bf16[8,136,128]{2,1,0:T(8,128)(2,1)S(1)}, u32[]{:S(2)}, u32[]{:S(2)}) async-start(bf16[8,136,128]{2,1,0:T(8,128)(2,1)} %states.1), calls=%async_computation.1 | async-start | bytes 557056 | tf_op jit(solution)/shard_map/all_to_all | solution.py:623
  56.8 3.6 %collective-permute-start.1 = (f32[1024,128]{1,0:T(8,128)S(1)}, f32[1024,128]{1,0:T(8,128)S(1)}, u32[]{:S(2)}, u32[]{:S(2)}) collective-permute-start(f32[1024,128]{1,0:T(8,128)S(1)} %get-tuple-element.27), channel_id=1, source_target_pairs={{0,4},{4,0},{8,12},{12,8},{16,20},{20,16},{24,28},{28,24},{32,36},... | collective-permute-start | bytes 1572872 | tf_op jit(solution)/shard_map/ppermute | solution.py:636
  60.6 27.6 %copy-start = (f32[1000,16]{0,1:T(8,128)S(1)}, f32[1000,16]{0,1:T(8,128)}, u32[]{:S(2)}) copy-start(f32[1000,16]{0,1:T(8,128)} %param.14) | copy-start | bytes 192004
  60.6 27.6 %copy-start.1 = (f32[128,16]{0,1:T(8,128)S(1)}, f32[128,16]{0,1:T(8,128)}, u32[]{:S(2)}) copy-start(f32[128,16]{0,1:T(8,128)} %param.13) | copy-start | bytes 24580
  60.6 27.6 %copy-start.3 = (s32[4]{0:T(128)S(1)}, s32[4]{0:T(128)}, u32[]{:S(2)}) copy-start(s32[4]{0:T(128)} %frame_ref.1) | copy-start | bytes 52
  84.5 5.3 %collective-permute-start.4 = (bf16[128,256]{1,0:T(8,128)(2,1)S(1)}, bf16[128,256]{1,0:T(8,128)(2,1)S(1)}, u32[]{:S(2)}, u32[]{:S(2)}) collective-permute-start(bf16[128,256]{1,0:T(8,128)(2,1)S(1)} %get-tuple-element.30.own_ref), channel_id=1, source_target_pairs={{0,3},{1,0},{2,1},{3,2},{4,7},{5,4},{6,5},{7,6},{8,11},{9,8},{10,9... | collective-permute-start | bytes 196616 | tf_op jit(solution)/shard_map/ppermute | solution.py:646
  87.1 4.7 %collective-permute-start.3 = (bf16[128,256]{1,0:T(8,128)(2,1)S(1)}, bf16[128,256]{1,0:T(8,128)(2,1)S(1)}, u32[]{:S(2)}, u32[]{:S(2)}) collective-permute-start(bf16[128,256]{1,0:T(8,128)(2,1)S(1)} %get-tuple-element.30.own_ref), channel_id=1, source_target_pairs={{0,2},{1,3},{2,0},{3,1},{4,6},{5,7},{6,4},{7,5},{8,10},{9,11},{10,... | collective-permute-start | bytes 196616 | tf_op jit(solution)/shard_map/ppermute | solution.py:646
  87.6 5.5 %collective-permute-start.2 = (bf16[128,256]{1,0:T(8,128)(2,1)S(1)}, bf16[128,256]{1,0:T(8,128)(2,1)S(1)}, u32[]{:S(2)}, u32[]{:S(2)}) collective-permute-start(bf16[128,256]{1,0:T(8,128)(2,1)S(1)} %get-tuple-element.30.own_ref), channel_id=1, source_target_pairs={{0,1},{1,2},{2,3},{3,0},{4,5},{5,6},{6,7},{7,4},{8,9},{9,10},{10,1... | collective-permute-start | bytes 196616 | tf_op jit(solution)/shard_map/ppermute | solution.py:646

commit v7 on v6

--- a/solution.py
+++ b/solution.py
@@ -506,7 +506,6 @@
     misc[pl.ds(1, 64, stride=8), :] = row_two
     misc[pl.ds(2, 64, stride=8), :] = jnp.broadcast_to(frames, (SEQ, LANES))
     out_ref[:, 0:16, :] = wide[...].reshape(SEQ, 16, LANES).astype(BF16)
-    out_ref[:, 16:32, :] = jnp.zeros((SEQ, 16, LANES), BF16)
     out_ref[:, 32:40, :] = misc[...].reshape(SEQ, 8, LANES).astype(BF16)
 
 
@@ -643,7 +642,7 @@
     proj, rest = call(
         proj_kernel, "proj", [VMEM], [((TOK, 2 * LANES), BF16), ((SEQ, 5, 4, LANES), BF16)]
     )(back)
-    ring = [lax.ppermute(proj, "head", [(i, (i + k) % 4) for i in range(4)]) for k in (1, 2, 3)]
+    one, three, two = [lax.ppermute(proj, "head", [(i, (i + k) % 4) for i in range(4)]) for k in (1, 3, 2)]
     act, grad_pre, grad_table = call(
         finish_kernel, "finish", [SMEM] + [VMEM] * 3,
         [(activations.shape, BF16), (raw.shape, F32), (table.shape, F32)],
@@ -651,7 +650,7 @@
     )(frame_step, rest, raw, table)
     grad_write, grad_read = call(
         total_kernel, "total", [VMEM] * 4, [(write_proj.shape, BF16), (read_proj.shape, BF16)]
-    )(proj, *ring)
+    )(proj, one, two, three)
     return (act, grad_write, grad_read, grad_pre.T, grad_table.T)
 
 

time: 94.1 us -> 94.1 us (level)
  no operation moved by 1% of the time
where the time goes in v7:
time: 94.1 us; the launch traced here: 93.8 us
  blocking collectives  61.3 us (65%)
  Pallas kernels  14.5 us (15%)
  starting transfers between devices  9.67 us (10%)
  waiting for transfers between devices  7.6 us (8%)
    all_to_all x1, blocking collectives, shards(): recv = lax.all_to_all(send, 'seq', 0, 0, tiled=True)  37.5 us
    all_to_all x1, blocking collectives, shards(): back = lax.all_to_all(out, 'seq', 0, 0, tiled=True)  23.8 us
    all_to_all x1, waiting for transfers between devices, shards(): lax.all_to_all(states, 'seq', 0, 0, tiled=True, axis_index_groups=STATE_G...  4.25 us
    all_to_all x1, starting transfers between devices, shards(): lax.all_to_all(states, 'seq', 0, 0, tiled=True, axis_index_groups=STATE_G...  3.84 us
    ppermute x3, starting transfers between devices, shards(): lax.ppermute(proj, 'head', [(i, (i + k) % 4) for i in range(4)])  3.69 us
    ppermute x3, waiting for transfers between devices, shards(): lax.ppermute(proj, 'head', [(i, (i + k) % 4) for i in range(4)])  3.34 us
    pallas_call x1, Pallas kernels, shards(): call(inner_kernel, 'inner', [VMEM] * 2, [((2 * LOCAL + 8, LANES), F32), (...  2.56 us
    pallas_call x1, Pallas kernels, shards(): call(pack_kernel, 'pack', [hbm] * 8, [((SEQ, 13, 4, LANES), BF16)], [(plt...  2.28 us
  transfers between devices with their start and end apart: 6, of which 3 were waited for; matrix products, arithmetic and copies ran while one was open for 0% of the time, Pallas kernels for 8%

profile of v7, /device:TPU:1, one launch (start us, length us, event | category | flops | bytes accessed | tf_op | source)
XLA Modules:
  0.0 93.8 jit_solution(4509707676987017910)
XLA Ops:
  0.6 2.3 %pack.1 = bf16[64,13,4,128]{3,2,1,0:T(4,128)(2,1)} custom-call(s32[1,128]{1,0:T(1,128)} %bitcast.13, s32[4]{0:T(128)} %frame_ref.1, f32[16,128]{1,0:T(8,128)} %bitcast.8, f32[16,1000]{1,0:T(8,128)} %bitcast.6, bf16[128,128]{1,0:T(8,128)(2,1)} %refs_4_.1, bf16[128,128]{1,0:T(8,128)(2,1)} %refs_5_.1, bf16[128,1024]{1,0:T(8,128)(2,1)} %refs_6_.1, ...), custom_call_target="tpu_custom_call" | custom-call | tf_op jit(solution)/shard_map/pack/pallas_call | solution.py:599
  2.9 0.0 copy-start.2
  2.9 37.5 %all_to_all.15.recv_ref = bf16[64,13,4,128]{3,2,1,0:T(4,128)(2,1)S(1)} all-to-all(bf16[64,13,4,128]{3,2,1,0:T(4,128)(2,1)} %pack.1), channel_id=1, replica_groups=mesh['seq'=64,'head'=4] {'seq'}, dimensions={0} | all-to-all | bytes 1703936 | tf_op jit(solution)/shard_map/all_to_all | solution.py:609
  40.5 0.5 collective-permute-start
  40.9 0.0 copy-done.2
  40.9 1.6 %unpack.1 = (bf16[2560,128]{1,0:T(8,128)(2,1)S(1)}, bf16[1024,128]{1,0:T(8,128)(2,1)S(1)}, bf16[2064,128]{1,0:T(8,128)(2,1)S(1)}) custom-call(f32[1,16]{1,0:T(1,128)S(1)} %bitcast.10, bf16[64,13,4,128]{3,2,1,0:T(4,128)(2,1)S(1)} %all_to_all.15.recv_ref), custom_call_target="tpu_custom_call" | custom-call | tf_op jit(solution)/shard_map/unpack/pallas_call | solution.py:615
  42.5 0.0 collective-permute-done.swap_ref
  42.6 0.3 gather.1.all_ref.data_ref
  42.9 1.1 %states.1 = bf16[8,136,128]{2,1,0:T(8,128)(2,1)} custom-call(bf16[4608,128]{1,0:T(8,128)(2,1)S(1)} %gather.1.all_ref.data_ref, bf16[2064,128]{1,0:T(8,128)(2,1)S(1)} %get-tuple-element.22.weight_ref), custom_call_target="tpu_custom_call" | custom-call | tf_op jit(solution)/shard_map/states/pallas_call | solution.py:621
  44.0 3.8 %all-to-all-start.1 = ((bf16[8,136,128]{2,1,0:T(8,128)(2,1)}), bf16[8,136,128]{2,1,0:T(8,128)(2,1)S(1)}, u32[]{:S(2)}, u32[]{:S(2)}) async-start(bf16[8,136,128]{2,1,0:T(8,128)(2,1)} %states.1), calls=%async_computation.1 | async-start | bytes 557056 | tf_op jit(solution)/shard_map/all_to_all | solution.py:622
  47.8 2.6 %inner.1 = (f32[2056,128]{1,0:T(8,128)S(1)}, f32[1408,128]{1,0:T(8,128)S(1)}) custom-call(f32[1,16]{1,0:T(1,128)S(1)} %bitcast.11, bf16[4608,128]{1,0:T(8,128)(2,1)S(1)} %gather.1.all_ref.data_ref), custom_call_target="tpu_custom_call" | custom-call | tf_op jit(solution)/shard_map/inner/pallas_call | solution.py:623
  50.4 4.3 %all-to-all-done.1.recv_ref = bf16[8,136,128]{2,1,0:T(8,128)(2,1)S(1)} async-done(((bf16[8,136,128]{2,1,0:T(8,128)(2,1)}), bf16[8,136,128]{2,1,0:T(8,128)(2,1)S(1)}, u32[]{:S(2)}, u32[]{:S(2)}) %all-to-all-start.1) | async-done | bytes 278560 | tf_op jit(solution)/shard_map/all_to_all | solution.py:622
  54.6 2.1 %outer.1 = (f32[1024,128]{1,0:T(8,128)S(1)}, f32[1024,128]{1,0:T(8,128)S(1)}, bf16[8224,128]{1,0:T(8,128)(2,1)S(1)}) custom-call(bf16[8,136,128]{2,1,0:T(8,128)(2,1)S(1)} %all-to-all-done.1.recv_ref, f32[2056,128]{1,0:T(8,128)S(1)} %get-tuple-element.23.sums_ref, bf16[4608,128]{1,0:T(8,128)(2,1)S(1)} %gather.1.all_ref.data_ref, ...), custom_call_target="tpu_custom_call" | custom-call | tf_op jit(solution)/shard_map/outer/pallas_call | solution.py:630
  56.8 1.7 %collective-permute-start.1 = (f32[1024,128]{1,0:T(8,128)S(1)}, f32[1024,128]{1,0:T(8,128)S(1)}, u32[]{:S(2)}, u32[]{:S(2)}) collective-permute-start(f32[1024,128]{1,0:T(8,128)S(1)} %get-tuple-element.27), channel_id=1, source_target_pairs={{0,4},{4,0},{8,12},{12,8},{16,20},{20,16},{24,28},{28,24},{32,36},... | collective-permute-start | bytes 1572872 | tf_op jit(solution)/shard_map/ppermute | solution.py:635
  58.4 1.9 %grads.1.in_ref = bf16[64,40,128]{2,1,0:T(8,128)(2,1)S(1)} custom-call(f32[1,16]{1,0:T(1,128)S(1)} %bitcast.12, bf16[4608,128]{1,0:T(8,128)(2,1)S(1)} %gather.1.all_ref.data_ref, bf16[8224,128]{1,0:T(8,128)(2,1)S(1)} %get-tuple-element.25.all_ref, f32[1408,128]{1,0:T(8,128)S(1)} %get-tuple-element.24.grad_ref), custom_call_target="tpu_custom_call" | custom-call | tf_op jit(solution)/shard_map/grads/pallas_call | solution.py:636
  60.4 0.0 collective-permute-done.1.got_ref
  60.4 0.2 join.1
  60.6 0.0 copy-start
  60.6 0.0 copy-start.1
  60.6 0.0 copy-start.3
  60.7 23.8 %all_to_all.16.recv_ref = bf16[64,9,4,128]{3,2,1,0:T(4,128)(2,1)S(1)} all-to-all(bf16[64,9,4,128]{3,2,1,0:T(4,128)(2,1)S(1)} %join.1), channel_id=1, replica_groups=mesh['seq'=64,'head'=4] {'seq'}, dimensions={0} | all-to-all | bytes 1179648 | tf_op jit(solution)/shard_map/all_to_all | solution.py:641
  84.4 0.1 proj.1
  84.5 2.6 %collective-permute-start.4 = (bf16[128,256]{1,0:T(8,128)(2,1)S(1)}, bf16[128,256]{1,0:T(8,128)(2,1)S(1)}, u32[]{:S(2)}, u32[]{:S(2)}) collective-permute-start(bf16[128,256]{1,0:T(8,128)(2,1)S(1)} %get-tuple-element.30.own_ref), channel_id=1, source_target_pairs={{0,3},{1,0},{2,1},{3,2},{4,7},{5,4},{6,5},{7,6},{8,11},{9,8},{10,9... | collective-permute-start | bytes 196616 | tf_op jit(solution)/shard_map/ppermute | solution.py:645
  87.1 0.5 collective-permute-start.3
  87.6 0.6 collective-permute-start.2
  88.2 0.0 copy-done
  88.2 0.0 copy-done.1
  88.2 0.0 copy-done.3
  88.2 1.6 %finish.1 = (bf16[128,1024]{1,0:T(8,128)(2,1)}, f32[16,128]{1,0:T(8,128)}, f32[16,1000]{1,0:T(8,128)}) custom-call(s32[4]{0:T(128)S(1)} %copy-done.3, bf16[64,5,4,128]{3,2,1,0:T(4,128)(2,1)S(1)} %get-tuple-element.28.recv_ref, f32[16,128]{1,0:T(8,128)S(1)} %bitcast.9, f32[16,1000]{1,0:T(8,128)S(1)} %bitcast.7), custom_call_target="tpu_custom_call" | custom-call | tf_op jit(solution)/shard_map/finish/pallas_call | solution.py:646
  89.8 0.0 collective-permute-done.4.three_ref
  89.8 2.0 %collective-permute-done.3.two_ref = bf16[128,256]{1,0:T(8,128)(2,1)S(1)} collective-permute-done((bf16[128,256]{1,0:T(8,128)(2,1)S(1)}, bf16[128,256]{1,0:T(8,128)(2,1)S(1)}, u32[]{:S(2)}, u32[]{:S(2)}) %collective-permute-start.3) | collective-permute-done | bytes 65568 | tf_op jit(solution)/shard_map/ppermute | solution.py:645
  91.7 1.4 %collective-permute-done.2.one_ref = bf16[128,256]{1,0:T(8,128)(2,1)S(1)} collective-permute-done((bf16[128,256]{1,0:T(8,128)(2,1)S(1)}, bf16[128,256]{1,0:T(8,128)(2,1)S(1)}, u32[]{:S(2)}, u32[]{:S(2)}) %collective-permute-start.2) | collective-permute-done | bytes 65568 | tf_op jit(solution)/shard_map/ppermute | solution.py:645
  93.1 0.7 total.1
  (1 shorter events, 0.0 us)
Async XLA Ops:
  2.9 38.0 %copy-start.2 = (f32[16]{0:T(128)S(1)}, f32[16]{0:T(128)}, u32[]{:S(2)}) copy-start(f32[16]{0:T(128)} %param.15) | copy-start | bytes 196
  40.5 2.1 %collective-permute-start = (bf16[64,4,4,128]{3,2,1,0:T(4,128)(2,1)S(1)}, bf16[64,4,4,128]{3,2,1,0:T(4,128)(2,1)S(1)}, u32[]{:S(2)}, u32[]{:S(2)}) collective-permute-start(bf16[64,4,4,128]{3,2,1,0:T(4,128)(2,1)S(1)} %cut.1), channel_id=1, source_target_pairs={{0,4},{4,0},{8,12},{12,8},{16,20},{20,16},{24,28},{28,24},{32,36},... | collective-permute-start | bytes 786440 | tf_op jit(solution)/shard_map/ppermute | solution.py:611
  44.0 10.7 %all-to-all-start.1 = ((bf16[8,136,128]{2,1,0:T(8,128)(2,1)}), bf16[8,136,128]{2,1,0:T(8,128)(2,1)S(1)}, u32[]{:S(2)}, u32[]{:S(2)}) async-start(bf16[8,136,128]{2,1,0:T(8,128)(2,1)} %states.1), calls=%async_computation.1 | async-start | bytes 557056 | tf_op jit(solution)/shard_map/all_to_all | solution.py:622
  56.8 3.6 %collective-permute-start.1 = (f32[1024,128]{1,0:T(8,128)S(1)}, f32[1024,128]{1,0:T(8,128)S(1)}, u32[]{:S(2)}, u32[]{:S(2)}) collective-permute-start(f32[1024,128]{1,0:T(8,128)S(1)} %get-tuple-element.27), channel_id=1, source_target_pairs={{0,4},{4,0},{8,12},{12,8},{16,20},{20,16},{24,28},{28,24},{32,36},... | collective-permute-start | bytes 1572872 | tf_op jit(solution)/shard_map/ppermute | solution.py:635
  60.6 27.6 %copy-start = (f32[1000,16]{0,1:T(8,128)S(1)}, f32[1000,16]{0,1:T(8,128)}, u32[]{:S(2)}) copy-start(f32[1000,16]{0,1:T(8,128)} %param.14) | copy-start | bytes 192004
  60.6 27.6 %copy-start.1 = (f32[128,16]{0,1:T(8,128)S(1)}, f32[128,16]{0,1:T(8,128)}, u32[]{:S(2)}) copy-start(f32[128,16]{0,1:T(8,128)} %param.13) | copy-start | bytes 24580
  60.6 27.6 %copy-start.3 = (s32[4]{0:T(128)S(1)}, s32[4]{0:T(128)}, u32[]{:S(2)}) copy-start(s32[4]{0:T(128)} %frame_ref.1) | copy-start | bytes 52
  84.5 5.3 %collective-permute-start.4 = (bf16[128,256]{1,0:T(8,128)(2,1)S(1)}, bf16[128,256]{1,0:T(8,128)(2,1)S(1)}, u32[]{:S(2)}, u32[]{:S(2)}) collective-permute-start(bf16[128,256]{1,0:T(8,128)(2,1)S(1)} %get-tuple-element.30.own_ref), channel_id=1, source_target_pairs={{0,3},{1,0},{2,1},{3,2},{4,7},{5,4},{6,5},{7,6},{8,11},{9,8},{10,9... | collective-permute-start | bytes 196616 | tf_op jit(solution)/shard_map/ppermute | solution.py:645
  87.1 4.7 %collective-permute-start.3 = (bf16[128,256]{1,0:T(8,128)(2,1)S(1)}, bf16[128,256]{1,0:T(8,128)(2,1)S(1)}, u32[]{:S(2)}, u32[]{:S(2)}) collective-permute-start(bf16[128,256]{1,0:T(8,128)(2,1)S(1)} %get-tuple-element.30.own_ref), channel_id=1, source_target_pairs={{0,2},{1,3},{2,0},{3,1},{4,6},{5,7},{6,4},{7,5},{8,10},{9,11},{10,... | collective-permute-start | bytes 196616 | tf_op jit(solution)/shard_map/ppermute | solution.py:645
  87.6 5.5 %collective-permute-start.2 = (bf16[128,256]{1,0:T(8,128)(2,1)S(1)}, bf16[128,256]{1,0:T(8,128)(2,1)S(1)}, u32[]{:S(2)}, u32[]{:S(2)}) collective-permute-start(bf16[128,256]{1,0:T(8,128)(2,1)S(1)} %get-tuple-element.30.own_ref), channel_id=1, source_target_pairs={{0,1},{1,2},{2,3},{3,0},{4,5},{5,6},{6,7},{7,4},{8,9},{9,10},{10,1... | collective-permute-start | bytes 196616 | tf_op jit(solution)/shard_map/ppermute | solution.py:645
